TPU v7x, 32 devices: a whole 2x2x4 slice. The times are simulated.
32 devices in a mesh: dp: 4 (over y, x), fsdp: 8 (over z, core).
Axes of the slice: x: 2, y: 2, z: 4, core: 2. Of those that a mesh axis runs over, the one named last changes fastest.
Arguments:
- token_ids: int32 [2, 32, 128], P(None, ('dp', 'fsdp')), may hold values from 0 to 50303
- loss_mask: int32 [2, 32, 128], P(None, ('dp', 'fsdp')), may hold values 0 or 1
- lengths: int32 [2, 32], P(None, ('dp', 'fsdp')), may hold values from 64 to 128, as said below
- buffer_ids: int32 [2, 32, 128], P(None, ('dp', 'fsdp')), may hold values from 0 to 2, never falling along the last dimension, each value on 1 to 64 neighbouring positions
- embed_table: float32 [50304, 512], P('fsdp'), may hold values from -6 to 6
- embed_moment: float32 [50304, 512], P(('fsdp', 'dp')), may hold values from -1.66893e-06 to 1.66893e-06
- embed_average: float32 [50304, 512], P(('fsdp', 'dp')), may hold values from -6 to 6
- head_table: float32 [50304, 512], P('fsdp'), may hold values from -0.25 to 0.25
- head_moment: float32 [50304, 512], P(('fsdp', 'dp')), may hold values from -1.66893e-06 to 1.66893e-06
- head_average: float32 [50304, 512], P(('fsdp', 'dp')), may hold values from -0.25 to 0.25
- in_weights: float32 [512, 3584], P('fsdp'), may hold values from -0.25 to 0.25
- in_moment: float32 [512, 3584], P('fsdp'), may hold values from -1.66893e-06 to 1.66893e-06
- in_average: float32 [512, 3584], P('fsdp'), may hold values from -0.25 to 0.25
- out_weights: float32 [2560, 512], P('fsdp')
- out_moment: float32 [2560, 512], P('fsdp'), may hold values from -1.66893e-06 to 1.66893e-06
- out_average: float32 [2560, 512], P('fsdp'), may hold values from -0.25 to 0.25
- vectors: float32 [7680], P('fsdp')
- vector_moment: float32 [7680], P('fsdp'), may hold values from -1.66893e-06 to 1.66893e-06
- vector_average: float32 [7680], P('fsdp')
Outputs:
- new_embed: float32 [50304, 512], P('fsdp')
- new_embed_moment: float32 [50304, 512], P(('fsdp', 'dp'))
- new_embed_average: float32 [50304, 512], P(('fsdp', 'dp'))
- new_head: float32 [50304, 512], P('fsdp')
- new_head_moment: float32 [50304, 512], P(('fsdp', 'dp'))
- new_head_average: float32 [50304, 512], P(('fsdp', 'dp'))
- new_in: float32 [512, 3584], P('fsdp')
- new_in_moment: float32 [512, 3584], P('fsdp')
- new_in_average: float32 [512, 3584], P('fsdp')
- new_out: float32 [2560, 512], P('fsdp')
- new_out_moment: float32 [2560, 512], P('fsdp')
- new_out_average: float32 [2560, 512], P('fsdp')
- new_vectors: float32 [7680], P('fsdp')
- new_vector_moment: float32 [7680], P('fsdp')
- new_vector_average: float32 [7680], P('fsdp')
- loss: float32 [], replicated
- grad_norm: float32 [], replicated
Inputs may be any that keep to these rules, and one draw needn't show every extreme that they name: `lengths`: each slot has 64 or 128 live positions. `buffer_ids`: along a slot the buffer numbers never fall; a buffer covers 1 to 64 positions.
All inputs are finite; a program needn't handle non-finite values. No bound on the sum of `loss_mask` on one device may be relied on, other than what follows from the above.
Results may differ from a plain program's by a relative error of at most 0.002.
The roundings to bfloat16 on the way count: a program that leaves them out, or rounds other values in their place, can miss the bound.
Values may be sent and summed in bfloat16 or wider, within the bound.
A program may use at most 320 MiB of HBM per device.

v0:
```python
import functools
import math

import jax
import jax.numpy as jnp
from jax import lax
from jax.sharding import PartitionSpec as P

HEADS = 8
NPARAM = 54664704
NSEG = 3


EPSILON = 1e-05
CLIP_LEVEL = 0.002
MOMENTUM = 0.5
DECAY = 0.5
NARROW = jnp.bfloat16
FLOAT = jnp.float32
ROWS_CONTRACT = (((0,), (0,)), ((), ()))
LAST_CONTRACT = (((1,), (1,)), ((), ()))


def combined_all(shard, axis, combine):
    everything = jax.tree.map(lambda part: lax.all_gather(part, axis), shard)
    first = jax.tree.map(lambda part: part[0], everything)

    def lap(k, so_far):
        return combine(so_far, jax.tree.map(lambda part: part[k], everything))

    return lax.fori_loop(1, lax.axis_size(axis), lap, first)


def slot_info(tokens, marks, length, buffers, buffer_count):
    seq = tokens.shape[0]
    places = jnp.arange(seq, dtype=jnp.int32)
    same_buffer = jnp.concatenate([buffers[1:] == buffers[:-1], jnp.zeros((1,), dtype=bool)])
    valid = jnp.where((marks == 1) & (places + 1 < length) & same_buffer, 1.0, 0.0).astype(FLOAT)
    member = buffers[None, :] == jnp.arange(buffer_count, dtype=jnp.int32)[:, None]
    weights = jnp.where(member, 1.0, 0.0).astype(FLOAT)
    tally = jnp.sum(weights * valid[None, :], axis=1)
    share = valid * jnp.sum(weights / jnp.maximum(tally, 1.0)[:, None], axis=0)
    counted = jnp.sum(jnp.where(tally > 0.5, 1.0, 0.0).astype(FLOAT))
    first = jnp.min(jnp.where(member, places[None, :], seq), axis=1)
    offset = places - jnp.sum(jnp.where(member, first[:, None], 0), axis=0)
    successor = jnp.concatenate([tokens[1:], jnp.zeros((1,), dtype=jnp.int32)])
    return (share, successor, offset, counted)


def vector_parts(vectors, width, hidden):
    amounts = [width] * 6 + [3 * width, width, hidden, width]
    parts = []
    begin = 0
    for amount in amounts:
        parts.append(vectors[begin : begin + amount])
        begin = begin + amount
    return parts


def rotary_tables(offset, rot):
    half = rot // 2
    freqs = jnp.power(10000.0, -2.0 * jnp.arange(half, dtype=FLOAT) / rot)
    angles = offset.astype(FLOAT)[:, None] * freqs[None, :]
    return (jnp.cos(angles)[:, None, :], jnp.sin(angles)[:, None, :])


def rotate(values, cosine, sine, rot):
    half = rot // 2
    first = values[..., :half]
    second = values[..., half:rot]
    return jnp.concatenate(
        [first * cosine - second * sine, second * cosine + first * sine, values[..., rot:]], axis=-1
    )


def rotate_back(grads, cosine, sine, rot):
    half = rot // 2
    first = grads[..., :half]
    second = grads[..., half:rot]
    return jnp.concatenate(
        [first * cosine + second * sine, second * cosine - first * sine, grads[..., rot:]], axis=-1
    )


def norm_forward(values, gain, bias):
    mean = jnp.mean(values, axis=-1, keepdims=True)
    centred = values - mean
    scale = lax.rsqrt(jnp.mean(centred * centred, axis=-1, keepdims=True) + EPSILON)
    unit = centred * scale
    return (unit * gain + bias, unit, scale)


def norm_backward(grads, unit, scale, gain):
    scaled = grads * gain
    back = scale * (
        scaled
        - jnp.mean(scaled, axis=-1, keepdims=True)
        - unit * jnp.mean(scaled * unit, axis=-1, keepdims=True)
    )
    return (back, jnp.sum(grads * unit, axis=0), jnp.sum(grads, axis=0))


def gelu_slope(values):
    return (
        0.5 * (1.0 + lax.erf(values * 0.7071067811865476))
        + values * jnp.exp(-0.5 * values * values) * 0.3989422804014327
    )


def attention_scores(queries, keys, allowed, factor):
    scores = jnp.einsum("qhd,khd->hqk", queries, keys, preferred_element_type=FLOAT) * factor
    return jnp.where(allowed[None, :, :], scores, -1e30)


def layer_forward(resid, in_full, out_full, parts, allowed, cosine, sine, factor):
    rows, width = resid.shape
    head_size = width // HEADS
    rot = head_size // 4
    normed_one, unit_one, scale_one = norm_forward(resid, parts[0], parts[1])
    normed_two, unit_two, scale_two = norm_forward(resid, parts[2], parts[3])
    input_one = normed_one.astype(NARROW)
    input_two = normed_two.astype(NARROW)
    triple = (
        jnp.dot(input_one, in_full[:, : 3 * width], preferred_element_type=FLOAT) + parts[6]
    ).reshape(rows, 3, HEADS, head_size)
    queries = rotate(triple[:, 0], cosine, sine, rot).astype(NARROW)
    keys = rotate(triple[:, 1], cosine, sine, rot).astype(NARROW)
    values = triple[:, 2].astype(NARROW)
    scores = attention_scores(queries, keys, allowed, factor)
    top = jnp.max(scores, axis=-1, keepdims=True)
    logsum = top + jnp.log(jnp.sum(jnp.exp(scores - top), axis=-1, keepdims=True))
    probs = jnp.exp(scores - logsum).astype(NARROW)
    mixed = (
        jnp.einsum("hqk,khd->qhd", probs, values, preferred_element_type=FLOAT)
        .astype(NARROW)
        .reshape(rows, width)
    )
    pre_act = jnp.dot(input_two, in_full[:, 3 * width :], preferred_element_type=FLOAT) + parts[8]
    activated = jax.nn.gelu(pre_act, approximate=False).astype(NARROW)
    joined = jnp.concatenate([mixed, activated], axis=1)
    result = resid + jnp.dot(joined, out_full, preferred_element_type=FLOAT) + parts[7] + parts[9]
    kept = (
        input_one,
        input_two,
        unit_one,
        scale_one,
        unit_two,
        scale_two,
        queries,
        keys,
        values,
        logsum,
        pre_act,
        joined,
    )
    return (result, kept)


def layer_backward(grad_out, in_full, out_full, parts, kept, allowed, cosine, sine, factor):
    (
        input_one,
        input_two,
        unit_one,
        scale_one,
        unit_two,
        scale_two,
        queries,
        keys,
        values,
        logsum,
        pre_act,
        joined,
    ) = kept
    rows, width = grad_out.shape
    head_size = width // HEADS
    rot = head_size // 4
    grad_low = grad_out.astype(NARROW)
    out_grad = lax.dot_general(joined, grad_low, ROWS_CONTRACT, preferred_element_type=FLOAT)
    joined_grad = lax.dot_general(grad_low, out_full, LAST_CONTRACT, preferred_element_type=FLOAT)
    mixed_grad = joined_grad[:, :width].astype(NARROW).reshape(rows, HEADS, head_size)
    pre_grad = joined_grad[:, width:] * gelu_slope(pre_act)
    pre_low = pre_grad.astype(NARROW)
    probs = jnp.exp(attention_scores(queries, keys, allowed, factor) - logsum)
    prob_grad = jnp.einsum("qhd,khd->hqk", mixed_grad, values, preferred_element_type=FLOAT)
    value_grad = jnp.einsum(
        "hqk,qhd->khd", probs.astype(NARROW), mixed_grad, preferred_element_type=FLOAT
    )
    score_grad = (
        probs * (prob_grad - jnp.sum(probs * prob_grad, axis=-1, keepdims=True)) * factor
    ).astype(NARROW)
    query_grad = rotate_back(
        jnp.einsum("hqk,khd->qhd", score_grad, keys, preferred_element_type=FLOAT),
        cosine,
        sine,
        rot,
    )
    key_grad = rotate_back(
        jnp.einsum("hqk,qhd->khd", score_grad, queries, preferred_element_type=FLOAT),
        cosine,
        sine,
        rot,
    )
    qkv_grad = jnp.stack([query_grad, key_grad, value_grad], axis=1).reshape(rows, 3 * width)
    qkv_low = qkv_grad.astype(NARROW)
    in_grad = jnp.concatenate(
        [
            lax.dot_general(input_one, qkv_low, ROWS_CONTRACT, preferred_element_type=FLOAT),
            lax.dot_general(input_two, pre_low, ROWS_CONTRACT, preferred_element_type=FLOAT),
        ],
        axis=1,
    )
    back_one = lax.dot_general(
        qkv_low, in_full[:, : 3 * width], LAST_CONTRACT, preferred_element_type=FLOAT
    )
    back_two = lax.dot_general(
        pre_low, in_full[:, 3 * width :], LAST_CONTRACT, preferred_element_type=FLOAT
    )
    grad_one, gain_one_grad, bias_one_grad = norm_backward(back_one, unit_one, scale_one, parts[0])
    grad_two, gain_two_grad, bias_two_grad = norm_backward(back_two, unit_two, scale_two, parts[2])
    resid_grad = grad_out + grad_one + grad_two
    residual_bias = jnp.sum(grad_out, axis=0)
    small = (
        gain_one_grad,
        bias_one_grad,
        gain_two_grad,
        bias_two_grad,
        jnp.sum(qkv_grad, axis=0),
        residual_bias,
        jnp.sum(pre_grad, axis=0),
        residual_bias,
    )
    return (resid_grad, in_grad, out_grad, small)


def logit_stats(items, head_low, columns):
    hidden_rows, target = items
    logits = lax.dot_general(hidden_rows, head_low, LAST_CONTRACT, preferred_element_type=FLOAT)
    top = jnp.max(logits, axis=1)
    total = jnp.sum(jnp.exp(logits - top[:, None]), axis=1)
    hit = jnp.sum(jnp.where(columns[None, :] == target[:, None], logits, 0.0), axis=1)
    return (top, total, hit)


def combine_softmax(first, second):
    top = jnp.maximum(first[0], second[0])
    total = first[1] * jnp.exp(first[0] - top) + second[1] * jnp.exp(second[0] - top)
    return (top, total, first[2] + second[2])


def update_rule(weight, grad, moment, average, rate, clip_factor):
    clipped = clip_factor * grad
    new_moment = MOMENTUM * moment + clipped
    new_weight = weight - rate * (clipped + MOMENTUM * new_moment)
    new_average = DECAY * average + (1.0 - DECAY) * new_weight
    return (new_weight, new_moment, new_average)


def shards(
    token_ids,
    loss_mask,
    lengths,
    buffer_ids,
    embed_table,
    embed_moment,
    embed_average,
    head_table,
    head_moment,
    head_average,
    in_weights,
    in_moment,
    in_average,
    out_weights,
    out_moment,
    out_average,
    vectors,
    vector_moment,
    vector_average,
):
    groups = lax.axis_size("fsdp")
    member = lax.axis_index("fsdp")
    batches = token_ids.shape[0]
    seq = token_ids.shape[2]
    vocab_rows, width = embed_table.shape
    hidden = out_weights.shape[0] * groups - width
    head_size = width // HEADS
    rot = head_size // 4
    factor = 1.0 / math.sqrt(head_size)
    vocab_start = member * vocab_rows
    columns = jnp.arange(vocab_rows, dtype=jnp.int32) + vocab_start
    embed_low = embed_table.astype(NARROW)
    head_low = head_table.astype(NARROW)
    all_tokens, all_marks, all_buffers, all_lengths = (
        lax.all_gather(token_ids, ("dp", "fsdp"), axis=1, tiled=True),
        lax.all_gather(loss_mask, ("dp", "fsdp"), axis=1, tiled=True),
        lax.all_gather(buffer_ids, ("dp", "fsdp"), axis=1, tiled=True),
        lax.all_gather(lengths, ("dp", "fsdp"), axis=1, tiled=True),
    )
    slot_rule = jax.vmap(jax.vmap(functools.partial(slot_info, buffer_count=NSEG)))
    shares_all, successors_all, offsets_all, counted = slot_rule(
        all_tokens, all_marks, all_lengths, all_buffers
    )
    count = jnp.maximum(jnp.sum(counted), 1.0)
    first_slot = lax.axis_index("dp") * groups

    def own_group(values):
        return lax.dynamic_slice_in_dim(values, first_slot, groups, 1)

    group_tokens = own_group(all_tokens)
    shares = own_group(shares_all)
    successors = own_group(successors_all)
    offsets = own_group(offsets_all)
    places = jnp.arange(seq, dtype=jnp.int32)
    rows_all = groups * seq
    block = math.gcd(rows_all, 512)
    blocks = rows_all // block
    loss_part = jnp.zeros((), FLOAT)
    embed_grad = jnp.zeros((vocab_rows, width), FLOAT)
    head_grad = jnp.zeros((vocab_rows, width), FLOAT)
    in_acc = jnp.zeros(in_weights.shape, FLOAT)
    out_acc = jnp.zeros(out_weights.shape, FLOAT)
    vector_acc = jnp.zeros(vectors.shape, FLOAT)
    for batch in range(batches):
        in_full, out_full, vector_full = (
            lax.all_gather(in_weights.astype(NARROW), "fsdp", axis=0, tiled=True),
            lax.all_gather(out_weights.astype(NARROW), "fsdp", axis=0, tiled=True),
            lax.all_gather(vectors.astype(NARROW), "fsdp", axis=0, tiled=True),
        )
        parts = vector_parts(vector_full.astype(FLOAT), width, hidden)
        buffers = buffer_ids[batch, 0]
        allowed = (buffers[:, None] == buffers[None, :]) & (places[None, :] <= places[:, None])
        cosine, sine = rotary_tables(
            lax.dynamic_index_in_dim(offsets[batch], member, 0, keepdims=False), rot
        )
        flat_tokens = group_tokens[batch].reshape(rows_all)
        local_rows = flat_tokens - vocab_start
        inside = (local_rows >= 0) & (local_rows < vocab_rows)
        safe_rows = jnp.clip(local_rows, 0, vocab_rows - 1)
        rows = jnp.take(embed_low, safe_rows, axis=0).astype(FLOAT)
        resid = lax.psum_scatter(
            jnp.where(inside[:, None], rows, 0.0).astype(jnp.bfloat16),
            "fsdp",
            scatter_dimension=0,
            tiled=True,
        ).astype(jnp.float32)
        layer_out, kept = layer_forward(
            resid, in_full, out_full, parts, allowed, cosine, sine, factor
        )
        final, unit_last, scale_last = norm_forward(layer_out, parts[4], parts[5])
        group_hidden = lax.all_gather(final.astype(NARROW), "fsdp", axis=0, tiled=True)
        hidden_blocks = group_hidden.reshape(blocks, block, width)
        target_blocks = successors[batch].reshape(blocks, block)
        tops, totals, hits = lax.map(
            functools.partial(logit_stats, head_low=head_low, columns=columns),
            (hidden_blocks, target_blocks),
        )
        tops, totals, hits = combined_all(
            (tops.reshape(rows_all), totals.reshape(rows_all), hits.reshape(rows_all)),
            "fsdp",
            combine_softmax,
        )
        logsum = tops + jnp.log(totals)
        weight_rows = shares[batch].reshape(rows_all) / count
        loss_part = loss_part + jnp.sum(
            lax.dynamic_slice_in_dim(weight_rows * (logsum - hits), member * seq, seq)
        )

        def head_step(carry, items):
            hidden_rows, target, weight, total_log = items
            logits = lax.dot_general(
                hidden_rows, head_low, LAST_CONTRACT, preferred_element_type=FLOAT
            )
            probs = jnp.exp(logits - total_log[:, None])
            onehot = jnp.where(columns[None, :] == target[:, None], 1.0, 0.0)
            logit_grad = (weight[:, None] * (probs - onehot)).astype(NARROW)
            back = jnp.dot(logit_grad, head_low, preferred_element_type=FLOAT)
            carry = carry + lax.dot_general(
                logit_grad, hidden_rows, ROWS_CONTRACT, preferred_element_type=FLOAT
            )
            return (carry, back)

        head_grad, back_blocks = lax.scan(
            head_step,
            head_grad,
            (
                hidden_blocks,
                target_blocks,
                weight_rows.reshape(blocks, block),
                logsum.reshape(blocks, block),
            ),
        )
        final_grad = lax.psum_scatter(
            back_blocks.reshape(rows_all, width), "fsdp", scatter_dimension=0, tiled=True
        )
        layer_grad, gain_last_grad, bias_last_grad = norm_backward(
            final_grad, unit_last, scale_last, parts[4]
        )
        in_back, out_back = (
            lax.all_gather(in_weights.astype(NARROW), "fsdp", axis=0, tiled=True),
            lax.all_gather(out_weights.astype(NARROW), "fsdp", axis=0, tiled=True),
        )
        resid_grad, in_grad, out_grad, small = layer_backward(
            layer_grad, in_back, out_back, parts, kept, allowed, cosine, sine, factor
        )
        vector_grad = jnp.concatenate(
            [
                small[0],
                small[1],
                small[2],
                small[3],
                gain_last_grad,
                bias_last_grad,
                small[4],
                small[5],
                small[6],
                small[7],
            ]
        )
        group_grad = lax.all_gather(resid_grad.astype(NARROW), "fsdp", axis=0, tiled=True)
        segment_rows = jnp.where(inside, local_rows, vocab_rows)
        embed_grad = (
            embed_grad
            + jax.ops.segment_sum(
                group_grad.astype(FLOAT), segment_rows, num_segments=vocab_rows + 1
            )[:vocab_rows]
        )
        in_part, out_part, vector_part = (
            lax.psum_scatter(in_grad, "fsdp", scatter_dimension=0, tiled=True),
            lax.psum_scatter(out_grad, "fsdp", scatter_dimension=0, tiled=True),
            lax.psum_scatter(vector_grad, "fsdp", scatter_dimension=0, tiled=True),
        )
        in_acc = in_acc + in_part
        out_acc = out_acc + out_part
        vector_acc = vector_acc + vector_part
    embed_sub, head_sub = (
        lax.psum_scatter(embed_grad, "dp", scatter_dimension=0, tiled=True),
        lax.psum_scatter(head_grad, "dp", scatter_dimension=0, tiled=True),
    )
    layer_grads = lax.psum((in_acc, out_acc, vector_acc), "dp")
    table_square = jnp.sum(embed_sub * embed_sub) + jnp.sum(head_sub * head_sub)
    layer_square = jnp.zeros((), FLOAT)
    for grad in layer_grads:
        layer_square = layer_square + jnp.sum(grad * grad)
    loss, square_all = lax.psum(
        (loss_part, table_square + layer_square / lax.axis_size("dp")), ("dp", "fsdp")
    )
    grad_norm = jnp.sqrt(square_all)
    clip_factor = CLIP_LEVEL / jnp.maximum(grad_norm, CLIP_LEVEL)
    base = math.sqrt(NPARAM) / CLIP_LEVEL
    sub_rows = embed_moment.shape[0]
    sub_start = lax.axis_index("dp") * sub_rows
    embed_part = lax.dynamic_slice_in_dim(embed_table, sub_start, sub_rows, 0)
    head_part = lax.dynamic_slice_in_dim(head_table, sub_start, sub_rows, 0)
    embed_new, embed_mom, embed_avg = update_rule(
        embed_part, embed_sub, embed_moment, embed_average, base, clip_factor
    )
    head_new, head_mom, head_avg = update_rule(
        head_part, head_sub, head_moment, head_average, base / math.sqrt(width), clip_factor
    )
    embed_whole, head_whole = (
        lax.all_gather(embed_new, "dp", axis=0, tiled=True),
        lax.all_gather(head_new, "dp", axis=0, tiled=True),
    )
    in_new, in_mom, in_avg = update_rule(
        in_weights, layer_grads[0], in_moment, in_average, base / math.sqrt(width), clip_factor
    )
    out_new, out_mom, out_avg = update_rule(
        out_weights, layer_grads[1], out_moment, out_average, base / math.sqrt(width), clip_factor
    )
    vec_new, vec_mom, vec_avg = update_rule(
        vectors, layer_grads[2], vector_moment, vector_average, 0.3 * base, clip_factor
    )
    return (
        embed_whole,
        embed_mom,
        embed_avg,
        head_whole,
        head_mom,
        head_avg,
        in_new,
        in_mom,
        in_avg,
        out_new,
        out_mom,
        out_avg,
        vec_new,
        vec_mom,
        vec_avg,
        loss,
        grad_norm,
    )


def solution(mesh):
    placed = (
        P(None, ("dp", "fsdp"), None),
        P(None, ("dp", "fsdp"), None),
        P(None, ("dp", "fsdp")),
        P(None, ("dp", "fsdp"), None),
        P("fsdp", None),
        P(("fsdp", "dp"), None),
        P(("fsdp", "dp"), None),
        P("fsdp", None),
        P(("fsdp", "dp"), None),
        P(("fsdp", "dp"), None),
        P("fsdp", None),
        P("fsdp", None),
        P("fsdp", None),
        P("fsdp", None),
        P("fsdp", None),
        P("fsdp", None),
        P("fsdp"),
        P("fsdp"),
        P("fsdp"),
    )
    return jax.shard_map(
        shards,
        mesh=mesh,
        in_specs=placed,
        out_specs=(
            P("fsdp", None),
            P(("fsdp", "dp"), None),
            P(("fsdp", "dp"), None),
            P("fsdp", None),
            P(("fsdp", "dp"), None),
            P(("fsdp", "dp"), None),
            P("fsdp", None),
            P("fsdp", None),
            P("fsdp", None),
            P("fsdp", None),
            P("fsdp", None),
            P("fsdp", None),
            P("fsdp"),
            P("fsdp"),
            P("fsdp"),
            P(),
            P(),
        ),
        check_vma=False,
    )
```

profile of v0, /device:TPU:0, one launch (start us, length us, event | category | flops | bytes accessed | tf_op | source)
XLA Modules:
  0.0 1649.7 jit_solution(2005950233702127580)
XLA Ops:
  7.2 43.5 %all_gather.64 = s32[2,32,128]{2,0,1:T(2,128)S(1)} all-gather(s32[2,1,128]{2,0,1:T(2,128)} %bitcast.342), channel_id=1, replica_groups=mesh['dp'=4,'fsdp'=8] {'dp','fsdp'}, dimensions={1}, use_global_device_ids=true | all-gather | bytes 33792 | tf_op jit(solution)/shard_map/all_gather | solution.py:293
  51.5 8.2 convert_element_type.170
  59.7 7.6 gather_fusion.1
  69.1 7.7 gather_fusion
  82.0 26.3 %all-reduce.2 = bf16[7680]{0:T(1024)(128)(2,1)S(1)} all-reduce(bf16[7680]{0:T(1024)(128)(2,1)S(1)} %dynamic-update-slice), channel_id=1, replica_groups=mesh['dp'=4,'fsdp'=8] {'fsdp'}, use_global_device_ids=true, to_apply=%add.2 | all-reduce | flops 7680 | bytes 30720
  108.3 36.7 %all_gather.67 = s32[2,32,128]{2,0,1:T(2,128)S(1)} all-gather(s32[2,1,128]{2,0,1:T(2,128)S(1)} %bitcast.339), channel_id=1, replica_groups=mesh['dp'=4,'fsdp'=8] {'dp','fsdp'}, dimensions={1}, use_global_device_ids=true | all-gather | bytes 33792 | tf_op jit(solution)/shard_map/all_gather | solution.py:295
  150.0 25.1 %all-gather.18.cloned.1.call-done = bf16[512,3584]{1,0:T(8,128)(2,1)} async-done(((bf16[64,3584]{1,0:T(8,128)(2,1)}), bf16[512,3584]{1,0:T(8,128)(2,1)}) %all-gather.18.cloned.1.call-update) | async-done | bytes 3670032 | tf_op jit(solution)/shard_map/all_gather | solution.py:324
  179.1 5.2 fusion.70
  184.3 25.7 %all-gather.20.cloned.1.call-done = bf16[2560,512]{1,0:T(8,128)(2,1)} async-done(((bf16[320,512]{1,0:T(8,128)(2,1)}), bf16[2560,512]{1,0:T(8,128)(2,1)}) %all-gather.20.cloned.1.call-update) | async-done | bytes 2621456 | tf_op jit(solution)/shard_map/all_gather | solution.py:325
  216.8 5.3 fusion.62
  224.1 8.2 convert_element_type.188
  232.3 39.3 %all-gather = s32[32,1,2]{2,1,0:T(1,128)S(1)} all-gather(s32[1,1,2]{2,1,0:T(1,128)S(1)} %bitcast.344), channel_id=1, replica_groups=mesh['dp'=4,'fsdp'=8] {'dp','fsdp'}, dimensions={0}, use_global_device_ids=true | all-gather | bytes 264 | tf_op jit(solution)/shard_map/all_gather | solution.py:296
  271.8 36.7 %all_gather.69 = s32[2,32,128]{2,0,1:T(2,128)S(1)} all-gather(s32[2,1,128]{2,0,1:T(2,128)S(1)} %bitcast.343), channel_id=1, replica_groups=mesh['dp'=4,'fsdp'=8] {'dp','fsdp'}, dimensions={1}, use_global_device_ids=true | all-gather | bytes 33792 | tf_op jit(solution)/shard_map/all_gather | solution.py:294
  310.6 36.8 %while.97 = (s32[]{:T(128)}, f32[2,512]{1,0:T(2,128)S(1)}, f32[2,512]{1,0:T(2,128)S(1)}, f32[2,512]{1,0:T(2,128)S(1)}, bf16[2,512,512]{2,1,0:T(8,128)(2,1)}, /*i...) while((s32[]{:T(128)}, f32[2,512]{1,0:T(2,128)S(1)}, ...), condition=%wide.region_41.43_spmd.clone, body=%wide.region_37.42_spmd.clone.sunk | while | flops 3316044544 | bytes 32795908 | solution.py:352
  310.7 11.4 fusion.305
  322.2 6.8 select_reduce_fusion.8
  329.1 11.4 fusion.305
  340.6 6.8 select_reduce_fusion.8
  347.5 14.0 all-gather.4
  361.6 14.0 all-gather.5
  375.6 14.0 all-gather.6
  389.7 36.8 %while.96 = (s32[]{:T(128)}, f32[2,512]{1,0:T(2,128)S(1)}, f32[2,512]{1,0:T(2,128)S(1)}, f32[2,512]{1,0:T(2,128)S(1)}, bf16[2,512,512]{2,1,0:T(8,128)(2,1)}, /*i...) while((s32[]{:T(128)}, f32[2,512]{1,0:T(2,128)S(1)}, ...), condition=%wide.region_16.18_spmd.clone, body=%wide.region_12.17_spmd.clone.sunk | while | flops 3316044544 | bytes 32795908 | solution.py:352
  389.7 11.4 fusion.303
  401.2 6.8 select_reduce_fusion.7
  408.1 11.4 fusion.303
  419.6 6.8 select_reduce_fusion.7
  426.5 14.1 all-gather.1
  440.7 14.0 all-gather.2
  454.7 14.2 all-gather.3
  471.1 50.1 %while.99 = (s32[]{:T(128)}, f32[6288,512]{1,0:T(8,128)}, f32[2,512,512]{2,1,0:T(8,128)S(1)}, f32[2,512]{1,0:T(2,128)S(1)}, bf16[2,512,512]{2,1,0:T(8,128)(2,1)S...) while((s32[]{:T(128)}, f32[6288,512]{1,0:T(8,128)}, ...), condition=%wide.region_20.22_spmd.clone, body=%wide.region_19.21_spmd.clone.sunk | while | flops 9915930624 | bytes 111631120 | solution.py:381
  471.2 9.2 multiply_convert_fusion.5
  480.4 9.7 select_add_fusion.2
  490.1 3.6 fusion.319
  493.7 9.2 multiply_convert_fusion.5
  503.0 13.0 select_add_fusion.2
  517.6 3.6 fusion.319
  524.3 53.9 %while.98 = (s32[]{:T(128)}, f32[6288,512]{1,0:T(8,128)}, f32[2,512,512]{2,1,0:T(8,128)}, f32[2,512]{1,0:T(2,128)S(1)}, bf16[2,512,512]{2,1,0:T(8,128)(2,1)S(1)}...) while((s32[]{:T(128)}, f32[6288,512]{1,0:T(8,128)}, ...), condition=%wide.region_45.47_spmd.clone, body=%wide.region_44.46_spmd.clone.sunk | while | flops 9912711168 | bytes 188898080 | solution.py:381
  524.3 9.5 multiply_convert_fusion.4
  533.8 7.0 convolution_add_fusion.9
  540.8 10.5 fusion.312
  551.4 9.3 multiply_convert_fusion.4
  560.7 6.9 convolution_add_fusion.9
  567.7 10.5 fusion.312
  580.5 30.9 %reduce-scatter.17.cloned.1.call-done = f32[128,512]{1,0:T(8,128)} async-done(((f32[1024,512]{1,0:T(8,128)}), f32[128,512]{1,0:T(8,128)}) %reduce-scatter.17.cloned.1.call-update) | async-done | bytes 262160 | tf_op jit(solution)/shard_map/reduce_scatter | solution.py:391
  658.4 3.4 maximum_add_fusion
  669.6 26.8 %all-reduce.5 = f32[7680]{0:T(1024)S(1)} all-reduce(f32[7680]{0:T(1024)S(1)} %add.577), channel_id=13, replica_groups=mesh['dp'=4,'fsdp'=8] {'fsdp'}, use_global_device_ids=true, to_apply=%region_76.78.clone | all-reduce | flops 7680 | bytes 61440
  696.5 9.7 psum.37
  706.2 13.0 scatter_custom_fusion.1
  719.2 13.2 scatter_custom_fusion
  732.5 14.8 slice_add_fusion
  747.3 8.1 reduce-scatter.21.cloned.1.call-done
  755.4 80.3 %reduce-scatter.19.cloned.1.call-done = f32[64,3584]{1,0:T(8,128)} async-done(((f32[512,3584]{1,0:T(8,128)}), f32[64,3584]{1,0:T(8,128)}) %reduce-scatter.19.cloned.1.call-update) | async-done | bytes 917520 | tf_op jit(solution)/shard_map/reduce_scatter | solution.py:427
  835.8 451.9 %fusion.242 = (f32[1584,512]{1,0:T(8,128)}, f32[1584,512]{1,0:T(8,128)S(1)}) fusion(f32[6288,512]{1,0:T(8,128)} %slice_add_fusion, f32[6288,512]{1,0:T(8,128)} %get-tuple-element.571), kind=kCustom, calls=%all-reduce-scatter.2 | all-reduce-scatter fusion | flops 6488065 | bytes 32244224
  1295.9 9.7 concatenate.68
  1305.6 7.5 concatenate.69
  1313.1 3.4 multiply_reduce_fusion.1
  1325.1 39.9 %all-reduce.8 = (f32[]{:T(128)}, f32[]{:T(128)}) all-reduce(f32[]{:T(128)S(6)} %add.555, f32[]{:T(128)S(6)} %add.572), channel_id=1, replica_groups=mesh['dp'=4,'fsdp'=8] {'dp','fsdp'}, use_global_device_ids=true, to_apply=%region_89.91 | all-reduce | flops 2 | bytes 16 | tf_op jit(solution)/shard_map/psum | solution.py:443
  1365.7 9.9 add_multiply_fusion.1
  1375.8 9.9 add_multiply_fusion
  1387.2 3.6 add_multiply_fusion.3
  1392.6 109.1 %all-gather.30.cloned.1.call-done = f32[4,1572,512]{2,1,0:T(8,128)} async-done(((f32[1,1572,512]{2,1,0:T(8,128)}), f32[4,1572,512]{2,1,0:T(8,128)}) %all-gather.30.cloned.1.call-update) | async-done | bytes 12877840 | tf_op jit(solution)/shard_map/all_gather | solution.py:460
  1501.7 13.2 reshape.596
  1515.0 114.4 %all-gather.32.cloned.1.call-done = f32[4,1572,512]{2,1,0:T(8,128)} async-done(((f32[1,1572,512]{2,1,0:T(8,128)}), f32[4,1572,512]{2,1,0:T(8,128)}) %all-gather.32.cloned.1.call-update) | async-done | bytes 12877840 | tf_op jit(solution)/shard_map/all_gather | solution.py:461
  1629.4 12.4 reshape.598
  (644 shorter events, 103.6 us)
Async XLA Ops:
  7.2 138.5 %reduce-scatter.15.cloned.1.call-start = ((), (), s32[]{:S(2)}) async-start(), calls=%async_computation.12 | async-start | bytes 1179648 | tf_op jit(solution)/shard_map/reduce_scatter | solution.py:339
  69.0 77.7 %reduce-scatter.11.cloned.1.call-start = ((), (), s32[]{:S(2)}) async-start(), calls=%async_computation.6 | async-start | bytes 1179648 | tf_op jit(solution)/shard_map/reduce_scatter | solution.py:339
  76.8 31.4 %copy-start.130 = (s32[2,1,128]{2,1,0:T(1,128)S(1)}, s32[2,1,128]{2,1,0:T(1,128)}, u32[]{:S(2)}) copy-start(s32[2,1,128]{2,1,0:T(1,128)} %param.36) | copy-start | bytes 3076
  78.5 96.6 %all-gather.18.cloned.1.call-start = ((), (), s32[]{:S(2)}) async-start(), calls=%async_computation.7 | async-start | bytes 4128768 | tf_op jit(solution)/shard_map/all_gather | solution.py:324
  79.4 130.6 %all-gather.20.cloned.1.call-start = ((), (), s32[]{:S(2)}) async-start(), calls=%async_computation.8 | async-start | bytes 2949120 | tf_op jit(solution)/shard_map/all_gather | solution.py:325
  80.3 230.3 %all-gather.26.cloned.1.call-start = ((), (), s32[]{:S(2)}) async-start(), calls=%async_computation.13 | async-start | bytes 1179648 | tf_op jit(solution)/shard_map/all_gather | solution.py:349
  145.5 32.4 %copy-start.74 = (f32[128,8]{0,1:T(8,128)}, f32[128,8]{0,1:T(8,128)S(1)}, u32[]{:S(2)}) copy-start(f32[128,8]{0,1:T(8,128)S(1)} %get-tuple-element.909) | copy-start | bytes 12292
  145.5 32.4 %copy-start.76 = (f32[128,8]{0,1:T(8,128)}, f32[128,8]{0,1:T(8,128)S(1)}, u32[]{:S(2)}) copy-start(f32[128,8]{0,1:T(8,128)S(1)} %get-tuple-element.910) | copy-start | bytes 12292
  145.5 69.4 %copy-start.78 = (f32[128,8]{0,1:T(8,128)}, f32[128,8]{0,1:T(8,128)S(1)}, u32[]{:S(2)}) copy-start(f32[128,8]{0,1:T(8,128)S(1)} %get-tuple-element.917) | copy-start | bytes 12292
  145.5 69.4 %copy-start.80 = (f32[128,8]{0,1:T(8,128)}, f32[128,8]{0,1:T(8,128)S(1)}, u32[]{:S(2)}) copy-start(f32[128,8]{0,1:T(8,128)S(1)} %get-tuple-element.918) | copy-start | bytes 12292
  145.5 67.1 %copy-start.82 = (f32[512]{0:T(512)}, f32[512]{0:T(512)S(1)}, u32[]{:S(2)}) copy-start(f32[512]{0:T(512)S(1)} %get-tuple-element.883) | copy-start | bytes 6148
  145.5 67.1 %copy-start.87 = (f32[512]{0:T(512)}, f32[512]{0:T(512)S(1)}, u32[]{:S(2)}) copy-start(f32[512]{0:T(512)S(1)} %get-tuple-element.884) | copy-start | bytes 6148
  145.5 71.2 %copy-start.84 = (f32[512]{0:T(512)}, f32[512]{0:T(512)S(1)}, u32[]{:S(2)}) copy-start(f32[512]{0:T(512)S(1)} %get-tuple-element.885) | copy-start | bytes 6148
  145.5 71.2 %copy-start.89 = (f32[512]{0:T(512)}, f32[512]{0:T(512)S(1)}, u32[]{:S(2)}) copy-start(f32[512]{0:T(512)S(1)} %get-tuple-element.886) | copy-start | bytes 6148
  145.6 77.4 %copy-start.68 = (f32[512]{0:T(512)}, f32[512]{0:T(512)S(1)}, u32[]{:S(2)}) copy-start(f32[512]{0:T(512)S(1)} %get-tuple-element.879) | copy-start | bytes 6148
  147.8 31.3 %copy-start.107 = (f32[128]{0:T(128)}, f32[128]{0:T(128)S(1)}, u32[]{:S(2)}) copy-start(f32[128]{0:T(128)S(1)} %broadcast_multiply_fusion.7) | copy-start | bytes 1540
  148.9 67.9 %copy-start.125 = (f32[128]{0:T(128)}, f32[128]{0:T(128)S(1)}, u32[]{:S(2)}) copy-start(f32[128]{0:T(128)S(1)} %broadcast_multiply_fusion.15) | copy-start | bytes 1540
  150.0 29.1 %copy-start.118 = (f32[128]{0:T(128)}, f32[128]{0:T(128)S(1)}, u32[]{:S(2)}) copy-start(f32[128]{0:T(128)S(1)} %add_rsqrt_fusion.1) | copy-start | bytes 1540
  150.0 66.8 %copy-start.131 = (f32[128]{0:T(128)}, f32[128]{0:T(128)S(1)}, u32[]{:S(2)}) copy-start(f32[128]{0:T(128)S(1)} %add_rsqrt_fusion.3) | copy-start | bytes 1540
  179.0 31.0 %copy-start.46 = (bf16[128,512]{1,0:T(8,128)(2,1)}, bf16[128,512]{1,0:T(8,128)(2,1)S(1)}, u32[]{:S(2)}) copy-start(bf16[128,512]{1,0:T(8,128)(2,1)S(1)} %copy.146) | copy-start | bytes 393220
  184.2 28.3 %copy-start.50 = (bf16[128,2048]{1,0:T(8,128)(2,1)}, bf16[128,2048]{1,0:T(8,128)(2,1)S(1)}, u32[]{:S(2)}) copy-start(bf16[128,2048]{1,0:T(8,128)(2,1)S(1)} %get-tuple-element.919) | copy-start | bytes 1572868
  184.3 28.4 %copy-start.38 = (bf16[128,512]{1,0:T(8,128)(2,1)S(1)}, bf16[128,512]{1,0:T(8,128)(2,1)}, u32[]{:S(2)}) copy-start(bf16[128,512]{1,0:T(8,128)(2,1)} %reduce-scatter.11.cloned.1.call-done) | copy-start | bytes 393220
  212.4 10.7 copy-start.21
  212.4 10.6 copy-start.110
  212.6 10.4 copy-start.121
  223.9 165.7 %all-gather.22.cloned.1.call-start = ((), (), s32[]{:S(2)}) async-start(), calls=%async_computation.9 | async-start | bytes 1179648 | tf_op jit(solution)/shard_map/all_gather | solution.py:349
  224.1 47.7 %copy-start.143 = (s32[2,1,128]{2,1,0:T(1,128)S(1)}, s32[2,1,128]{2,1,0:T(1,128)}, u32[]{:S(2)}) copy-start(s32[2,1,128]{2,1,0:T(1,128)} %param.34) | copy-start | bytes 3076
  310.1 268.4 %reduce-scatter.13.cloned.1.call-start = ((), (), s32[]{:S(2)}) async-start(), calls=%async_computation.10 | async-start | bytes 2359296 | tf_op jit(solution)/shard_map/reduce_scatter | solution.py:391
  347.5 42.2 %copy-start.53 = (s32[2,512]{1,0:T(2,128)}, s32[2,512]{1,0:T(2,128)S(1)}, u32[]{:S(2)}) copy-start(s32[2,512]{1,0:T(2,128)S(1)} %get-tuple-element.1528) | copy-start | bytes 12292
  426.5 44.6 %copy-start.6 = (bf16[2,512,512]{2,1,0:T(8,128)(2,1)S(1)}, bf16[2,512,512]{2,1,0:T(8,128)(2,1)}, u32[]{:S(2)}) copy-start(bf16[2,512,512]{2,1,0:T(8,128)(2,1)} %get-tuple-element.1488) | copy-start | bytes 3145732
  471.1 51.5 %copy-start.94 = (f32[1,8,128]{2,1,0:T(8,128)S(1)}, f32[1,8,128]{2,1,0:T(8,128)}, u32[]{:S(2)}) copy-start(f32[1,8,128]{2,1,0:T(8,128)} %get-tuple-element.829) | copy-start | bytes 12292
  471.1 51.5 %copy-start.93 = (f32[1024]{0:T(1024)S(1)}, f32[1024]{0:T(1024)}, u32[]{:S(2)}) copy-start(f32[1024]{0:T(1024)} %get-tuple-element.828) | copy-start | bytes 12292
  480.4 9.7 copy-start.2
  480.4 9.7 copy-start.4
  503.0 13.0 copy-start.2
  503.0 14.7 copy-start.4
  522.5 88.9 %reduce-scatter.17.cloned.1.call-start = ((), (), s32[]{:S(2)}) async-start(), calls=%async_computation.14 | async-start | bytes 2359296 | tf_op jit(solution)/shard_map/reduce_scatter | solution.py:391
  524.2 54.3 %copy-start.69 = (f32[512]{0:T(512)S(1)}, f32[512]{0:T(512)}, u32[]{:S(2)}) copy-start(f32[512]{0:T(512)} %copy-done.68) | copy-start | bytes 6148
  524.2 54.3 %copy-start.113 = (f32[128]{0:T(128)S(1)}, f32[128]{0:T(128)}, u32[]{:S(2)}) copy-start(f32[128]{0:T(128)} %copy-done.112) | copy-start | bytes 1540
  524.2 54.3 %copy-start.124 = (f32[128]{0:T(128)S(1)}, f32[128]{0:T(128)}, u32[]{:S(2)}) copy-start(f32[128]{0:T(128)} %copy-done.123) | copy-start | bytes 1540
  524.2 87.2 %copy-start.22 = (f32[128,512]{1,0:T(8,128)S(1)}, f32[128,512]{1,0:T(8,128)}, u32[]{:S(2)}) copy-start(f32[128,512]{1,0:T(8,128)} %copy-done.21) | copy-start | bytes 786436
  524.2 87.2 %copy-start.111 = (f32[128]{0:T(128)S(1)}, f32[128]{0:T(128)}, u32[]{:S(2)}) copy-start(f32[128]{0:T(128)} %copy-done.110) | copy-start | bytes 1540
  524.2 87.2 %copy-start.122 = (f32[128]{0:T(128)S(1)}, f32[128]{0:T(128)}, u32[]{:S(2)}) copy-start(f32[128]{0:T(128)} %copy-done.121) | copy-start | bytes 1540
  540.8 10.5 copy-start.1
  567.7 10.5 copy-start.1
  578.2 36.0 %copy-start.9 = (bf16[2560,512]{1,0:T(8,128)(2,1)S(1)}, bf16[2560,512]{1,0:T(8,128)(2,1)}, u32[]{:S(2)}) copy-start(bf16[2560,512]{1,0:T(8,128)(2,1)} %all-gather.20.cloned.1.call-done) | copy-start | bytes 7864324
  578.2 38.2 %copy-start.18 = (f32[8,128,128]{1,2,0:T(8,128)S(1)}, f32[8,128,128]{1,2,0:T(8,128)}, u32[]{:S(2)}) copy-start(f32[8,128,128]{1,2,0:T(8,128)} %copy-done.17) | copy-start | bytes 1572868
  578.2 38.2 %copy-start.73 = (f32[8,128]{1,0:T(8,128)S(1)}, f32[8,128]{1,0:T(8,128)}, u32[]{:S(2)}) copy-start(f32[8,128]{1,0:T(8,128)} %copy-done.72) | copy-start | bytes 12292
  578.2 128.0 %all-gather.28.cloned.1.call-start = ((), (), s32[]{:S(2)}) async-start(), calls=%async_computation.15 | async-start | bytes 1179648 | tf_op jit(solution)/shard_map/all_gather | solution.py:418
  580.5 38.8 %copy-start.103 = (bf16[128,8,8]{0,2,1:T(8,128)(2,1)S(1)}, bf16[128,8,8]{0,2,1:T(8,128)(2,1)}, u32[]{:S(2)}) copy-start(bf16[128,8,8]{0,2,1:T(8,128)(2,1)} %copy-done.102) | copy-start | bytes 49156
  628.2 10.0 copy-start.75
  628.2 10.0 copy-start.77
  648.7 70.5 %all-gather.24.cloned.1.call-start = ((), (), s32[]{:S(2)}) async-start(), calls=%async_computation.11 | async-start | bytes 1179648 | tf_op jit(solution)/shard_map/all_gather | solution.py:418
  649.3 106.2 %reduce-scatter.21.cloned.1.call-start = ((), (), s32[]{:S(2)}) async-start(), calls=%async_computation.17 | async-start | bytes 5898240 | tf_op jit(solution)/shard_map/reduce_scatter | solution.py:428
  654.6 181.1 %reduce-scatter.19.cloned.1.call-start = ((), (), s32[]{:S(2)}) async-start(), calls=%async_computation.16 | async-start | bytes 8257536 | tf_op jit(solution)/shard_map/reduce_scatter | solution.py:427
  662.0 657.2 %all-reduce.13.cloned.1.call-start = ((), (), s32[]{:S(2)}) async-start(), calls=%async_computation.20 | async-start | bytes 3145728 | tf_op jit(solution)/shard_map/psum | solution.py:438
  835.7 666.0 %all-gather.30.cloned.1.call-start = ((), (), s32[]{:S(2)}) async-start(), calls=%async_computation.18 | async-start | bytes 16138240 | tf_op jit(solution)/shard_map/all_gather | solution.py:460
  1287.6 18.0 %copy-start.7 = (f32[1584,512]{1,0:T(8,128)}, f32[1584,512]{1,0:T(8,128)S(1)}, u32[]{:S(2)}) copy-start(f32[1584,512]{1,0:T(8,128)S(1)} %get-tuple-element.807) | copy-start | bytes 9732100
  1288.6 7.3 collective-permute-start
  1292.0 13.7 collective-permute-start.1
  1375.7 10.1 copy-start.106
  1375.7 10.1 copy-start.128
  1375.7 10.1 copy-start.129
  1375.7 253.7 %all-gather.32.cloned.1.call-start = ((), (), s32[]{:S(2)}) async-start(), calls=%async_computation.19 | async-start | bytes 16138240 | tf_op jit(solution)/shard_map/all_gather | solution.py:461
  (109 other events, 468.3 us)
Sparse Core Ops, SparseCore 0:
  69.1 28.7 reduce-scatter.14
  100.8 30.6 reduce-scatter.10
  133.7 41.3 all-gather.17
  177.2 32.7 all-gather.19
  224.1 21.0 all-gather.25
  310.2 19.5 all-gather.21
  522.6 33.2 reduce-scatter.12
  578.3 33.0 reduce-scatter.16
  648.8 20.6 all-gather.27
  671.5 21.9 all-gather.23
  695.8 59.5 reduce-scatter.20
  757.6 78.0 reduce-scatter.18
  838.8 85.1 all-reduce.12
  1375.8 125.9 all-gather.29
  1504.2 125.2 all-gather.31
where the time goes:
time: 1660 us; the launch traced here: 1650 us
  blocking collectives  795 us (48%)
  waiting for transfers between devices  395 us (24%)
  matrix products  196 us (12%)
  other arithmetic  153 us (9%)
  local copies, waits for them, and re-layouts  75.4 us (5%)
  between operations  25.9 us (2%)
    unnamed x3, blocking collectives  505 us
    all_gather x1, waiting for transfers between devices, shards(): lax.all_gather(head_new, 'dp', axis=0, tiled=True)  114 us
    all_gather x1, waiting for transfers between devices, shards(): lax.all_gather(embed_new, 'dp', axis=0, tiled=True)  109 us
    all_gather x6, blocking collectives, combined_all(): everything = jax.tree.map(lambda part: lax.all_gather(part, axis), shard)  84.4 us
    reduce_scatter x1, waiting for transfers between devices, shards(): lax.psum_scatter(in_grad, 'fsdp', scatter_dimension=0, tiled=True)  80.3 us
    unnamed x325, local copies, waits for them, and re-layouts  54 us
    dot_general x4, matrix products, logit_stats(): lax.dot_general(hidden_rows, head_low, LAST_CONTRACT, preferred_element_t...  45.8 us
    all_gather x1, blocking collectives, shards(): lax.all_gather(token_ids, ('dp', 'fsdp'), axis=1, tiled=True)  43.5 us
  transfers between devices with their start and end apart: 17, of which 7 were waited for; matrix products, arithmetic and copies ran while one was open for 42% of the time, Pallas kernels for 0%

commit v1 on v0

v1 whole, which is shorter than its diff:
```python
import functools
import math

import jax
import jax.numpy as jnp
from jax import lax
from jax.experimental import pallas as pl
from jax.experimental.pallas import tpu as pltpu
from jax.sharding import PartitionSpec as P

HEADS = 8
NPARAM = 54664704
NSEG = 3


EPSILON = 1e-05
CLIP_LEVEL = 0.002
MOMENTUM = 0.5
DECAY = 0.5
NARROW = jnp.bfloat16
FLOAT = jnp.float32
ROWS_CONTRACT = (((0,), (0,)), ((), ()))
LAST_CONTRACT = (((1,), (1,)), ((), ()))


VMEM_LIMIT = 60 * 2**20


def slot_info(tokens, marks, length, buffers, buffer_count):
    seq = tokens.shape[0]
    places = jnp.arange(seq, dtype=jnp.int32)
    same_buffer = jnp.concatenate([buffers[1:] == buffers[:-1], jnp.zeros((1,), dtype=bool)])
    valid = jnp.where((marks == 1) & (places + 1 < length) & same_buffer, 1.0, 0.0).astype(FLOAT)
    member = buffers[None, :] == jnp.arange(buffer_count, dtype=jnp.int32)[:, None]
    weights = jnp.where(member, 1.0, 0.0).astype(FLOAT)
    tally = jnp.sum(weights * valid[None, :], axis=1)
    divisor = valid * jnp.sum(weights * tally[:, None], axis=0)
    counted = jnp.sum(jnp.where(tally > 0.5, 1.0, 0.0).astype(FLOAT))
    first = jnp.min(jnp.where(member, places[None, :], seq), axis=1)
    offset = places - jnp.sum(jnp.where(member, first[:, None], 0), axis=0)
    return (divisor.astype(jnp.int32), offset, counted.astype(jnp.int32))


def vector_parts(vectors, width, hidden):
    amounts = [width] * 6 + [3 * width, width, hidden, width]
    parts = []
    begin = 0
    for amount in amounts:
        parts.append(vectors[begin : begin + amount])
        begin = begin + amount
    return parts


def rotary_tables(offset, rot):
    half = rot // 2
    freqs = jnp.power(10000.0, -2.0 * jnp.arange(half, dtype=FLOAT) / rot)
    angles = offset.astype(FLOAT)[:, None] * freqs[None, :]
    return (jnp.cos(angles)[:, None, :], jnp.sin(angles)[:, None, :])


def rotate(values, cosine, sine, rot):
    half = rot // 2
    first = values[..., :half]
    second = values[..., half:rot]
    return jnp.concatenate(
        [first * cosine - second * sine, second * cosine + first * sine, values[..., rot:]], axis=-1
    )


def rotate_back(grads, cosine, sine, rot):
    half = rot // 2
    first = grads[..., :half]
    second = grads[..., half:rot]
    return jnp.concatenate(
        [first * cosine + second * sine, second * cosine - first * sine, grads[..., rot:]], axis=-1
    )


def norm_unit(values):
    mean = jnp.mean(values, axis=-1, keepdims=True)
    centred = values - mean
    scale = lax.rsqrt(jnp.mean(centred * centred, axis=-1, keepdims=True) + EPSILON)
    return (centred * scale, scale)


def norm_back(scaled, unit, scale):
    return scale * (
        scaled
        - jnp.mean(scaled, axis=-1, keepdims=True)
        - unit * jnp.mean(scaled * unit, axis=-1, keepdims=True)
    )


def gelu_slope(values):
    return (
        0.5 * (1.0 + lax.erf(values * 0.7071067811865476))
        + values * jnp.exp(-0.5 * values * values) * 0.3989422804014327
    )


def attention_scores(queries, keys, allowed, factor):
    scores = jnp.einsum("bqhd,bkhd->bhqk", queries, keys, preferred_element_type=FLOAT) * factor
    return jnp.where(allowed[:, None, :, :], scores, -1e30)


def layer_forward(resid, in_full, out_full, parts, allowed, cosine, sine, factor):
    rows, width = resid.shape
    batches = allowed.shape[0]
    seq = rows // batches
    head_size = width // HEADS
    rot = head_size // 4
    unit, scale = norm_unit(resid)
    input_one = (unit * parts[0] + parts[1]).astype(NARROW)
    input_two = (unit * parts[2] + parts[3]).astype(NARROW)
    triple = (
        jnp.dot(input_one, in_full[:, : 3 * width], preferred_element_type=FLOAT) + parts[6]
    ).reshape(rows, 3, HEADS, head_size)
    shape = (batches, seq, HEADS, head_size)
    queries = rotate(triple[:, 0], cosine, sine, rot).astype(NARROW).reshape(shape)
    keys = rotate(triple[:, 1], cosine, sine, rot).astype(NARROW).reshape(shape)
    values = triple[:, 2].astype(NARROW).reshape(shape)
    scores = attention_scores(queries, keys, allowed, factor)
    top = jnp.max(scores, axis=-1, keepdims=True)
    logsum = top + jnp.log(jnp.sum(jnp.exp(scores - top), axis=-1, keepdims=True))
    probs = jnp.exp(scores - logsum).astype(NARROW)
    mixed = (
        jnp.einsum("bhqk,bkhd->bqhd", probs, values, preferred_element_type=FLOAT)
        .astype(NARROW)
        .reshape(rows, width)
    )
    pre_act = jnp.dot(input_two, in_full[:, 3 * width :], preferred_element_type=FLOAT) + parts[8]
    activated = jax.nn.gelu(pre_act, approximate=False).astype(NARROW)
    joined = jnp.concatenate([mixed, activated], axis=1)
    result = resid + jnp.dot(joined, out_full, preferred_element_type=FLOAT) + parts[7] + parts[9]
    kept = (input_one, input_two, unit, scale, queries, keys, values, logsum, pre_act, joined)
    return (result, kept)


def layer_backward(grad_out, in_full, out_full, parts, kept, allowed, cosine, sine, factor):
    input_one, input_two, unit, scale, queries, keys, values, logsum, pre_act, joined = kept
    rows, width = grad_out.shape
    batches = allowed.shape[0]
    head_size = width // HEADS
    rot = head_size // 4
    grad_low = grad_out.astype(NARROW)
    out_grad = lax.dot_general(joined, grad_low, ROWS_CONTRACT, preferred_element_type=FLOAT)
    joined_grad = lax.dot_general(grad_low, out_full, LAST_CONTRACT, preferred_element_type=FLOAT)
    mixed_grad = joined_grad[:, :width].astype(NARROW).reshape(batches, -1, HEADS, head_size)
    pre_grad = joined_grad[:, width:] * gelu_slope(pre_act)
    pre_low = pre_grad.astype(NARROW)
    probs = jnp.exp(attention_scores(queries, keys, allowed, factor) - logsum)
    prob_grad = jnp.einsum("bqhd,bkhd->bhqk", mixed_grad, values, preferred_element_type=FLOAT)
    value_grad = jnp.einsum(
        "bhqk,bqhd->bkhd", probs.astype(NARROW), mixed_grad, preferred_element_type=FLOAT
    )
    score_grad = (
        probs * (prob_grad - jnp.sum(probs * prob_grad, axis=-1, keepdims=True)) * factor
    ).astype(NARROW)
    flat = (rows, HEADS, head_size)
    query_grad = rotate_back(
        jnp.einsum("bhqk,bkhd->bqhd", score_grad, keys, preferred_element_type=FLOAT).reshape(flat),
        cosine,
        sine,
        rot,
    )
    key_grad = rotate_back(
        jnp.einsum("bhqk,bqhd->bkhd", score_grad, queries, preferred_element_type=FLOAT).reshape(
            flat
        ),
        cosine,
        sine,
        rot,
    )
    qkv_grad = jnp.stack([query_grad, key_grad, value_grad.reshape(flat)], axis=1).reshape(
        rows, 3 * width
    )
    qkv_low = qkv_grad.astype(NARROW)
    in_grad = jnp.concatenate(
        [
            lax.dot_general(input_one, qkv_low, ROWS_CONTRACT, preferred_element_type=FLOAT),
            lax.dot_general(input_two, pre_low, ROWS_CONTRACT, preferred_element_type=FLOAT),
        ],
        axis=1,
    )
    back_one = lax.dot_general(
        qkv_low, in_full[:, : 3 * width], LAST_CONTRACT, preferred_element_type=FLOAT
    )
    back_two = lax.dot_general(
        pre_low, in_full[:, 3 * width :], LAST_CONTRACT, preferred_element_type=FLOAT
    )
    resid_grad = grad_out + norm_back(back_one * parts[0] + back_two * parts[2], unit, scale)
    residual_bias = jnp.sum(grad_out, axis=0)
    small = (
        jnp.sum(back_one * unit, axis=0),
        jnp.sum(back_one, axis=0),
        jnp.sum(back_two * unit, axis=0),
        jnp.sum(back_two, axis=0),
        jnp.sum(qkv_grad, axis=0),
        residual_bias,
        jnp.sum(pre_grad, axis=0),
        residual_bias,
    )
    return (resid_grad, in_grad, out_grad, small)


def block_rows(rows, cap):
    best = rows
    for size in range(8, cap + 1, 8):
        if rows % size == 0:
            best = size
    return best


def head_forward(table, hidden, target):
    vocab, width = table.shape
    rows = hidden.shape[0]
    tile = 512
    block = block_rows(vocab, 1100)
    blocks = vocab // block
    lines = -(-(2 * blocks + 1) // 8) * 8

    def kernel(table_ref, hidden_ref, target_ref, exps_ref, stats_ref):
        here = hidden_ref[...]
        places = lax.broadcasted_iota(jnp.int32, (block, tile), 0)
        hit = jnp.zeros((1, tile), FLOAT)
        for b in range(blocks):
            part = slice(b * block, (b + 1) * block)
            logits = lax.dot_general(
                table_ref[part, :], here, LAST_CONTRACT, preferred_element_type=FLOAT
            )
            top = jnp.max(logits, axis=0, keepdims=True)
            exps = jnp.exp(logits - top)
            stats_ref[0, b : b + 1, :] = top
            stats_ref[0, blocks + b : blocks + b + 1, :] = jnp.sum(exps, axis=0, keepdims=True)
            hit = hit + jnp.sum(
                jnp.where(places == target_ref[0] - b * block, logits, 0.0), axis=0, keepdims=True
            )
            exps_ref[part, :] = exps.astype(NARROW)
        stats_ref[0, 2 * blocks : 2 * blocks + 1, :] = hit

    whole = pl.BlockSpec(memory_space=pltpu.VMEM)
    tiles = rows // tile
    exps, stats = pl.pallas_call(
        kernel,
        grid=(tiles,),
        in_specs=[
            whole,
            pl.BlockSpec((tile, width), lambda i: (i, 0)),
            pl.BlockSpec((1, 1, tile), lambda i: (i, 0, 0)),
        ],
        out_specs=[
            pl.BlockSpec((vocab, tile), lambda i: (0, i)),
            pl.BlockSpec((1, lines, tile), lambda i: (i, 0, 0)),
        ],
        out_shape=[
            jax.ShapeDtypeStruct((vocab, rows), NARROW),
            jax.ShapeDtypeStruct((tiles, lines, tile), FLOAT),
        ],
        compiler_params=pltpu.CompilerParams(vmem_limit_bytes=VMEM_LIMIT),
        cost_estimate=pl.CostEstimate(
            flops=2 * vocab * rows * width,
            bytes_accessed=vocab * (rows + width) * 2,
            transcendentals=vocab * rows,
        ),
    )(table, hidden, target.reshape(tiles, 1, tile))
    tops = stats[:, :blocks].transpose(1, 0, 2).reshape(blocks, rows)
    totals = stats[:, blocks : 2 * blocks].transpose(1, 0, 2).reshape(blocks, rows)
    hits = stats[:, 2 * blocks].reshape(rows)
    return exps, tops, totals, hits


def head_back(table, exps, scales, weights, target):
    vocab, width = table.shape
    rows = exps.shape[1]
    tile = 256
    blocks = scales.shape[0]
    block = vocab // blocks

    def kernel(table_ref, exps_ref, scale_ref, weight_ref, target_ref, back_ref):
        places = lax.broadcasted_iota(jnp.int32, (block, tile), 0)
        total = jnp.zeros((tile, width), FLOAT)
        for b in range(blocks):
            part = slice(b * block, (b + 1) * block)
            grads = exps_ref[part, :].astype(FLOAT) * scale_ref[0, b : b + 1, :]
            grads = jnp.where(
                places == target_ref[0] - b * block, grads - weight_ref[0], grads
            ).astype(NARROW)
            total = total + lax.dot_general(
                grads, table_ref[part, :], ROWS_CONTRACT, preferred_element_type=FLOAT
            )
        back_ref[...] = total

    tiles = rows // tile
    line = pl.BlockSpec((1, 1, tile), lambda i: (i, 0, 0))
    return pl.pallas_call(
        kernel,
        grid=(tiles,),
        in_specs=[
            pl.BlockSpec(memory_space=pltpu.VMEM),
            pl.BlockSpec((vocab, tile), lambda i: (0, i)),
            pl.BlockSpec((1, blocks, tile), lambda i: (i, 0, 0)),
            line,
            line,
        ],
        out_specs=pl.BlockSpec((tile, width), lambda i: (i, 0)),
        out_shape=jax.ShapeDtypeStruct((rows, width), FLOAT),
        compiler_params=pltpu.CompilerParams(vmem_limit_bytes=VMEM_LIMIT),
        cost_estimate=pl.CostEstimate(
            flops=2 * vocab * rows * width,
            bytes_accessed=vocab * (rows + width) * 2,
            transcendentals=0,
        ),
    )(
        table,
        exps,
        scales.reshape(blocks, tiles, tile).transpose(1, 0, 2),
        weights.reshape(tiles, 1, tile),
        target.reshape(tiles, 1, tile),
    )


MESH = pl.DeviceIdType.MESH


def meet(peers):
    barrier = pltpu.get_barrier_semaphore()
    for peer in peers:
        pl.semaphore_signal(barrier, inc=1, device_id=peer, device_id_type=MESH)
    pl.semaphore_wait(barrier, len(peers))


class Place:
    def __init__(self, groups, replicas):
        self.groups = groups
        self.replicas = replicas
        self.chips = groups // 2
        self.replica = lax.axis_index("dp")
        self.member = lax.axis_index("fsdp")
        self.chip = self.member // 2
        self.core = self.member % 2
        self.sibling_member = self.chip * 2 + 1 - self.core

    def lane_chip(self, step):
        return lax.rem(self.chip + step, self.chips)

    def at(self, replica, member):
        return {"dp": replica, "fsdp": member}

    def lane(self, step):
        return self.at(self.replica, self.lane_chip(step) * 2 + self.core)

    def plane_replica(self, step):
        return lax.rem(self.replica + step, self.replicas)

    def plane(self, step):
        return self.at(self.plane_replica(step), self.member)

    def sibling(self):
        return self.at(self.replica, self.sibling_member)

    def lanes(self):
        return [self.lane(step) for step in range(1, self.chips)]

    def planes(self):
        return [self.plane(step) for step in range(1, self.replicas)]


def remote(source, target, send, recv, device):
    return pltpu.make_async_remote_copy(
        src_ref=source,
        dst_ref=target,
        send_sem=send,
        recv_sem=recv,
        device_id=device,
        device_id_type=MESH,
    )


def head_table_grad(table, hidden, logsum, weights, target, token_grad, groups, replicas):
    vocab, width = table.shape
    rows = hidden.shape[0]
    own = token_grad.shape[0]
    tile = math.gcd(rows, 2048)
    block = block_rows(vocab, 1100)
    tiles = rows // tile
    steps = vocab // block
    chips = groups // 2
    last = steps - 1
    when_plane, when_core = min(1, last), min(3, last)

    def kernel(
        table_ref,
        hidden_ref,
        logsum_ref,
        weight_ref,
        target_ref,
        own_ref,
        grad_ref,
        square_ref,
        all_ref,
        local_sem,
        lane_send,
        lane_recv,
        plane_send,
        plane_recv,
        core_send,
        core_recv,
    ):
        step = pl.program_id(0)
        place = Place(groups, replicas)
        me = place.replica * groups + place.member

        def slot(replica, member):
            return all_ref.at[replica * groups + member]

        def lane_copy(k):
            here = all_ref.at[me]
            return remote(own_ref, here, lane_send.at[k], lane_recv.at[k], place.lane(k))

        def lane_wait(k):
            back = lax.rem(place.chip + chips - k, chips) * 2 + place.core
            there = slot(place.replica, back)
            remote(there, there, lane_send.at[k], lane_recv.at[k], place.lane(k)).wait_recv()

        def plane_copy(k, c):
            here = slot(place.replica, c * 2 + place.core)
            return remote(here, here, plane_send.at[k, c], plane_recv.at[k, c], place.plane(k))

        def plane_wait(k, c):
            back = lax.rem(place.replica + replicas - k, replicas)
            there = slot(back, c * 2 + place.core)
            remote(
                there, there, plane_send.at[k, c], plane_recv.at[k, c], place.plane(k)
            ).wait_recv()

        def core_copy(r, c):
            here = slot(r, c * 2 + place.core)
            return remote(here, here, core_send.at[r, c], core_recv.at[r, c], place.sibling())

        def core_wait(r, c):
            there = slot(r, c * 2 + 1 - place.core)
            remote(
                there, there, core_send.at[r, c], core_recv.at[r, c], place.sibling()
            ).wait_recv()

        local = pltpu.make_async_copy(own_ref, all_ref.at[me], local_sem)

        @pl.when(step == 0)
        def _():
            meet(place.lanes() + place.planes() + [place.sibling()])
            local.start()
            for k in range(1, chips):
                lane_copy(k).start()

        @pl.when(step == when_plane)
        def _():
            local.wait()
            for k in range(1, chips):
                lane_wait(k)
            for c in range(chips):
                for k in range(1, replicas):
                    plane_copy(k, c).start()
                core_copy(place.replica, c).start()

        @pl.when(step == when_core)
        def _():
            for k in range(1, replicas):
                for c in range(chips):
                    plane_wait(k, c)
            for k in range(1, replicas):
                for c in range(chips):
                    core_copy(place.plane_replica(k), c).start()

        start = step * block
        part = table_ref[...].astype(NARROW)
        places = lax.broadcasted_iota(jnp.int32, (block, tile), 0)

        def lap(k, carry):
            here = hidden_ref[pl.ds(pl.multiple_of(k * tile, tile), tile), :]
            logits = lax.dot_general(part, here, LAST_CONTRACT, preferred_element_type=FLOAT)
            probs = jnp.exp(logits - logsum_ref[k])
            grads = jnp.where(
                places == target_ref[k] - start, probs - weight_ref[k], probs
            ).astype(NARROW)
            piece = jnp.dot(grads, here, preferred_element_type=FLOAT)

            @pl.when(k == 0)
            def _():
                grad_ref[...] = piece

            @pl.when(k > 0)
            def _():
                grad_ref[...] += piece

            return carry

        lax.fori_loop(0, tiles, lap, 0)
        squares = jnp.sum(jnp.square(grad_ref[...]), axis=0, keepdims=True)

        @pl.when(step == 0)
        def _():
            square_ref[...] = squares

        @pl.when(step > 0)
        def _():
            square_ref[...] += squares

        @pl.when(step == last)
        def _():
            for r in range(replicas):
                for c in range(chips):
                    core_wait(r, c)
            for k in range(1, chips):
                lane_copy(k).wait_send()
            for c in range(chips):
                for k in range(1, replicas):
                    plane_copy(k, c).wait_send()
                for r in range(replicas):
                    core_copy(r, c).wait_send()

    whole = pl.BlockSpec(memory_space=pltpu.VMEM)
    anywhere = pl.BlockSpec(memory_space=pl.ANY)
    shape = (tiles, 1, tile)
    dma = pltpu.SemaphoreType.DMA
    return pl.pallas_call(
        kernel,
        grid=(steps,),
        in_specs=[pl.BlockSpec((block, width), lambda i: (i, 0))] + [whole] * 4 + [anywhere],
        out_specs=[
            pl.BlockSpec((block, width), lambda i: (i, 0)),
            pl.BlockSpec((1, width), lambda i: (0, 0)),
            anywhere,
        ],
        out_shape=[
            jax.ShapeDtypeStruct((vocab, width), FLOAT),
            jax.ShapeDtypeStruct((1, width), FLOAT),
            jax.ShapeDtypeStruct((groups * replicas, own, width), NARROW),
        ],
        scratch_shapes=[
            dma,
            dma((chips,)),
            dma((chips,)),
            dma((replicas, chips)),
            dma((replicas, chips)),
            dma((replicas, chips)),
            dma((replicas, chips)),
        ],
        compiler_params=pltpu.CompilerParams(
            vmem_limit_bytes=VMEM_LIMIT, collective_id=1, has_side_effects=True
        ),
        cost_estimate=pl.CostEstimate(
            flops=4 * vocab * rows * width,
            bytes_accessed=vocab * width * 8 + rows * width * 4,
            transcendentals=vocab * rows,
        ),
    )(
        table,
        hidden,
        logsum.reshape(shape),
        weights.reshape(shape),
        target.reshape(shape),
        token_grad,
    )


def exchange_scalars(line, groups, replicas):
    amount = groups * replicas

    def kernel(own_ref, all_ref, local_sem, send_sem, recv_sem):
        place = Place(groups, replicas)
        me = place.replica * groups + place.member

        def device(index):
            return place.at(index // groups, lax.rem(index, groups))

        barrier = pltpu.get_barrier_semaphore()

        def greet(k, carry):
            pl.semaphore_signal(
                barrier, inc=1, device_id=device(lax.rem(me + k, amount)), device_id_type=MESH
            )
            return carry

        def copy(k):
            return remote(
                own_ref,
                all_ref.at[me],
                send_sem.at[k],
                recv_sem.at[k],
                device(lax.rem(me + k, amount)),
            )

        def begin(k, carry):
            copy(k).start()
            return carry

        def finish(k, carry):
            there = all_ref.at[lax.rem(me + amount - k, amount)]
            remote(there, there, send_sem.at[k], recv_sem.at[k], device(me)).wait_recv()
            copy(k).wait_send()
            return carry

        lax.fori_loop(1, amount, greet, 0)
        local = pltpu.make_async_copy(own_ref, all_ref.at[me], local_sem)
        local.start()
        pl.semaphore_wait(barrier, amount - 1)
        lax.fori_loop(1, amount, begin, 0)
        local.wait()
        lax.fori_loop(1, amount, finish, 0)

    whole = pl.BlockSpec(memory_space=pltpu.VMEM)
    dma = pltpu.SemaphoreType.DMA
    return pl.pallas_call(
        kernel,
        in_specs=[whole],
        out_specs=whole,
        out_shape=jax.ShapeDtypeStruct((amount,) + line.shape, line.dtype),
        scratch_shapes=[dma, dma((amount,)), dma((amount,))],
        compiler_params=pltpu.CompilerParams(collective_id=2, has_side_effects=True),
    )(line)


def chunk_lists(local, inside, chunk):
    chunks = local.shape[0] // chunk
    flags = inside.reshape(chunks, chunk)
    spots = jnp.arange(chunk, dtype=jnp.int32)
    ahead = (spots[:, None] < spots[None, :]).astype(NARROW)
    order = jnp.dot(flags.astype(NARROW), ahead, preferred_element_type=FLOAT).astype(jnp.int32)
    chosen = (order[:, None, :] == spots[None, :, None]) & flags[:, None, :]
    places = jnp.sum(jnp.where(chosen, spots[None, None, :], 0), axis=2)
    rows = jnp.sum(jnp.where(chosen, local.reshape(chunks, 1, chunk), 0), axis=2)
    return places, rows, jnp.sum(flags.astype(jnp.int32), axis=1)


def embed_table_grad(token_grads, places, rows, counts, vocab):
    chunks, chunk = places.shape
    width = token_grads.shape[-1]
    padded = vocab + 8
    unroll = 4

    def kernel(
        count_ref, place_ref, row_ref, tokens_ref, grad_ref, square_ref, wide_ref, total_ref, sem
    ):
        step = pl.program_id(0)

        @pl.when(step == 0)
        def _():
            total_ref[...] = jnp.zeros_like(total_ref)

        wide_ref[...] = tokens_ref[...].astype(FLOAT)
        amount = count_ref[step]

        def lap(j, carry):
            for u in range(unroll):
                spot = j * unroll + u
                row = jnp.where(spot < amount, row_ref[0, 0, spot], vocab)
                place = place_ref[0, 0, spot]
                total_ref[pl.ds(row, 1), :] += wide_ref[pl.ds(place, 1), :]
            return carry

        lax.fori_loop(0, (amount + unroll - 1) // unroll, lap, 0)

        @pl.when(step == chunks - 1)
        def _():
            out = pltpu.make_async_copy(total_ref.at[pl.ds(0, vocab), :], grad_ref, sem)
            out.start()
            square_ref[...] = jnp.sum(
                jnp.square(total_ref[pl.ds(0, vocab), :]), axis=0, keepdims=True
            )
            out.wait()

    line = pl.BlockSpec((1, 1, chunk), lambda i, c: (i, 0, 0), memory_space=pltpu.SMEM)
    return pl.pallas_call(
        kernel,
        grid_spec=pltpu.PrefetchScalarGridSpec(
            num_scalar_prefetch=1,
            grid=(chunks,),
            in_specs=[line, line, pl.BlockSpec((chunk, width), lambda i, c: (i, 0))],
            out_specs=[
                pl.BlockSpec(memory_space=pl.ANY),
                pl.BlockSpec((1, width), lambda i, c: (0, 0)),
            ],
            scratch_shapes=[
                pltpu.VMEM((chunk, width), FLOAT),
                pltpu.VMEM((padded, width), FLOAT),
                pltpu.SemaphoreType.DMA,
            ],
        ),
        out_shape=[
            jax.ShapeDtypeStruct((vocab, width), FLOAT),
            jax.ShapeDtypeStruct((1, width), FLOAT),
        ],
        compiler_params=pltpu.CompilerParams(vmem_limit_bytes=VMEM_LIMIT),
    )(
        counts,
        places.reshape(chunks, 1, chunk),
        rows.reshape(chunks, 1, chunk),
        token_grads.reshape(chunks * chunk, width),
    )


def update_rule(weight, grad, moment, average, rate, clip_factor):
    clipped = clip_factor * grad
    new_moment = MOMENTUM * moment + clipped
    new_weight = weight - rate * (clipped + MOMENTUM * new_moment)
    new_average = DECAY * average + (1.0 - DECAY) * new_weight
    return (new_weight, new_moment, new_average)


def table_update(table, grad, moment_low, moment, average, rate, clip):
    vocab, width = table.shape
    sub = moment.shape[0]
    block = block_rows(vocab, 1100)

    def whole_kernel(clip_ref, table_ref, grad_ref, moment_ref, new_ref):
        new_ref[...], _, _ = update_rule(
            table_ref[...],
            grad_ref[...],
            moment_ref[...].astype(FLOAT),
            table_ref[...],
            rate,
            clip_ref[0],
        )

    spec = pl.BlockSpec((block, width), lambda i: (i, 0))
    scalar = pl.BlockSpec(memory_space=pltpu.SMEM)
    new_table = pl.pallas_call(
        whole_kernel,
        grid=(vocab // block,),
        in_specs=[scalar, spec, spec, spec],
        out_specs=spec,
        out_shape=jax.ShapeDtypeStruct((vocab, width), FLOAT),
        compiler_params=pltpu.CompilerParams(vmem_limit_bytes=VMEM_LIMIT),
    )(clip, table, grad, moment_low)

    window = max(-(-(sub + sub * r % 8) // 8) * 8 for r in range(vocab // sub))
    tile = 256

    def own_kernel(
        clip_ref, table_ref, grad_ref, moment_ref, average_ref, moment_out, average_out, *scratch
    ):
        table_win, grad_win, sems = scratch
        begin = lax.axis_index("dp") * sub
        low = pl.multiple_of(begin // 8 * 8, 8)
        shift = begin - low
        copies = [
            pltpu.make_async_copy(table_ref.at[pl.ds(low, window), :], table_win, sems.at[0]),
            pltpu.make_async_copy(grad_ref.at[pl.ds(low, window), :], grad_win, sems.at[1]),
        ]
        for copy in copies:
            copy.start()
        for copy in copies:
            copy.wait()
        for first in range(0, sub, tile):
            size = min(tile, sub - first)
            span = min(-(-size // 8) * 8 + 8, window - first)
            amount = jnp.where(shift == 0, 0, span - shift)
            own_table = pltpu.roll(table_win[first : first + span, :], amount, 0)[:size]
            own_grad = pltpu.roll(grad_win[first : first + span, :], amount, 0)[:size]
            _, new_moment, new_average = update_rule(
                own_table,
                own_grad,
                moment_ref[first : first + size, :],
                average_ref[first : first + size, :],
                rate,
                clip_ref[0],
            )
            moment_out[first : first + size, :] = new_moment
            average_out[first : first + size, :] = new_average

    anywhere = pl.BlockSpec(memory_space=pl.ANY)
    whole = pl.BlockSpec(memory_space=pltpu.VMEM)
    state = jax.ShapeDtypeStruct((sub, width), FLOAT)
    new_moment, new_average = pl.pallas_call(
        own_kernel,
        in_specs=[scalar, anywhere, anywhere, whole, whole],
        out_specs=[whole, whole],
        out_shape=[state, state],
        scratch_shapes=[
            pltpu.VMEM((window, width), FLOAT),
            pltpu.VMEM((window, width), FLOAT),
            pltpu.SemaphoreType.DMA((2,)),
        ],
        compiler_params=pltpu.CompilerParams(vmem_limit_bytes=VMEM_LIMIT),
    )(clip, table, grad, moment, average)
    return new_table, new_moment, new_average


def shards(
    token_ids,
    loss_mask,
    lengths,
    buffer_ids,
    embed_table,
    embed_moment,
    embed_average,
    head_table,
    head_moment,
    head_average,
    in_weights,
    in_moment,
    in_average,
    out_weights,
    out_moment,
    out_average,
    vectors,
    vector_moment,
    vector_average,
):
    groups = lax.axis_size("fsdp")
    replicas = lax.axis_size("dp")
    member = lax.axis_index("fsdp")
    replica = lax.axis_index("dp")
    batches, _, seq = token_ids.shape
    vocab_rows, width = embed_table.shape
    hidden = out_weights.shape[0] * groups - width
    head_size = width // HEADS
    rot = head_size // 4
    factor = 1.0 / math.sqrt(head_size)
    vocab_start = member * vocab_rows
    own_rows = batches * seq
    rows_all = groups * own_rows

    tokens, marks, buffers = token_ids[:, 0], loss_mask[:, 0], buffer_ids[:, 0]
    divisor, offset, counted = jax.vmap(functools.partial(slot_info, buffer_count=NSEG))(
        tokens, marks, lengths[:, 0], buffers
    )
    packed = jnp.concatenate(
        [tokens, divisor, jnp.broadcast_to(jnp.sum(counted), (1, seq))], axis=0
    )
    everyone = lax.all_gather(packed, ("dp", "fsdp"))
    in_full, out_full, vector_full = (
        lax.all_gather(in_weights.astype(NARROW), "fsdp", axis=0, tiled=True),
        lax.all_gather(out_weights.astype(NARROW), "fsdp", axis=0, tiled=True),
        lax.all_gather(vectors.astype(NARROW), "fsdp", axis=0, tiled=True),
    )
    embed_moment_low = lax.all_gather(embed_moment.astype(NARROW), "dp", axis=0, tiled=True)
    head_moment_low = lax.all_gather(head_moment.astype(NARROW), "dp", axis=0, tiled=True)
    tokens_all = everyone[:, :batches]
    count = jnp.maximum(jnp.sum(everyone[:, 2 * batches, 0]).astype(FLOAT), 1.0)
    divisor_all = everyone[:, batches : 2 * batches].astype(FLOAT)
    share_all = jnp.where(divisor_all > 0.5, 1.0 / jnp.maximum(divisor_all, 1.0), 0.0)
    weight_all = (share_all / count).reshape(-1)
    target_all = (
        jnp.concatenate([tokens_all[:, :, 1:], jnp.zeros_like(tokens_all[:, :, :1])], axis=2)
        .reshape(-1)
    ) - vocab_start
    tokens_flat = tokens_all.reshape(-1)
    local_all = tokens_flat - vocab_start
    inside_all = (local_all >= 0) & (local_all < vocab_rows)

    def group_part(values):
        return lax.dynamic_slice_in_dim(values, replica * rows_all, rows_all, 0)

    local_rows = group_part(local_all)
    inside = (local_rows >= 0) & (local_rows < vocab_rows)
    rows = jnp.take(embed_table, jnp.clip(local_rows, 0, vocab_rows - 1), axis=0)
    resid = lax.psum_scatter(
        jnp.where(inside[:, None], rows, 0.0).astype(NARROW),
        "fsdp",
        scatter_dimension=0,
        tiled=True,
    ).astype(FLOAT)
    parts = vector_parts(vector_full.astype(FLOAT), width, hidden)
    places = jnp.arange(seq, dtype=jnp.int32)
    allowed = (buffers[:, :, None] == buffers[:, None, :]) & (
        places[None, None, :] <= places[None, :, None]
    )
    cosine, sine = rotary_tables(offset.reshape(-1), rot)
    layer_out, kept = layer_forward(resid, in_full, out_full, parts, allowed, cosine, sine, factor)
    unit_last, scale_last = norm_unit(layer_out)
    final = (unit_last * parts[4] + parts[5]).astype(NARROW)
    group_hidden = lax.all_gather(final, "fsdp", axis=0, tiled=True)
    all_hidden = lax.all_gather(group_hidden, "dp", axis=0, tiled=True)

    head_low = head_table.astype(NARROW)
    target = group_part(target_all)
    weight = group_part(weight_all)
    exps, tops, totals, hits = head_forward(head_low, group_hidden, target)
    top = jnp.max(tops, axis=0)
    total = jnp.sum(totals * jnp.exp(tops - top), axis=0)
    stats = lax.all_gather(jnp.stack([top, total, hits]), "fsdp")
    top_all = jnp.max(stats[:, 0], axis=0)
    logsum = top_all + jnp.log(jnp.sum(stats[:, 1] * jnp.exp(stats[:, 0] - top_all), axis=0))
    logsum_all = lax.all_gather(logsum, "dp", axis=0, tiled=True)
    own = member * own_rows
    loss_part = jnp.sum(
        lax.dynamic_slice_in_dim(
            weight * (logsum - jnp.sum(stats[:, 2], axis=0)), own, own_rows
        )
    )
    scales = weight * jnp.exp(tops - logsum)
    back = head_back(head_low, exps, scales, weight, target)
    final_grad = lax.psum_scatter(back, "fsdp", scatter_dimension=0, tiled=True)

    less_weight = logsum_all - jnp.log(jnp.maximum(weight_all, 1e-30))
    shifted = jnp.where(weight_all > 0.0, less_weight, 1e30)
    chunk = min(512, rows_all)
    lists = chunk_lists(local_all, inside_all, chunk)

    layer_grad = norm_back(final_grad * parts[4], unit_last, scale_last)
    resid_grad, in_grad, out_grad, small = layer_backward(
        layer_grad, in_full, out_full, parts, kept, allowed, cosine, sine, factor
    )
    vector_grad = jnp.concatenate(
        [
            small[0],
            small[1],
            small[2],
            small[3],
            jnp.sum(final_grad * unit_last, axis=0),
            jnp.sum(final_grad, axis=0),
            small[4],
            small[5],
            small[6],
            small[7],
        ]
    )
    token_grad, in_grad, out_grad, vector_grad, embed_moment_low, head_moment_low, lists = (
        lax.optimization_barrier(
            (
                resid_grad.astype(NARROW),
                in_grad,
                out_grad,
                vector_grad,
                embed_moment_low,
                head_moment_low,
                lists,
            )
        )
    )
    layer_grads = [
        lax.psum(lax.psum_scatter(grad, "fsdp", scatter_dimension=0, tiled=True), "dp")
        for grad in (in_grad, out_grad, vector_grad)
    ]
    head_grad, head_square, token_grads = head_table_grad(
        head_table, all_hidden, shifted, weight_all, target_all, token_grad, groups, replicas
    )
    embed_grad, embed_square = embed_table_grad(token_grads, *lists, vocab_rows)
    square = jnp.sum(embed_square) + jnp.sum(head_square)
    for grad in layer_grads:
        square = square + jnp.sum(grad * grad)
    line = jnp.stack([loss_part, square / replicas])[:, None]
    line = jnp.pad(jnp.broadcast_to(line, (2, 128)), ((0, 6), (0, 0)))
    pair = jnp.sum(exchange_scalars(line, groups, replicas)[:, :2, 0], axis=0)
    loss = pair[0]
    grad_norm = jnp.sqrt(pair[1])
    clip_factor = CLIP_LEVEL / jnp.maximum(grad_norm, CLIP_LEVEL)
    clip = clip_factor.reshape(1)
    base = math.sqrt(NPARAM) / CLIP_LEVEL
    root = math.sqrt(width)
    embed = table_update(
        embed_table, embed_grad, embed_moment_low, embed_moment, embed_average, base, clip
    )
    head = table_update(
        head_table, head_grad, head_moment_low, head_moment, head_average, base / root, clip
    )
    inner = update_rule(
        in_weights, layer_grads[0], in_moment, in_average, base / root, clip_factor
    )
    outer = update_rule(
        out_weights, layer_grads[1], out_moment, out_average, base / root, clip_factor
    )
    vector = update_rule(
        vectors, layer_grads[2], vector_moment, vector_average, 0.3 * base, clip_factor
    )
    return (*embed, *head, *inner, *outer, *vector, loss, grad_norm)


def solution(mesh):
    placed = (
        P(None, ("dp", "fsdp"), None),
        P(None, ("dp", "fsdp"), None),
        P(None, ("dp", "fsdp")),
        P(None, ("dp", "fsdp"), None),
        P("fsdp", None),
        P(("fsdp", "dp"), None),
        P(("fsdp", "dp"), None),
        P("fsdp", None),
        P(("fsdp", "dp"), None),
        P(("fsdp", "dp"), None),
        P("fsdp", None),
        P("fsdp", None),
        P("fsdp", None),
        P("fsdp", None),
        P("fsdp", None),
        P("fsdp", None),
        P("fsdp"),
        P("fsdp"),
        P("fsdp"),
    )
    return jax.shard_map(
        shards,
        mesh=mesh,
        in_specs=placed,
        out_specs=(
            P("fsdp", None),
            P(("fsdp", "dp"), None),
            P(("fsdp", "dp"), None),
            P("fsdp", None),
            P(("fsdp", "dp"), None),
            P(("fsdp", "dp"), None),
            P("fsdp", None),
            P("fsdp", None),
            P("fsdp", None),
            P("fsdp", None),
            P("fsdp", None),
            P("fsdp", None),
            P("fsdp"),
            P("fsdp"),
            P("fsdp"),
            P(),
            P(),
        ),
        check_vma=False,
    )
```

time: 1660 us -> 953 us (0.57)
  blocking collectives: 795 us -> 130 us
  Pallas kernels: 0 us -> 296 us
  matrix products: 196 us -> 27.8 us
  other arithmetic: 153 us -> 66.7 us
  waiting for transfers between devices: 395 us -> 356 us
  local copies, waits for them, and re-layouts: 75.4 us -> 43.6 us
    unnamed x3 -> x2, blocking collectives: 505 us -> 54.7 us
    pallas_call x0 -> x9, Pallas kernels: none -> 296 us  [the longest x1 154 us: head_table_grad(): pl.pallas_call(kernel, grid=(steps,), in_specs=[pl.BlockSpec((block, widt...]
    all_gather x10 -> x3, blocking collectives: 241 us -> 66 us  [the longest x1 43.7 us: shards(): everyone = lax.all_gather(packed, ('dp', 'fsdp'))]
    dot_general x28 -> x7, matrix products: 164 us -> 7.7 us  [the longest x1 2.87 us: layer_backward(): jnp.einsum('bhqk,bkhd->bqhd', score_grad, keys, preferred_element_type=FL...]
    all_gather x6 -> x4, waiting for transfers between devices: 224 us -> 156 us  [the longest x1 87.7 us: shards(): all_hidden = lax.all_gather(group_hidden, 'dp', axis=0, tiled=True)]
    unnamed x325 -> x157, local copies, waits for them, and re-layouts: 54 us -> 9.84 us
    psum x2 -> x1, blocking collectives: 49.6 us -> 9.09 us  [shards(): lax.psum(lax.psum_scatter(grad, 'fsdp', scatter_dimension=0, tiled=True),...]
    scatter-add x2 -> x0, other arithmetic: 26.2 us -> none  [shards(): jax.ops.segment_sum(group_grad.astype(FLOAT), segment_rows, num_segments=...]
  transfers between devices with their start and end apart: 17 -> 11, of which waited for: 7 -> 8; matrix products, arithmetic and copies ran while one was open for 42% -> 7% of each run, Pallas kernels for 0% -> 24%
where the time goes in v1:
time: 953 us; the launch traced here: 944 us
  waiting for transfers between devices  356 us (37%)
  Pallas kernels  296 us (31%)
  blocking collectives  130 us (14%)
  other arithmetic  66.7 us (7%)
  local copies, waits for them, and re-layouts  43.6 us (5%)
  matrix products  27.8 us (3%)
  between operations  22.7 us (2%)
    pallas_call x1, Pallas kernels, head_table_grad(): pl.pallas_call(kernel, grid=(steps,), in_specs=[pl.BlockSpec((block, widt...  154 us
    reduce_scatter x2, waiting for transfers between devices, shards(): lax.psum_scatter(grad, 'fsdp', scatter_dimension=0, tiled=True)  88.6 us
    all_gather x1, waiting for transfers between devices, shards(): all_hidden = lax.all_gather(group_hidden, 'dp', axis=0, tiled=True)  87.7 us
    all_gather x1, waiting for transfers between devices, shards(): lax.all_gather(head_moment.astype(NARROW), 'dp', axis=0, tiled=True)  57.8 us
    unnamed x2, blocking collectives  54.7 us
    reduce_scatter x1, waiting for transfers between devices, shards(): final_grad = lax.psum_scatter(back, 'fsdp', scatter_dimension=0, tiled=True)  47.6 us
    all_gather x1, blocking collectives, shards(): everyone = lax.all_gather(packed, ('dp', 'fsdp'))  43.7 us
    all_gather x1, waiting for transfers between devices, shards(): lax.all_gather(in_weights.astype(NARROW), 'fsdp', axis=0, tiled=True)  40.3 us
  transfers between devices with their start and end apart: 11, of which 8 were waited for; matrix products, arithmetic and copies ran while one was open for 7% of the time, Pallas kernels for 24%

profile of v1, /device:TPU:0, one launch (start us, length us, event | category | flops | bytes accessed | tf_op | source)
XLA Modules:
  0.0 944.0 jit_solution(15570801596642890600)
XLA Ops:
  12.5 43.7 %all-gather.2 = s32[32,5,128]{2,1,0:T(8,128)S(1)} all-gather(s32[1,5,128]{2,1,0:T(8,128)S(1)} %add_bitcast_fusion), channel_id=2, replica_groups=mesh['dp'=4,'fsdp'=8] {'dp','fsdp'}, dimensions={0}, use_global_device_ids=true | all-gather | bytes 84480 | tf_op jit(solution)/shard_map/all_gather | solution.py:831
  56.2 1.2 fusion.90
  58.0 12.2 %gather_fusion = bf16[2048,512]{1,0:T(8,128)(2,1)S(1)} fusion(f32[6288,512]{1,0:T(8,128)} %table_ref.7, s32[2048]{0:T(1024)S(1)} %fusion.91), kind=kCustom, calls=%fused_computation | custom fusion | bytes 4202496 | tf_op jit(solution)/shard_map/jit(_take)/gather | solution.py:857
  70.3 2.7 select_convert_fusion
  73.1 1.1 copy-done.3
  77.4 26.7 %all-reduce.3 = bf16[7680]{0:T(1024)(128)(2,1)S(1)} all-reduce(bf16[7680]{0:T(1024)(128)(2,1)S(1)} %dynamic-update-slice), channel_id=1, replica_groups=mesh['dp'=4,'fsdp'=8] {'fsdp'}, use_global_device_ids=true, to_apply=%add.3 | all-reduce | flops 7680 | bytes 30720
  106.5 1.1 convert_reduce_fusion
  107.6 1.2 fusion.59
  108.8 40.3 %all-gather.13.cloned.1.call-done = bf16[512,3584]{1,0:T(8,128)(2,1)} async-done(((bf16[64,3584]{1,0:T(8,128)(2,1)}), bf16[512,3584]{1,0:T(8,128)(2,1)}) %all-gather.13.cloned.1.call-update) | async-done | bytes 3670032 | tf_op jit(solution)/shard_map/all_gather | solution.py:833
  149.1 2.1 convolution_add_fusion
  154.2 7.6 fusion.4
  161.8 22.3 %all-gather.15.cloned.1.call-done = bf16[2560,512]{1,0:T(8,128)(2,1)} async-done(((bf16[320,512]{1,0:T(8,128)(2,1)}), bf16[2560,512]{1,0:T(8,128)(2,1)}) %all-gather.15.cloned.1.call-update) | async-done | bytes 2621456 | tf_op jit(solution)/shard_map/all_gather | solution.py:834
  184.1 3.0 fusion.120
  187.4 0.9 add_convert_fusion
  188.3 3.3 convert_bitcast_fusion.1
  191.7 3.3 convert_bitcast_fusion
  195.3 8.3 convert_element_type.114.table_ref
  205.6 10.9 %all-gather.17.cloned.1.call-done.hidden_ref = bf16[2048,512]{1,0:T(8,128)(2,1)} async-done(((bf16[256,512]{1,0:T(8,128)(2,1)}), bf16[2048,512]{1,0:T(8,128)(2,1)}) %all-gather.17.cloned.1.call-update) | async-done | bytes 2097168 | tf_op jit(solution)/shard_map/all_gather | solution.py:873
  216.5 30.3 %shard_map.314 = (bf16[6288,2048]{1,0:T(8,128)(2,1)}, f32[4,16,512]{2,1,0:T(8,128)}) custom-call(bf16[6288,512]{1,0:T(8,128)(2,1)} %convert_element_type.114.table_ref, bf16[2048,512]{1,0:T(8,128)(2,1)} %all-gather.17.cloned.1.call-done.hidden_ref, s32[4,1,512]{2,1,0:T(1,128)} %bitcast.174), custom_call_target="tpu_custom_call" | custom-call | flops 13186891776 | bytes 32194560 | tf_op jit(solution)/shard_map/pallas_call | solution.py:243
  248.5 0.9 bitcast_reduce_fusion
  249.4 1.0 fusion.83
  250.4 14.2 %all-gather.3 = f32[8,3,2048]{2,1,0:T(4,128)S(1)} all-gather(f32[1,3,2048]{2,1,0:T(4,128)S(1)} %maximum_bitcast_fusion.2), channel_id=3, replica_groups=mesh['dp'=4,'fsdp'=8] {'fsdp'}, dimensions={0}, use_global_device_ids=true | all-gather | bytes 221184 | tf_op jit(solution)/shard_map/all_gather | solution.py:882
  266.1 23.8 %shard_map.315 = f32[2048,512]{1,0:T(8,128)} custom-call(bf16[6288,512]{1,0:T(8,128)(2,1)} %convert_element_type.114.table_ref, bf16[6288,2048]{1,0:T(8,128)(2,1)} %get-tuple-element.38.exps_ref, f32[8,6,256]{2,1,0:T(8,128)} %multiply_bitcast_fusion.scale_ref, f32[8,1,256]{2,1,0:T(1,128)} %bitcast.173, s32[8,1,256]{2,1,0:T(1,128)} %bitcast.175), custom_call_target="tpu_custom_call" | custom-call | flops 13186891776 | bytes 32194560 | tf_op jit(solution)/shard_map/pallas_call | solution.py:295
  291.7 8.0 select_reduce_fusion
  299.7 6.2 reshape.367.moment_ref
  305.8 57.8 %all-gather.23.cloned.1.call-done = bf16[4,1572,512]{2,1,0:T(8,128)(2,1)} async-done(((bf16[1,1572,512]{2,1,0:T(8,128)(2,1)}), bf16[4,1572,512]{2,1,0:T(8,128)(2,1)}) %all-gather.23.cloned.1.call-update) | async-done | bytes 6438928 | tf_op jit(solution)/shard_map/all_gather | solution.py:838
  363.7 5.3 reshape.369.moment_ref
  369.0 47.6 %reduce-scatter.7.cloned.1.call-done = f32[256,512]{1,0:T(8,128)} async-done(((f32[2048,512]{1,0:T(8,128)}), f32[256,512]{1,0:T(8,128)}) %reduce-scatter.7.cloned.1.call-update) | async-done | bytes 524304 | tf_op jit(solution)/shard_map/reduce_scatter | solution.py:894
  416.6 2.1 multiply_reduce_fusion.3
  418.7 1.8 fusion.114
  420.5 0.9 fusion.77
  421.4 1.5 copy-done
  424.0 1.3 fusion.69
  425.3 2.2 convolution_bitcast_fusion.1
  427.6 2.9 convolution_bitcast_fusion.2
  430.5 1.0 copy-done.18
  432.3 3.2 fusion.38
  436.9 1.1 copy-done.10
  438.8 1.0 fusion.112
  439.8 1.0 copy-done.68
  441.6 1.0 fusion.109
  442.8 0.9 fusion.60
  444.5 3.5 pad_maximum_fusion
  448.0 0.9 fusion.56.own_ref
  451.0 1.4 fusion.96
  452.4 8.1 all_gather.47
  462.4 28.0 %all-reduce.4 = f32[7680]{0:T(1024)S(1)} all-reduce(f32[7680]{0:T(1024)S(1)} %constant_dynamic-update-slice_fusion.1), channel_id=8, replica_groups=mesh['dp'=4,'fsdp'=8] {'fsdp'}, use_global_device_ids=true, to_apply=%region_47.48.clone | all-reduce | flops 7680 | bytes 61440
  490.4 9.1 psum.23
  500.1 7.6 reduce-scatter.11.cloned.1.call-done
  507.7 81.0 %reduce-scatter.9.cloned.1.call-done = f32[64,3584]{1,0:T(8,128)} async-done(((f32[512,3584]{1,0:T(8,128)}), f32[64,3584]{1,0:T(8,128)}) %reduce-scatter.9.cloned.1.call-update) | async-done | bytes 917520 | tf_op jit(solution)/shard_map/reduce_scatter | solution.py:933
  588.8 87.7 %all-gather.19.cloned.1.call-done.hidden_ref = bf16[8192,512]{1,0:T(8,128)(2,1)} async-done(((bf16[2048,512]{1,0:T(8,128)(2,1)}), bf16[8192,512]{1,0:T(8,128)(2,1)}) %all-gather.19.cloned.1.call-update) | async-done | bytes 8388624 | tf_op jit(solution)/shard_map/all_gather | solution.py:874
  676.4 153.8 %shard_map.316 = (f32[6288,512]{1,0:T(8,128)}, f32[1,512]{1,0:T(1,128)}, bf16[32,256,512]{2,1,0:T(8,128)(2,1)}) custom-call(f32[6288,512]{1,0:T(8,128)} %table_ref.9, bf16[8192,512]{1,0:T(8,128)(2,1)} %all-gather.19.cloned.1.call-done.hidden_ref, f32[4,1,2048]{2,1,0:T(1,128)} %bitcast.168, f32[4,1,2048]{2,1,0:T(1,128)} %bitcast.156, ...), custom_call_target="tpu_custom_call" | custom-call | flops 105495134208 | bytes 42532864 | tf_op jit(solution)/shard_map/pallas_call | solution.py:525
  830.2 22.4 %shard_map.317 = (f32[6288,512]{1,0:T(8,128)}, f32[1,512]{1,0:T(1,128)}) custom-call(s32[16]{0:T(128)} %reduce_sum.385.count_ref, s32[16,1,512]{2,1,0:T(1,128)} %reshape.343.place_ref, s32[16,1,512]{2,1,0:T(1,128)} %reshape.344.row_ref, bf16[8192,512]{1,0:T(8,128)(2,1)} %bitcast.143), custom_call_target="tpu_custom_call" | custom-call | tf_op jit(solution)/shard_map/pallas_call | solution.py:673
  852.6 1.3 reduce_sum.386
  855.8 2.0 multiply_reduce_fusion.1
  857.9 1.9 multiply_reduce_fusion.2
  863.1 10.5 %shard_map.318 = f32[32,8,128]{2,1,0:T(8,128)} custom-call(f32[8,128]{1,0:T(8,128)} %pad.9.own_ref), custom_call_target="tpu_custom_call" | custom-call | tf_op jit(solution)/shard_map/pallas_call | solution.py:613
  873.6 1.1 slice_reduce_fusion.1
  875.9 15.5 %shard_map.319 = f32[6288,512]{1,0:T(8,128)} custom-call(f32[1]{0:T(128)} %bitcast.40.clip_ref, f32[6288,512]{1,0:T(8,128)} %table_ref.7, f32[6288,512]{1,0:T(8,128)} %get-tuple-element.49.grad_ref, bf16[6288,512]{1,0:T(8,128)(2,1)} %reshape.367.moment_ref), custom_call_target="tpu_custom_call" | custom-call | tf_op jit(solution)/shard_map/pallas_call | solution.py:727
  891.4 11.8 %shard_map.320 = (f32[1572,512]{1,0:T(8,128)}, f32[1572,512]{1,0:T(8,128)}) custom-call(f32[1]{0:T(128)} %bitcast.40.clip_ref, f32[6288,512]{1,0:T(8,128)} %table_ref.7, f32[6288,512]{1,0:T(8,128)} %get-tuple-element.49.grad_ref, f32[1572,512]{1,0:T(8,128)} %moment_ref.2, f32[1572,512]{1,0:T(8,128)} %average_ref.2), custom_call_target="tpu_custom_call" | custom-call | tf_op jit(solution)/shard_map/pallas_call | solution.py:774
  903.3 15.7 %shard_map.321 = f32[6288,512]{1,0:T(8,128)} custom-call(f32[1]{0:T(128)} %bitcast.40.clip_ref, f32[6288,512]{1,0:T(8,128)} %table_ref.9, f32[6288,512]{1,0:T(8,128)} %get-tuple-element.53.grad_ref, bf16[6288,512]{1,0:T(8,128)(2,1)} %reshape.369.moment_ref), custom_call_target="tpu_custom_call" | custom-call | tf_op jit(solution)/shard_map/pallas_call | solution.py:727
  919.0 12.0 %shard_map.322 = (f32[1572,512]{1,0:T(8,128)}, f32[1572,512]{1,0:T(8,128)}) custom-call(f32[1]{0:T(128)} %bitcast.40.clip_ref, f32[6288,512]{1,0:T(8,128)} %table_ref.9, f32[6288,512]{1,0:T(8,128)} %get-tuple-element.53.grad_ref, f32[1572,512]{1,0:T(8,128)} %moment_ref.3, f32[1572,512]{1,0:T(8,128)} %average_ref.3), custom_call_target="tpu_custom_call" | custom-call | tf_op jit(solution)/shard_map/pallas_call | solution.py:774
  931.1 1.8 add_multiply_fusion
  933.7 1.5 add_multiply_fusion.1
  (273 shorter events, 34.3 us)
Async XLA Ops:
  7.2 99.3 %reduce-scatter.5.cloned.1.call-start = ((), (), s32[]{:S(2)}) async-start(), calls=%async_computation.4 | async-start | bytes 2359296 | tf_op jit(solution)/shard_map/reduce_scatter | solution.py:858
  73.0 2.1 copy-start.8
  73.0 2.9 copy-start.51
  73.0 2.9 copy-start.66
  73.0 32.4 %copy-start.33 = (s32[2,1,128]{2,1,0:T(1,128)S(1)}, s32[2,1,128]{2,1,0:T(1,128)}, u32[]{:S(2)}) copy-start(s32[2,1,128]{2,1,0:T(1,128)} %param.22) | copy-start | bytes 3076
  73.0 76.0 %all-gather.13.cloned.1.call-start = ((), (), s32[]{:S(2)}) async-start(), calls=%async_computation.5 | async-start | bytes 4128768 | tf_op jit(solution)/shard_map/all_gather | solution.py:833
  75.0 109.1 %all-gather.15.cloned.1.call-start = ((), (), s32[]{:S(2)}) async-start(), calls=%async_computation.6 | async-start | bytes 2949120 | tf_op jit(solution)/shard_map/all_gather | solution.py:834
  75.8 140.7 %all-gather.17.cloned.1.call-start = ((), (), s32[]{:S(2)}) async-start(), calls=%async_computation.7 | async-start | bytes 2359296 | tf_op jit(solution)/shard_map/all_gather | solution.py:873
  104.7 44.3 %copy-start.53 = (f32[512]{0:T(512)}, f32[512]{0:T(512)S(1)}, u32[]{:S(2)}) copy-start(f32[512]{0:T(512)S(1)} %get-tuple-element.116) | copy-start | bytes 6148
  104.7 44.3 %copy-start.55 = (f32[512]{0:T(512)}, f32[512]{0:T(512)S(1)}, u32[]{:S(2)}) copy-start(f32[512]{0:T(512)S(1)} %get-tuple-element.117) | copy-start | bytes 6148
  106.5 45.5 %copy-start.29 = (f32[256,8]{0,1:T(8,128)}, f32[256,8]{0,1:T(8,128)S(1)}, u32[]{:S(2)}) copy-start(f32[256,8]{0,1:T(8,128)S(1)} %get-tuple-element.122) | copy-start | bytes 24580
  106.5 45.5 %copy-start.31 = (f32[256,8]{0,1:T(8,128)}, f32[256,8]{0,1:T(8,128)S(1)}, u32[]{:S(2)}) copy-start(f32[256,8]{0,1:T(8,128)S(1)} %get-tuple-element.123) | copy-start | bytes 24580
  107.6 41.5 %copy-start.39 = (f32[256]{0:T(256)}, f32[256]{0:T(256)S(1)}, u32[]{:S(2)}) copy-start(f32[256]{0:T(256)S(1)} %broadcast_multiply_fusion.5) | copy-start | bytes 3076
  108.8 40.3 %copy-start.47 = (f32[256]{0:T(256)}, f32[256]{0:T(256)S(1)}, u32[]{:S(2)}) copy-start(f32[256]{0:T(256)S(1)} %add_rsqrt_fusion.1) | copy-start | bytes 3076
  153.0 1.2 copy-start.2
  153.0 1.2 copy-start.34
  153.0 1.2 copy-start.36
  154.1 29.9 %copy-start.12 = (bf16[256,512]{1,0:T(8,128)(2,1)}, bf16[256,512]{1,0:T(8,128)(2,1)S(1)}, u32[]{:S(2)}) copy-start(bf16[256,512]{1,0:T(8,128)(2,1)S(1)} %reshape.374) | copy-start | bytes 786436
  154.2 29.9 %copy-start.64 = (f32[512]{0:T(512)S(1)}, f32[512]{0:T(512)}, u32[]{:S(2)}) copy-start(f32[512]{0:T(512)} %get-tuple-element.114) | copy-start | bytes 6148
  154.2 29.9 %copy-start.65 = (f32[512]{0:T(512)S(1)}, f32[512]{0:T(512)}, u32[]{:S(2)}) copy-start(f32[512]{0:T(512)} %get-tuple-element.115) | copy-start | bytes 6148
  184.1 3.3 copy-start.44
  184.1 3.3 copy-start.57
  188.3 111.4 %all-gather.21.cloned.1.call-start = ((), (), s32[]{:S(2)}) async-start(), calls=%async_computation.12 | async-start | bytes 8069120 | tf_op jit(solution)/shard_map/all_gather | solution.py:837
  191.6 172.0 %all-gather.23.cloned.1.call-start = ((), (), s32[]{:S(2)}) async-start(), calls=%async_computation.13 | async-start | bytes 8069120 | tf_op jit(solution)/shard_map/all_gather | solution.py:838
  195.0 221.6 %reduce-scatter.7.cloned.1.call-start = ((), (), s32[]{:S(2)}) async-start(), calls=%async_computation.8 | async-start | bytes 4718592 | tf_op jit(solution)/shard_map/reduce_scatter | solution.py:894
  203.6 43.2 %copy-start.38 = (s32[32,2,128]{2,1,0:T(2,128)}, s32[32,2,128]{2,1,0:T(2,128)S(1)}, u32[]{:S(2)}) copy-start(s32[32,2,128]{2,1,0:T(2,128)S(1)} %pad_subtract_fusion) | copy-start | bytes 98308
  205.6 41.2 %copy-start.24 = (f32[32,2,128]{2,1,0:T(2,128)}, f32[32,2,128]{2,1,0:T(2,128)S(1)}, u32[]{:S(2)}) copy-start(f32[32,2,128]{2,1,0:T(2,128)S(1)} %fusion.89) | copy-start | bytes 98308
  205.6 41.2 %copy-start.46 = (f32[2048]{0:T(1024)}, f32[2048]{0:T(1024)S(1)}, u32[]{:S(2)}) copy-start(f32[2048]{0:T(1024)S(1)} %dynamic_slice.12) | copy-start | bytes 24580
  290.0 217.8 %reduce-scatter.11.cloned.1.call-start = ((), (), s32[]{:S(2)}) async-start(), calls=%async_computation.11 | async-start | bytes 5898240 | tf_op jit(solution)/shard_map/reduce_scatter | solution.py:933
  416.6 3.9 copy-start.7
  421.4 1.5 copy-start
  427.5 4.0 copy-start.30
  427.5 4.0 copy-start.32
  430.4 1.8 copy-start.11
  430.4 1.8 copy-start.13
  436.4 1.6 copy-start.10
  436.5 2.3 copy-start.1
  438.8 2.0 copy-start.68
  439.8 1.7 copy-start.35
  439.8 1.7 copy-start.41
  439.8 1.7 copy-start.49
  439.8 1.7 copy-start.54
  441.5 1.2 copy-start.50
  441.5 1.2 copy-start.37
  448.9 139.8 %reduce-scatter.9.cloned.1.call-start = ((), (), s32[]{:S(2)}) async-start(), calls=%async_computation.10 | async-start | bytes 8257536 | tf_op jit(solution)/shard_map/reduce_scatter | solution.py:933
  449.7 1.3 copy-start.25
  449.7 11.4 %copy-start.27 = (s32[16,512]{1,0:T(8,128)S(1)}, s32[16,512]{1,0:T(8,128)}, u32[]{:S(2)}) copy-start(s32[16,512]{1,0:T(8,128)} %get-tuple-element.40) | copy-start | bytes 98308
  449.7 12.1 %copy-start.26 = (s32[16,512]{1,0:T(8,128)S(1)}, s32[16,512]{1,0:T(8,128)}, u32[]{:S(2)}) copy-start(s32[16,512]{1,0:T(8,128)} %get-tuple-element.41) | copy-start | bytes 98308
  449.7 226.7 %all-gather.19.cloned.1.call-start = ((), (), s32[]{:S(2)}) async-start(), calls=%async_computation.9 | async-start | bytes 10485760 | tf_op jit(solution)/shard_map/all_gather | solution.py:874
  450.3 405.5 %all-reduce.8.cloned.1.call-start = ((), (), s32[]{:S(2)}) async-start(), calls=%async_computation.14 | async-start | bytes 3145728 | tf_op jit(solution)/shard_map/psum | solution.py:933
  499.5 330.7 %copy-start.42 = (f32[960]{0:T(1024)}, f32[960]{0:T(1024)S(1)}, u32[]{:S(2)}) copy-start(f32[960]{0:T(1024)S(1)} %psum.23) | copy-start | bytes 11524
  830.2 23.7 %copy-start.67 = (f32[1,512]{1,0:T(1,128)S(1)}, f32[1,512]{1,0:T(1,128)}, u32[]{:S(2)}) copy-start(f32[1,512]{1,0:T(1,128)} %get-tuple-element.45) | copy-start | bytes 6148
  919.0 12.0 %copy-start.4 = (f32[64,3584]{1,0:T(8,128)S(1)}, f32[64,3584]{1,0:T(8,128)}, u32[]{:S(2)}) copy-start(f32[64,3584]{1,0:T(8,128)} %param.29) | copy-start | bytes 2752516
  919.0 12.0 %copy-start.5 = (f32[64,3584]{1,0:T(8,128)S(1)}, f32[64,3584]{1,0:T(8,128)}, u32[]{:S(2)}) copy-start(f32[64,3584]{1,0:T(8,128)} %get-tuple-element.71) | copy-start | bytes 2752516
  919.0 12.0 %copy-start.14 = (f32[64,3584]{1,0:T(8,128)S(1)}, f32[64,3584]{1,0:T(8,128)}, u32[]{:S(2)}) copy-start(f32[64,3584]{1,0:T(8,128)} %param.31) | copy-start | bytes 2752516
  919.0 12.0 %copy-start.15 = (f32[64,3584]{1,0:T(8,128)S(1)}, f32[64,3584]{1,0:T(8,128)}, u32[]{:S(2)}) copy-start(f32[64,3584]{1,0:T(8,128)} %param.30) | copy-start | bytes 2752516
  931.0 1.8 copy-start.6
  931.0 1.8 copy-start.9
  931.1 2.2 copy-start.16
  931.1 2.6 copy-start.17
  933.7 1.5 copy-start.43
  933.7 1.5 copy-start.52
  933.7 1.5 copy-start.61
  933.7 1.5 copy-start.62
  (16 other events, 15.9 us)
Sparse Core Ops, SparseCore 0:
  73.1 32.2 reduce-scatter.4
  107.6 41.3 all-gather.12
  151.3 32.7 all-gather.14
  188.4 28.0 all-gather.16
  218.8 71.0 all-gather.20
  292.1 71.5 all-gather.22
  366.5 50.0 reduce-scatter.6
  449.0 58.6 reduce-scatter.10
  510.6 78.0 reduce-scatter.8
  590.4 85.9 all-gather.18
  679.6 86.7 all-reduce.7

commit v2 on v1

--- a/solution.py
+++ b/solution.py
@@ -211,114 +211,6 @@
     return best
 
 
-def head_forward(table, hidden, target):
-    vocab, width = table.shape
-    rows = hidden.shape[0]
-    tile = 512
-    block = block_rows(vocab, 1100)
-    blocks = vocab // block
-    lines = -(-(2 * blocks + 1) // 8) * 8
-
-    def kernel(table_ref, hidden_ref, target_ref, exps_ref, stats_ref):
-        here = hidden_ref[...]
-        places = lax.broadcasted_iota(jnp.int32, (block, tile), 0)
-        hit = jnp.zeros((1, tile), FLOAT)
-        for b in range(blocks):
-            part = slice(b * block, (b + 1) * block)
-            logits = lax.dot_general(
-                table_ref[part, :], here, LAST_CONTRACT, preferred_element_type=FLOAT
-            )
-            top = jnp.max(logits, axis=0, keepdims=True)
-            exps = jnp.exp(logits - top)
-            stats_ref[0, b : b + 1, :] = top
-            stats_ref[0, blocks + b : blocks + b + 1, :] = jnp.sum(exps, axis=0, keepdims=True)
-            hit = hit + jnp.sum(
-                jnp.where(places == target_ref[0] - b * block, logits, 0.0), axis=0, keepdims=True
-            )
-            exps_ref[part, :] = exps.astype(NARROW)
-        stats_ref[0, 2 * blocks : 2 * blocks + 1, :] = hit
-
-    whole = pl.BlockSpec(memory_space=pltpu.VMEM)
-    tiles = rows // tile
-    exps, stats = pl.pallas_call(
-        kernel,
-        grid=(tiles,),
-        in_specs=[
-            whole,
-            pl.BlockSpec((tile, width), lambda i: (i, 0)),
-            pl.BlockSpec((1, 1, tile), lambda i: (i, 0, 0)),
-        ],
-        out_specs=[
-            pl.BlockSpec((vocab, tile), lambda i: (0, i)),
-            pl.BlockSpec((1, lines, tile), lambda i: (i, 0, 0)),
-        ],
-        out_shape=[
-            jax.ShapeDtypeStruct((vocab, rows), NARROW),
-            jax.ShapeDtypeStruct((tiles, lines, tile), FLOAT),
-        ],
-        compiler_params=pltpu.CompilerParams(vmem_limit_bytes=VMEM_LIMIT),
-        cost_estimate=pl.CostEstimate(
-            flops=2 * vocab * rows * width,
-            bytes_accessed=vocab * (rows + width) * 2,
-            transcendentals=vocab * rows,
-        ),
-    )(table, hidden, target.reshape(tiles, 1, tile))
-    tops = stats[:, :blocks].transpose(1, 0, 2).reshape(blocks, rows)
-    totals = stats[:, blocks : 2 * blocks].transpose(1, 0, 2).reshape(blocks, rows)
-    hits = stats[:, 2 * blocks].reshape(rows)
-    return exps, tops, totals, hits
-
-
-def head_back(table, exps, scales, weights, target):
-    vocab, width = table.shape
-    rows = exps.shape[1]
-    tile = 256
-    blocks = scales.shape[0]
-    block = vocab // blocks
-
-    def kernel(table_ref, exps_ref, scale_ref, weight_ref, target_ref, back_ref):
-        places = lax.broadcasted_iota(jnp.int32, (block, tile), 0)
-        total = jnp.zeros((tile, width), FLOAT)
-        for b in range(blocks):
-            part = slice(b * block, (b + 1) * block)
-            grads = exps_ref[part, :].astype(FLOAT) * scale_ref[0, b : b + 1, :]
-            grads = jnp.where(
-                places == target_ref[0] - b * block, grads - weight_ref[0], grads
-            ).astype(NARROW)
-            total = total + lax.dot_general(
-                grads, table_ref[part, :], ROWS_CONTRACT, preferred_element_type=FLOAT
-            )
-        back_ref[...] = total
-
-    tiles = rows // tile
-    line = pl.BlockSpec((1, 1, tile), lambda i: (i, 0, 0))
-    return pl.pallas_call(
-        kernel,
-        grid=(tiles,),
-        in_specs=[
-            pl.BlockSpec(memory_space=pltpu.VMEM),
-            pl.BlockSpec((vocab, tile), lambda i: (0, i)),
-            pl.BlockSpec((1, blocks, tile), lambda i: (i, 0, 0)),
-            line,
-            line,
-        ],
-        out_specs=pl.BlockSpec((tile, width), lambda i: (i, 0)),
-        out_shape=jax.ShapeDtypeStruct((rows, width), FLOAT),
-        compiler_params=pltpu.CompilerParams(vmem_limit_bytes=VMEM_LIMIT),
-        cost_estimate=pl.CostEstimate(
-            flops=2 * vocab * rows * width,
-            bytes_accessed=vocab * (rows + width) * 2,
-            transcendentals=0,
-        ),
-    )(
-        table,
-        exps,
-        scales.reshape(blocks, tiles, tile).transpose(1, 0, 2),
-        weights.reshape(tiles, 1, tile),
-        target.reshape(tiles, 1, tile),
-    )
-
-
 MESH = pl.DeviceIdType.MESH
 
 
@@ -376,8 +268,739 @@
     )
 
 
-def head_table_grad(table, hidden, logsum, weights, target, token_grad, groups, replicas):
+def start_kernel(packed, line, in_shard, out_shard, table, batches, groups, replicas):
     vocab, width = table.shape
+    seq = packed.shape[1]
+    own = batches * seq
+    chips = groups // 2
+    amount = groups * replicas
+    shards_in = (in_shard, out_shard)
+    split = all(shard.shape[0] % (16 * replicas) == 0 for shard in shards_in)
+    pieces = replicas if split else 1
+    unroll = 8
+
+    def kernel(
+        packed_ref,
+        line_ref,
+        in_ref,
+        out_ref,
+        table_ref,
+        every_ref,
+        lines_ref,
+        in_full,
+        out_full,
+        resid_ref,
+        in_low,
+        out_low,
+        wide,
+        looked,
+        to_core,
+        from_core,
+        to_lane,
+        from_lane,
+        ids,
+        table_sem,
+        ids_sem,
+        local_sem,
+        meta_send,
+        meta_recv,
+        line_send,
+        line_recv,
+        lane_send,
+        lane_recv,
+        plane_send,
+        plane_recv,
+        core_send,
+        core_recv,
+        part_send,
+        part_recv,
+        sum_send,
+        sum_recv,
+    ):
+        place = Place(groups, replicas)
+        member = place.member
+        core = place.core
+        replica = place.replica
+        me = replica * groups + member
+        fulls = (in_full, out_full)
+        lows = (in_low, out_low)
+
+        def device(index):
+            return place.at(index // groups, lax.rem(index, groups))
+
+        def chip_at(j):
+            return lax.rem(place.chip + j, chips)
+
+        def chip_before(j):
+            return lax.rem(place.chip + chips - j, chips)
+
+        def replica_before(k):
+            return lax.rem(replica + replicas - k, replicas)
+
+        def lane_device(j):
+            return place.at(replica, chip_at(j) * 2 + core)
+
+        def plane_device(k):
+            return place.at(lax.rem(replica + k, replicas), member)
+
+        def meta_copy(k):
+            return remote(
+                packed_ref,
+                every_ref.at[me],
+                meta_send.at[k],
+                meta_recv.at[k],
+                device(lax.rem(me + k, amount)),
+            )
+
+        def line_copy(k):
+            return remote(
+                line_ref,
+                lines_ref.at[member],
+                line_send.at[k],
+                line_recv.at[k],
+                place.at(replica, lax.rem(member + k, groups)),
+            )
+
+        def piece(w, slot, from_replica):
+            full = fulls[w]
+            if not split:
+                return full.at[slot]
+            rows = full.shape[1] // pieces
+            return full.at[slot, pl.ds(pl.multiple_of(from_replica * rows, 16), rows), :]
+
+        def own_piece(w):
+            low = lows[w]
+            if not split:
+                return low
+            rows = low.shape[0] // pieces
+            return low.at[pl.ds(pl.multiple_of(replica * rows, 16), rows), :]
+
+        def lane_copy(w, j):
+            return remote(
+                own_piece(w),
+                piece(w, member, replica),
+                lane_send.at[w, j],
+                lane_recv.at[w, j],
+                lane_device(j),
+            )
+
+        def lane_wait(w, j):
+            there = piece(w, chip_before(j) * 2 + core, replica)
+            remote(
+                there, there, lane_send.at[w, j], lane_recv.at[w, j], lane_device(j)
+            ).wait_recv()
+
+        def plane_copy(w, k, j):
+            there = piece(w, chip_before(j) * 2 + core, replica)
+            return remote(
+                there, there, plane_send.at[w, k, j], plane_recv.at[w, k, j], plane_device(k)
+            )
+
+        def plane_wait(w, k, j):
+            there = piece(w, chip_before(j) * 2 + core, replica_before(k))
+            remote(
+                there, there, plane_send.at[w, k, j], plane_recv.at[w, k, j], plane_device(k)
+            ).wait_recv()
+
+        def core_copy(w, j):
+            here = fulls[w].at[chip_before(j) * 2 + core]
+            return remote(here, here, core_send.at[w, j], core_recv.at[w, j], place.sibling())
+
+        def own_core_copy(w):
+            return remote(
+                lows[w],
+                fulls[w].at[member],
+                core_send.at[w, 0],
+                core_recv.at[w, 0],
+                place.sibling(),
+            )
+
+        def core_wait(w, j):
+            there = fulls[w].at[chip_before(j) * 2 + 1 - core]
+            remote(
+                there, there, core_send.at[w, j], core_recv.at[w, j], place.sibling()
+            ).wait_recv()
+
+        def part_copy(j):
+            return remote(
+                to_core.at[j], from_core.at[j], part_send.at[j], part_recv.at[j], place.sibling()
+            )
+
+        def sum_copy(j):
+            return remote(
+                to_lane.at[j], from_lane.at[j], sum_send.at[j], sum_recv.at[j], lane_device(j)
+            )
+
+        fetch = pltpu.make_async_copy(table_ref, wide, table_sem)
+        fetch.start()
+        barrier = pltpu.get_barrier_semaphore()
+
+        def greet(k, carry):
+            pl.semaphore_signal(
+                barrier, inc=1, device_id=device(lax.rem(me + k, amount)), device_id_type=MESH
+            )
+            return carry
+
+        lax.fori_loop(1, amount, greet, 0)
+        in_low[...] = in_ref[...].astype(NARROW)
+        out_low[...] = out_ref[...].astype(NARROW)
+        every_ref[me] = packed_ref[...]
+        lines_ref[member] = line_ref[...]
+        pl.semaphore_wait(barrier, amount - 1)
+
+        def tell(k, carry):
+            meta_copy(k).start()
+            return carry
+
+        lax.fori_loop(1, amount, tell, 0)
+        for k in range(1, groups):
+            line_copy(k).start()
+        for w in range(2):
+            for j in range(1, chips):
+                lane_copy(w, j).start()
+            own_core_copy(w).start()
+        kept = [
+            pltpu.make_async_copy(lows[w], fulls[w].at[member], local_sem.at[w])
+            for w in range(2)
+        ]
+        for copy in kept:
+            copy.start()
+
+        def hear(k, carry):
+            there = every_ref.at[lax.rem(me + amount - k, amount)]
+            remote(there, there, meta_send.at[k], meta_recv.at[k], device(me)).wait_recv()
+            return carry
+
+        lax.fori_loop(1, amount, hear, 0)
+        load = pltpu.make_async_copy(
+            every_ref.at[pl.ds(replica * groups, groups)], ids, ids_sem
+        )
+        load.start()
+        load.wait()
+        fetch.wait()
+        start = member * vocab
+
+        def look(slot):
+            for b in range(batches):
+
+                def lap(i, carry):
+                    for u in range(unroll):
+                        spot = i * unroll + u
+                        row = ids[slot, b, spot] - start
+                        inside = (row >= 0) & (row < vocab)
+                        safe = jnp.where(inside, row, 0)
+                        keep = jnp.where(inside, 1.0, 0.0)
+                        looked[pl.ds(b * seq + spot, 1), :] = wide[pl.ds(safe, 1), :] * keep
+                    return carry
+
+                lax.fori_loop(0, seq // unroll, lap, 0)
+            return looked[...].astype(NARROW)
+
+        def lap(step, carry):
+            j = lax.rem(step + 1, chips)
+            there = chip_at(j) * 2
+            to_core[j] = look(there + 1 - core)
+            part_copy(j).start()
+            mine = look(there + core).astype(FLOAT)
+            part_copy(j).wait_recv()
+            mine = mine + from_core[j].astype(FLOAT)
+
+            @pl.when(j > 0)
+            def _():
+                to_lane[j] = mine.astype(NARROW)
+                sum_copy(j).start()
+
+            @pl.when(j == 0)
+            def _():
+                resid_ref[...] = mine
+
+            return carry
+
+        lax.fori_loop(0, chips, lap, 0)
+        for w in range(2):
+            for j in range(1, chips):
+                lane_wait(w, j)
+                if split:
+                    for k in range(1, replicas):
+                        plane_copy(w, k, j).start()
+        for j in range(1, chips):
+            sum_copy(j).wait_recv()
+            resid_ref[...] += from_lane[j].astype(FLOAT)
+        for w in range(2):
+            for j in range(1, chips):
+                if split:
+                    for k in range(1, replicas):
+                        plane_wait(w, k, j)
+                core_copy(w, j).start()
+        for w in range(2):
+            kept[w].wait()
+            for j in range(chips):
+                core_wait(w, j)
+                if j == 0:
+                    own_core_copy(w).wait_send()
+                else:
+                    core_copy(w, j).wait_send()
+                    lane_copy(w, j).wait_send()
+                if split and j > 0:
+                    for k in range(1, replicas):
+                        plane_copy(w, k, j).wait_send()
+        for k in range(1, groups):
+            there = lines_ref.at[lax.rem(member + groups - k, groups)]
+            remote(
+                there, there, line_send.at[k], line_recv.at[k], place.at(replica, member)
+            ).wait_recv()
+            line_copy(k).wait_send()
+        for j in range(chips):
+            part_copy(j).wait_send()
+            if j > 0:
+                sum_copy(j).wait_send()
+
+        def told(k, carry):
+            meta_copy(k).wait_send()
+            return carry
+
+        lax.fori_loop(1, amount, told, 0)
+
+    whole = pl.BlockSpec(memory_space=pltpu.VMEM)
+    anywhere = pl.BlockSpec(memory_space=pl.ANY)
+    dma = pltpu.SemaphoreType.DMA
+    vmem = pltpu.VMEM
+    every, lines, in_full, out_full, resid = pl.pallas_call(
+        kernel,
+        in_specs=[whole, whole, whole, whole, anywhere],
+        out_specs=[whole, whole, anywhere, anywhere, whole],
+        out_shape=[
+            jax.ShapeDtypeStruct((amount,) + packed.shape, jnp.int32),
+            jax.ShapeDtypeStruct((groups,) + line.shape, FLOAT),
+            jax.ShapeDtypeStruct((groups,) + in_shard.shape, NARROW),
+            jax.ShapeDtypeStruct((groups,) + out_shard.shape, NARROW),
+            jax.ShapeDtypeStruct((own, width), FLOAT),
+        ],
+        scratch_shapes=[
+            vmem(in_shard.shape, NARROW),
+            vmem(out_shard.shape, NARROW),
+            vmem((vocab, width), FLOAT),
+            vmem((own, width), FLOAT),
+            vmem((chips, own, width), NARROW),
+            vmem((chips, own, width), NARROW),
+            vmem((chips, own, width), NARROW),
+            vmem((chips, own, width), NARROW),
+            pltpu.SMEM((groups,) + packed.shape, jnp.int32),
+            dma,
+            dma,
+            dma((2,)),
+            dma((amount,)),
+            dma((amount,)),
+            dma((groups,)),
+            dma((groups,)),
+            dma((2, chips)),
+            dma((2, chips)),
+            dma((2, replicas, chips)),
+            dma((2, replicas, chips)),
+            dma((2, chips)),
+            dma((2, chips)),
+            dma((chips,)),
+            dma((chips,)),
+            dma((chips,)),
+            dma((chips,)),
+        ],
+        compiler_params=pltpu.CompilerParams(
+            vmem_limit_bytes=VMEM_LIMIT, collective_id=4, has_side_effects=True
+        ),
+        cost_estimate=pl.CostEstimate(
+            flops=0, bytes_accessed=vocab * width * 4, transcendentals=0
+        ),
+    )(packed, line, in_shard, out_shard, table)
+    return (
+        every,
+        lines,
+        in_full.reshape(-1, in_shard.shape[1]),
+        out_full.reshape(-1, out_shard.shape[1]),
+        resid,
+    )
+
+
+def head_kernel(table, own_hidden, target, weight, groups, replicas):
+    vocab, width = table.shape
+    own = own_hidden.shape[0]
+    block = block_rows(vocab, 1100)
+    blocks = vocab // block
+    chips = groups // 2
+    lines = -(-blocks // 8) * 8
+
+    def kernel(
+        table_ref,
+        own_ref,
+        target_ref,
+        weight_ref,
+        grad_ref,
+        logsum_ref,
+        loss_ref,
+        all_ref,
+        wide,
+        low,
+        hid,
+        exps,
+        tops,
+        totals,
+        hits,
+        shares,
+        to_core,
+        from_core,
+        to_lane,
+        from_lane,
+        table_sem,
+        local_sem,
+        lane_send,
+        lane_recv,
+        core_send,
+        core_recv,
+        plane_send,
+        plane_recv,
+        pass_send,
+        pass_recv,
+        stat_send,
+        stat_recv,
+        line_send,
+        line_recv,
+        part_send,
+        part_recv,
+        sum_send,
+        sum_recv,
+    ):
+        place = Place(groups, replicas)
+        me = place.member
+        core = place.core
+
+        def table_copy(b):
+            return pltpu.make_async_copy(
+                table_ref.at[pl.ds(b * block, block), :], wide.at[b % 2], table_sem.at[b % 2]
+            )
+
+        def chip_at(j):
+            return lax.rem(place.chip + j, chips)
+
+        def chip_before(j):
+            return lax.rem(place.chip + chips - j, chips)
+
+        def lane_device(j):
+            return place.at(place.replica, chip_at(j) * 2 + core)
+
+        def plane_device(k):
+            return place.at(lax.rem(place.replica + k, replicas), me)
+
+        def replica_before(k):
+            return lax.rem(place.replica + replicas - k, replicas)
+
+        def lane_copy(j):
+            return remote(own_ref, hid.at[me], lane_send.at[j], lane_recv.at[j], lane_device(j))
+
+        def lane_slot(j):
+            return chip_before(j) * 2 + core
+
+        def lane_wait(j):
+            there = hid.at[lane_slot(j)]
+            remote(there, there, lane_send.at[j], lane_recv.at[j], lane_device(j)).wait_recv()
+
+        def core_copy(j):
+            here = hid.at[lane_slot(j)]
+            return remote(here, here, core_send.at[j], core_recv.at[j], place.sibling())
+
+        def core_wait(j):
+            there = hid.at[chip_before(j) * 2 + 1 - core]
+            remote(there, there, core_send.at[j], core_recv.at[j], place.sibling()).wait_recv()
+
+        def plane_copy(k, j):
+            slot = lane_slot(j)
+            return remote(
+                hid.at[slot],
+                all_ref.at[place.replica * groups + slot],
+                plane_send.at[k, j],
+                plane_recv.at[k, j],
+                plane_device(k),
+            )
+
+        def plane_wait(k, j):
+            there = all_ref.at[replica_before(k) * groups + lane_slot(j)]
+            remote(
+                there, there, plane_send.at[k, j], plane_recv.at[k, j], plane_device(k)
+            ).wait_recv()
+
+        def pass_copy(k, j):
+            here = all_ref.at[replica_before(k) * groups + lane_slot(j)]
+            return remote(
+                here, here, pass_send.at[k, j], pass_recv.at[k, j], place.sibling()
+            )
+
+        def pass_wait(k, j):
+            there = all_ref.at[
+                replica_before(k) * groups + chip_before(j) * 2 + 1 - core
+            ]
+            remote(
+                there, there, pass_send.at[k, j], pass_recv.at[k, j], place.sibling()
+            ).wait_recv()
+
+        def member_at(k):
+            return lax.rem(me + k, groups)
+
+        def stat_copy(k):
+            return remote(
+                shares.at[me],
+                shares.at[me],
+                stat_send.at[k],
+                stat_recv.at[k],
+                place.at(place.replica, member_at(k)),
+            )
+
+        def stat_wait(k):
+            there = shares.at[lax.rem(me + groups - k, groups)]
+            remote(
+                there, there, stat_send.at[k], stat_recv.at[k], place.at(place.replica, me)
+            ).wait_recv()
+
+        def line_copy(k):
+            here = logsum_ref.at[place.replica]
+            return remote(here, here, line_send.at[k], line_recv.at[k], plane_device(k))
+
+        def line_wait(k):
+            there = logsum_ref.at[replica_before(k)]
+            remote(there, there, line_send.at[k], line_recv.at[k], plane_device(k)).wait_recv()
+
+        def part_copy(j):
+            return remote(
+                to_core.at[j], from_core.at[j], part_send.at[j], part_recv.at[j], place.sibling()
+            )
+
+        def sum_copy(j):
+            return remote(
+                to_lane.at[j], from_lane.at[j], sum_send.at[j], sum_recv.at[j], lane_device(j)
+            )
+
+        table_copy(0).start()
+        if blocks > 1:
+            table_copy(1).start()
+        meet(
+            [place.at(place.replica, member_at(k)) for k in range(1, groups)] + place.planes()
+        )
+        own_core = remote(own_ref, hid.at[me], core_send.at[0], core_recv.at[0], place.sibling())
+        own_core.start()
+        for j in range(1, chips):
+            lane_copy(j).start()
+        hid[me] = own_ref[...]
+        for k in range(1, replicas):
+            plane_copy(k, 0).start()
+        for b in range(blocks):
+            table_copy(b).wait()
+            low[b] = wide[b % 2].astype(NARROW)
+            if b + 2 < blocks:
+                table_copy(b + 2).start()
+
+        spots = lax.broadcasted_iota(jnp.int32, (block, own), 0)
+
+        def forward(step, carry):
+            j = step // 2
+            other = lax.rem(step, 2)
+
+            @pl.when(step == 1)
+            def _():
+                there = hid.at[place.sibling_member]
+                remote(
+                    there, there, core_send.at[0], core_recv.at[0], place.sibling()
+                ).wait_recv()
+
+            @pl.when((step > 1) & (other == 0))
+            def _():
+                lane_wait(j)
+                core_copy(j).start()
+
+                def spread(k, carry):
+                    plane_copy(k, j).start()
+                    return carry
+
+                lax.fori_loop(1, replicas, spread, 0)
+
+            @pl.when((step > 1) & (other == 1))
+            def _():
+                core_wait(j)
+
+            member = chip_before(j) * 2 + lax.rem(core + other, 2)
+            here = hid[member]
+            wanted = target_ref[member]
+            hit = jnp.zeros((1, own), FLOAT)
+            for b in range(blocks):
+                logits = lax.dot_general(
+                    low[b], here, LAST_CONTRACT, preferred_element_type=FLOAT
+                )
+                top = jnp.max(logits, axis=0, keepdims=True)
+                values = jnp.exp(logits - top)
+                tops[member, b : b + 1, :] = top
+                totals[member, b : b + 1, :] = jnp.sum(values, axis=0, keepdims=True)
+                hit = hit + jnp.sum(
+                    jnp.where(spots == wanted - b * block, logits, 0.0), axis=0, keepdims=True
+                )
+                exps[b, member] = values.astype(NARROW)
+            hits[pl.ds(member, 1), :] = hit
+            block_tops = tops[member, :blocks, :]
+            top = jnp.max(block_tops, axis=0, keepdims=True)
+            total = jnp.sum(
+                totals[member, :blocks, :] * jnp.exp(block_tops - top), axis=0, keepdims=True
+            )
+            shares[me, pl.ds(member, 1), :] = top + jnp.log(total)
+            return carry
+
+        lax.fori_loop(0, groups, forward, 0)
+        local = pltpu.make_async_copy(
+            hid, all_ref.at[pl.ds(place.replica * groups, groups)], local_sem
+        )
+        local.start()
+        for k in range(1, groups):
+            stat_copy(k).start()
+        for k in range(1, groups):
+            stat_wait(k)
+        every = shares[...]
+        top = jnp.max(every, axis=0)
+        logsum_ref[place.replica] = top + jnp.log(jnp.sum(jnp.exp(every - top[None]), axis=0))
+        for k in range(1, replicas):
+            line_copy(k).start()
+
+        def member_back(member):
+            wanted = target_ref[member]
+            weights = weight_ref[member]
+            logsum = logsum_ref[place.replica, pl.ds(member, 1), :]
+            total = jnp.zeros((own, width), FLOAT)
+            for b in range(blocks):
+                scale = weights * jnp.exp(tops[member, b : b + 1, :] - logsum)
+                grads = exps[b, member].astype(FLOAT) * scale
+                grads = jnp.where(spots == wanted - b * block, grads - weights, grads)
+                total = total + lax.dot_general(
+                    grads.astype(NARROW), low[b], ROWS_CONTRACT, preferred_element_type=FLOAT
+                )
+            return total
+
+        def backward(step, carry):
+            j = lax.rem(step + 1, chips)
+
+            @pl.when(step == chips - 1)
+            def _():
+                for k in range(1, replicas):
+                    for c in range(chips):
+                        plane_wait(k, c)
+                for k in range(1, replicas):
+                    for c in range(chips):
+                        pass_copy(k, c).start()
+
+            there = chip_at(j) * 2
+            to_core[j] = member_back(there + 1 - core)
+            part_copy(j).start()
+            mine = member_back(there + core)
+            part_copy(j).wait_recv()
+            mine = mine + from_core[j]
+
+            @pl.when(j > 0)
+            def _():
+                to_lane[j] = mine
+                sum_copy(j).start()
+
+            @pl.when(j == 0)
+            def _():
+                grad_ref[...] = mine
+
+            return carry
+
+        lax.fori_loop(0, chips, backward, 0)
+        held = lax.broadcasted_iota(jnp.int32, (groups, own), 0) == me
+        amounts = jnp.concatenate([weight_ref[m] for m in range(groups)], axis=0)
+        losses = amounts * (jnp.where(held, logsum_ref[place.replica], 0.0) - hits[...])
+        loss_ref[...] = jnp.sum(losses, axis=0, keepdims=True)
+        for j in range(1, chips):
+            sum_copy(j).wait_recv()
+            grad_ref[...] += from_lane[j]
+        local.wait()
+        own_core.wait_send()
+        for k in range(1, groups):
+            stat_copy(k).wait_send()
+        for k in range(1, replicas):
+            line_wait(k)
+            line_copy(k).wait_send()
+            for j in range(chips):
+                pass_wait(k, j)
+                plane_copy(k, j).wait_send()
+                pass_copy(k, j).wait_send()
+        for j in range(chips):
+            part_copy(j).wait_send()
+            if j > 0:
+                lane_copy(j).wait_send()
+                core_copy(j).wait_send()
+                sum_copy(j).wait_send()
+
+    whole = pl.BlockSpec(memory_space=pltpu.VMEM)
+    anywhere = pl.BlockSpec(memory_space=pl.ANY)
+    dma = pltpu.SemaphoreType.DMA
+    vmem = pltpu.VMEM
+    grad, logsum, loss, everyone = pl.pallas_call(
+        kernel,
+        in_specs=[anywhere, whole, whole, whole],
+        out_specs=[whole, whole, whole, anywhere],
+        out_shape=[
+            jax.ShapeDtypeStruct((own, width), FLOAT),
+            jax.ShapeDtypeStruct((replicas, groups, own), FLOAT),
+            jax.ShapeDtypeStruct((1, own), FLOAT),
+            jax.ShapeDtypeStruct((replicas * groups, own, width), NARROW),
+        ],
+        scratch_shapes=[
+            vmem((2, block, width), FLOAT),
+            vmem((blocks, block, width), NARROW),
+            vmem((groups, own, width), NARROW),
+            vmem((blocks, groups, block, own), NARROW),
+            vmem((groups, lines, own), FLOAT),
+            vmem((groups, lines, own), FLOAT),
+            vmem((groups, own), FLOAT),
+            vmem((groups, groups, own), FLOAT),
+            vmem((chips, own, width), FLOAT),
+            vmem((chips, own, width), FLOAT),
+            vmem((chips, own, width), FLOAT),
+            vmem((chips, own, width), FLOAT),
+            dma((2,)),
+            dma,
+            dma((chips,)),
+            dma((chips,)),
+            dma((chips,)),
+            dma((chips,)),
+            dma((replicas, chips)),
+            dma((replicas, chips)),
+            dma((replicas, chips)),
+            dma((replicas, chips)),
+            dma((groups,)),
+            dma((groups,)),
+            dma((replicas,)),
+            dma((replicas,)),
+            dma((chips,)),
+            dma((chips,)),
+            dma((chips,)),
+            dma((chips,)),
+        ],
+        compiler_params=pltpu.CompilerParams(
+            vmem_limit_bytes=VMEM_LIMIT, collective_id=3, has_side_effects=True
+        ),
+        cost_estimate=pl.CostEstimate(
+            flops=4 * vocab * groups * own * width,
+            bytes_accessed=vocab * width * 4,
+            transcendentals=vocab * groups * own,
+        ),
+    )(
+        table,
+        own_hidden,
+        target.reshape(groups, 1, own),
+        weight.reshape(groups, 1, own),
+    )
+    return grad, logsum.reshape(-1), jnp.sum(loss), everyone.reshape(-1, width)
+
+
+def head_table_grad(
+    table, hidden, logsum, weights, target, token_grad, slices, groups, replicas
+):
+    vocab, width = table.shape
+    amount = groups * replicas
     rows = hidden.shape[0]
     own = token_grad.shape[0]
     tile = math.gcd(rows, 2048)
@@ -395,10 +1018,15 @@
         weight_ref,
         target_ref,
         own_ref,
+        slices_ref,
         grad_ref,
         square_ref,
         all_ref,
+        summed_ref,
+        gathered,
         local_sem,
+        slice_send,
+        slice_recv,
         lane_send,
         lane_recv,
         plane_send,
@@ -443,14 +1071,46 @@
                 there, there, core_send.at[r, c], core_recv.at[r, c], place.sibling()
             ).wait_recv()
 
+        def device(index):
+            return place.at(index // groups, lax.rem(index, groups))
+
+        def slice_copy(k):
+            there = lax.rem(me + k, amount)
+            return remote(
+                slices_ref.at[lax.rem(there, groups)],
+                gathered.at[me],
+                slice_send.at[k],
+                slice_recv.at[k],
+                device(there),
+            )
+
         local = pltpu.make_async_copy(own_ref, all_ref.at[me], local_sem)
 
         @pl.when(step == 0)
         def _():
-            meet(place.lanes() + place.planes() + [place.sibling()])
+            barrier = pltpu.get_barrier_semaphore()
+
+            def greet(k, carry):
+                pl.semaphore_signal(
+                    barrier,
+                    inc=1,
+                    device_id=device(lax.rem(me + k, amount)),
+                    device_id_type=MESH,
+                )
+                return carry
+
+            lax.fori_loop(1, amount, greet, 0)
+            pl.semaphore_wait(barrier, amount - 1)
             local.start()
             for k in range(1, chips):
                 lane_copy(k).start()
+
+            def give(k, carry):
+                slice_copy(k).start()
+                return carry
+
+            lax.fori_loop(1, amount, give, 0)
+            gathered[me] = slices_ref[place.member]
 
         @pl.when(step == when_plane)
         def _():
@@ -507,6 +1167,14 @@
 
         @pl.when(step == last)
         def _():
+            def take(k, carry):
+                there = gathered.at[lax.rem(me + amount - k, amount)]
+                remote(there, there, slice_send.at[k], slice_recv.at[k], device(me)).wait_recv()
+                slice_copy(k).wait_send()
+                return carry
+
+            lax.fori_loop(1, amount, take, 0)
+            summed_ref[...] = jnp.sum(gathered[...], axis=0)
             for r in range(replicas):
                 for c in range(chips):
                     core_wait(r, c)
@@ -525,19 +1193,26 @@
     return pl.pallas_call(
         kernel,
         grid=(steps,),
-        in_specs=[pl.BlockSpec((block, width), lambda i: (i, 0))] + [whole] * 4 + [anywhere],
+        in_specs=[pl.BlockSpec((block, width), lambda i: (i, 0))]
+        + [whole] * 4
+        + [anywhere, whole],
         out_specs=[
             pl.BlockSpec((block, width), lambda i: (i, 0)),
             pl.BlockSpec((1, width), lambda i: (0, 0)),
             anywhere,
+            whole,
         ],
         out_shape=[
             jax.ShapeDtypeStruct((vocab, width), FLOAT),
             jax.ShapeDtypeStruct((1, width), FLOAT),
             jax.ShapeDtypeStruct((groups * replicas, own, width), NARROW),
+            jax.ShapeDtypeStruct(slices.shape[1:], FLOAT),
         ],
         scratch_shapes=[
+            pltpu.VMEM((amount,) + slices.shape[1:], FLOAT),
             dma,
+            dma((amount,)),
+            dma((amount,)),
             dma((chips,)),
             dma((chips,)),
             dma((replicas, chips)),
@@ -560,6 +1235,7 @@
         weights.reshape(shape),
         target.reshape(shape),
         token_grad,
+        slices,
     )
 
 
@@ -710,7 +1386,7 @@
 def table_update(table, grad, moment_low, moment, average, rate, clip):
     vocab, width = table.shape
     sub = moment.shape[0]
-    block = block_rows(vocab, 1100)
+    block = 512
 
     def whole_kernel(clip_ref, table_ref, grad_ref, moment_ref, new_ref):
         new_ref[...], _, _ = update_rule(
@@ -726,7 +1402,7 @@
     scalar = pl.BlockSpec(memory_space=pltpu.SMEM)
     new_table = pl.pallas_call(
         whole_kernel,
-        grid=(vocab // block,),
+        grid=(-(-vocab // block),),
         in_specs=[scalar, spec, spec, spec],
         out_specs=spec,
         out_shape=jax.ShapeDtypeStruct((vocab, width), FLOAT),
@@ -734,52 +1410,65 @@
     )(clip, table, grad, moment_low)
 
     window = max(-(-(sub + sub * r % 8) // 8) * 8 for r in range(vocab // sub))
-    tile = 256
+    tile = 264
+    tiles = -(-window // tile)
 
     def own_kernel(
         clip_ref, table_ref, grad_ref, moment_ref, average_ref, moment_out, average_out, *scratch
     ):
         table_win, grad_win, sems = scratch
+        step = pl.program_id(0)
         begin = lax.axis_index("dp") * sub
         low = pl.multiple_of(begin // 8 * 8, 8)
         shift = begin - low
-        copies = [
-            pltpu.make_async_copy(table_ref.at[pl.ds(low, window), :], table_win, sems.at[0]),
-            pltpu.make_async_copy(grad_ref.at[pl.ds(low, window), :], grad_win, sems.at[1]),
-        ]
-        for copy in copies:
-            copy.start()
-        for copy in copies:
-            copy.wait()
-        for first in range(0, sub, tile):
-            size = min(tile, sub - first)
-            span = min(-(-size // 8) * 8 + 8, window - first)
-            amount = jnp.where(shift == 0, 0, span - shift)
-            own_table = pltpu.roll(table_win[first : first + span, :], amount, 0)[:size]
-            own_grad = pltpu.roll(grad_win[first : first + span, :], amount, 0)[:size]
-            _, new_moment, new_average = update_rule(
-                own_table,
-                own_grad,
-                moment_ref[first : first + size, :],
-                average_ref[first : first + size, :],
-                rate,
-                clip_ref[0],
-            )
-            moment_out[first : first + size, :] = new_moment
-            average_out[first : first + size, :] = new_average
+
+        def fetch(t):
+            first = t * tile
+            size = min(tile, window - first)
+            return [
+                pltpu.make_async_copy(
+                    source.at[pl.ds(low + first, size), :],
+                    win.at[pl.ds(first, size), :],
+                    sems.at[i, t],
+                )
+                for i, (source, win) in enumerate(((table_ref, table_win), (grad_ref, grad_win)))
+            ]
+
+        for t in range(tiles):
+
+            @pl.when(step == t)
+            def _():
+                if t == 0:
+                    for other in range(tiles):
+                        for copy in fetch(other):
+                            copy.start()
+                    for copy in fetch(0):
+                        copy.wait()
+                if t + 1 < tiles:
+                    for copy in fetch(t + 1):
+                        copy.wait()
+
+        first = pl.multiple_of(step * tile, 8)
+        amount = jnp.where(shift == 0, 0, tile + 8 - shift)
+        own_table = pltpu.roll(table_win[pl.ds(first, tile + 8), :], amount, 0)[:tile]
+        own_grad = pltpu.roll(grad_win[pl.ds(first, tile + 8), :], amount, 0)[:tile]
+        _, moment_out[...], average_out[...] = update_rule(
+            own_table, own_grad, moment_ref[...], average_ref[...], rate, clip_ref[0]
+        )
 
     anywhere = pl.BlockSpec(memory_space=pl.ANY)
-    whole = pl.BlockSpec(memory_space=pltpu.VMEM)
     state = jax.ShapeDtypeStruct((sub, width), FLOAT)
+    piece = pl.BlockSpec((tile, width), lambda i: (i, 0))
     new_moment, new_average = pl.pallas_call(
         own_kernel,
-        in_specs=[scalar, anywhere, anywhere, whole, whole],
-        out_specs=[whole, whole],
+        grid=(tiles,),
+        in_specs=[scalar, anywhere, anywhere, piece, piece],
+        out_specs=[piece, piece],
         out_shape=[state, state],
         scratch_shapes=[
-            pltpu.VMEM((window, width), FLOAT),
-            pltpu.VMEM((window, width), FLOAT),
-            pltpu.SemaphoreType.DMA((2,)),
+            pltpu.VMEM((tiles * tile + 8, width), FLOAT),
+            pltpu.VMEM((tiles * tile + 8, width), FLOAT),
+            pltpu.SemaphoreType.DMA((2, tiles)),
         ],
         compiler_params=pltpu.CompilerParams(vmem_limit_bytes=VMEM_LIMIT),
     )(clip, table, grad, moment, average)
@@ -826,13 +1515,21 @@
         tokens, marks, lengths[:, 0], buffers
     )
     packed = jnp.concatenate(
-        [tokens, divisor, jnp.broadcast_to(jnp.sum(counted), (1, seq))], axis=0
-    )
-    everyone = lax.all_gather(packed, ("dp", "fsdp"))
-    in_full, out_full, vector_full = (
-        lax.all_gather(in_weights.astype(NARROW), "fsdp", axis=0, tiled=True),
-        lax.all_gather(out_weights.astype(NARROW), "fsdp", axis=0, tiled=True),
-        lax.all_gather(vectors.astype(NARROW), "fsdp", axis=0, tiled=True),
+        [
+            tokens,
+            divisor,
+            jnp.broadcast_to(jnp.sum(counted), (8 - 2 * batches, seq)),
+        ],
+        axis=0,
+    )
+    amount = vectors.shape[0]
+    line = jnp.pad(vectors, (0, -amount % 1024)).reshape(-1, 128)
+    everyone, lines, in_full, out_full, resid = start_kernel(
+        packed, line, in_weights, out_weights, embed_table, batches, groups, replicas
+    )
+    vector_full = lines.reshape(groups, -1)[:, :amount].reshape(-1).astype(NARROW)
+    embed_moment, head_moment, everyone = lax.optimization_barrier(
+        (embed_moment, head_moment, everyone)
     )
     embed_moment_low = lax.all_gather(embed_moment.astype(NARROW), "dp", axis=0, tiled=True)
     head_moment_low = lax.all_gather(head_moment.astype(NARROW), "dp", axis=0, tiled=True)
@@ -852,15 +1549,6 @@
     def group_part(values):
         return lax.dynamic_slice_in_dim(values, replica * rows_all, rows_all, 0)
 
-    local_rows = group_part(local_all)
-    inside = (local_rows >= 0) & (local_rows < vocab_rows)
-    rows = jnp.take(embed_table, jnp.clip(local_rows, 0, vocab_rows - 1), axis=0)
-    resid = lax.psum_scatter(
-        jnp.where(inside[:, None], rows, 0.0).astype(NARROW),
-        "fsdp",
-        scatter_dimension=0,
-        tiled=True,
-    ).astype(FLOAT)
     parts = vector_parts(vector_full.astype(FLOAT), width, hidden)
     places = jnp.arange(seq, dtype=jnp.int32)
     allowed = (buffers[:, :, None] == buffers[:, None, :]) & (
@@ -870,28 +1558,9 @@
     layer_out, kept = layer_forward(resid, in_full, out_full, parts, allowed, cosine, sine, factor)
     unit_last, scale_last = norm_unit(layer_out)
     final = (unit_last * parts[4] + parts[5]).astype(NARROW)
-    group_hidden = lax.all_gather(final, "fsdp", axis=0, tiled=True)
-    all_hidden = lax.all_gather(group_hidden, "dp", axis=0, tiled=True)
-
-    head_low = head_table.astype(NARROW)
-    target = group_part(target_all)
-    weight = group_part(weight_all)
-    exps, tops, totals, hits = head_forward(head_low, group_hidden, target)
-    top = jnp.max(tops, axis=0)
-    total = jnp.sum(totals * jnp.exp(tops - top), axis=0)
-    stats = lax.all_gather(jnp.stack([top, total, hits]), "fsdp")
-    top_all = jnp.max(stats[:, 0], axis=0)
-    logsum = top_all + jnp.log(jnp.sum(stats[:, 1] * jnp.exp(stats[:, 0] - top_all), axis=0))
-    logsum_all = lax.all_gather(logsum, "dp", axis=0, tiled=True)
-    own = member * own_rows
-    loss_part = jnp.sum(
-        lax.dynamic_slice_in_dim(
-            weight * (logsum - jnp.sum(stats[:, 2], axis=0)), own, own_rows
-        )
-    )
-    scales = weight * jnp.exp(tops - logsum)
-    back = head_back(head_low, exps, scales, weight, target)
-    final_grad = lax.psum_scatter(back, "fsdp", scatter_dimension=0, tiled=True)
+    final_grad, logsum_all, loss_part, all_hidden = head_kernel(
+        head_table, final, group_part(target_all), group_part(weight_all), groups, replicas
+    )
 
     less_weight = logsum_all - jnp.log(jnp.maximum(weight_all, 1e-30))
     shifted = jnp.where(weight_all > 0.0, less_weight, 1e30)
@@ -929,13 +1598,24 @@
             )
         )
     )
-    layer_grads = [
-        lax.psum(lax.psum_scatter(grad, "fsdp", scatter_dimension=0, tiled=True), "dp")
-        for grad in (in_grad, out_grad, vector_grad)
+    parts_low = [
+        lax.psum_scatter(grad, "fsdp", scatter_dimension=0, tiled=True)
+        for grad in (in_grad, out_grad)
     ]
-    head_grad, head_square, token_grads = head_table_grad(
-        head_table, all_hidden, shifted, weight_all, target_all, token_grad, groups, replicas
-    )
+    slices = jnp.pad(vector_grad.reshape(groups, amount), ((0, 0), (0, -amount % 1024)))
+    head_grad, head_square, token_grads, vector_sum = head_table_grad(
+        head_table,
+        all_hidden,
+        shifted,
+        weight_all,
+        target_all,
+        token_grad,
+        slices.reshape(groups, -1, 128),
+        groups,
+        replicas,
+    )
+    parts_low, token_grads = lax.optimization_barrier((parts_low, token_grads))
+    layer_grads = list(lax.psum(parts_low, "dp")) + [vector_sum.reshape(-1)[:amount]]
     embed_grad, embed_square = embed_table_grad(token_grads, *lists, vocab_rows)
     square = jnp.sum(embed_square) + jnp.sum(head_square)
     for grad in layer_grads:

time: 953 us -> 600 us (0.63)
  waiting for transfers between devices: 356 us -> 60.1 us
  blocking collectives: 130 us -> 0 us
  Pallas kernels: 296 us -> 397 us
  other arithmetic: 66.7 us -> 50.1 us
    all_gather x4 -> x0, waiting for transfers between devices: 161 us -> none  [the longest x1 87.7 us: shards(): all_hidden = lax.all_gather(group_hidden, 'dp', axis=0, tiled=True)]
    pallas_call x6, Pallas kernels: 109 us -> 217 us  [the longest x1 93 us: head_kernel(): pl.pallas_call(kernel, in_specs=[anywhere, whole, whole, whole], out_spec...]
    reduce_scatter x2, waiting for transfers between devices: 88.6 us -> 14 us  [shards(): lax.psum_scatter(grad, 'fsdp', scatter_dimension=0, tiled=True)]
    all_gather x3 -> x0, blocking collectives: 66 us -> none  [the longest x1 43.7 us: shards(): everyone = lax.all_gather(packed, ('dp', 'fsdp'))]
    unnamed x2 -> x0, blocking collectives: 54.7 us -> none
    all_gather x1, waiting for transfers between devices: 57.8 us -> 9.81 us  [shards(): lax.all_gather(head_moment.astype(NARROW), 'dp', axis=0, tiled=True)]
    reduce_scatter x2 -> x0, waiting for transfers between devices: 47.6 us -> none  [the longest x1 47.6 us: shards(): final_grad = lax.psum_scatter(back, 'fsdp', scatter_dimension=0, tiled=True)]
    psum x1, waiting for transfers between devices: 0.02 us -> 35.8 us  [shards(): lax.psum(parts_low, 'dp')]
  transfers between devices with their start and end apart: 11 -> 5, of which waited for: 8 -> 3; matrix products, arithmetic and copies ran while one was open for 7% -> 14% of each run, Pallas kernels for 24% -> 44%
where the time goes in v2:
time: 600 us; the launch traced here: 594 us
  Pallas kernels  397 us (66%)
  waiting for transfers between devices  60.1 us (10%)
  other arithmetic  50.1 us (8%)
  local copies, waits for them, and re-layouts  34.9 us (6%)
  matrix products  30.4 us (5%)
  between operations  21.1 us (4%)
    pallas_call x1, Pallas kernels, head_table_grad(): pl.pallas_call(kernel, grid=(steps,), in_specs=[pl.BlockSpec((block, widt...  150 us
    pallas_call x1, Pallas kernels, head_kernel(): pl.pallas_call(kernel, in_specs=[anywhere, whole, whole, whole], out_spec...  93 us
    pallas_call x1, Pallas kernels, start_kernel(): pl.pallas_call(kernel, in_specs=[whole, whole, whole, whole, anywhere], o...  66.4 us
    pallas_call x2, Pallas kernels, table_update(): pl.pallas_call(whole_kernel, grid=(-(-vocab // block),), in_specs=[scalar...  37.5 us
    psum x1, waiting for transfers between devices, shards(): lax.psum(parts_low, 'dp')  35.8 us
    pallas_call x2, Pallas kernels, table_update(): pl.pallas_call(own_kernel, grid=(tiles,), in_specs=[scalar, anywhere, any...  20 us
    pallas_call x1, Pallas kernels, embed_table_grad(): pl.pallas_call(kernel, grid_spec=pltpu.PrefetchScalarGridSpec(num_scalar_...  19.6 us
    reduce_scatter x2, waiting for transfers between devices, shards(): lax.psum_scatter(grad, 'fsdp', scatter_dimension=0, tiled=True)  14 us
  transfers between devices with their start and end apart: 5, of which 3 were waited for; matrix products, arithmetic and copies ran while one was open for 14% of the time, Pallas kernels for 44%

profile of v2, /device:TPU:0, one launch (start us, length us, event | category | flops | bytes accessed | tf_op | source)
XLA Modules:
  0.0 594.2 jit_solution(6854088462769360848)
XLA Ops:
  7.2 0.8 slice_compare_fusion
  8.1 0.8 fusion.69
  8.8 0.8 fusion.66
  9.6 0.8 fusion.67
  11.0 1.3 pad_bitcast_fusion.1.line_ref
  13.0 1.3 add_add_fusion.packed_ref
  14.4 66.4 %shard_map.314 = (s32[32,8,128]{2,1,0:T(8,128)}, f32[8,8,128]{2,1,0:T(8,128)}, bf16[8,64,3584]{2,1,0:T(8,128)(2,1)}, bf16[8,320,512]{2,1,0:T(8,128)(2,1)}, f32[256,512]{1,0:T(8,128)}) custom-call(s32[8,128]{1,0:T(8,128)} %add_add_fusion.packed_ref, f32[8,128]{1,0:T(8,128)} %pad_bitcast_fusion.1.line_ref, f32[64,3584]{1,0:T(8,128)} %in_ref.1, ...), custom_call_target="tpu_custom_call" | custom-call | bytes 12877824 | tf_op jit(solution)/shard_map/pallas_call | solution.py:568
  80.8 1.4 convert_bitcast_fusion.1
  82.2 3.3 convert_bitcast_fusion
  85.8 0.8 copy-done
  86.9 2.3 convolution_add_fusion
  89.2 1.6 copy.90
  90.9 1.1 slice.260
  92.0 1.3 slice_bitcast_fusion
  93.5 1.0 slice.152
  94.5 1.6 slice_reduce_fusion.1
  98.5 8.1 %fusion.4 = (bf16[256,2048]{1,0:T(8,128)(2,1)S(1)}, f32[256,2048]{1,0:T(8,128)}) fusion(f32[2048]{0:T(1024)S(1)} %slice-done, bf16[512,3584]{1,0:T(8,128)(2,1)} %bitcast.127, f32[512]{0:T(512)S(1)} %get-tuple-element.129, f32[512]{0:T(512)S(1)} %get-tuple-element.130, f32[256]{0:T(256)S(1)} %add_rsqrt_fusion.1, f32[256,512]{1,0:T(8,128)S(1)} %copy-done, ...), kind=kOutput, calls=%fused_computation.12 | convolution fusion | flops 572129280 | bytes 5781504 | tf_op jit(solution)/shard_map/dot_general | solution.py:131
  106.6 0.9 fusion.83
  108.4 0.9 fusion.64
  110.7 0.9 add_convert_fusion.1.own_ref
  111.5 93.0 %shard_map.315 = (f32[256,512]{1,0:T(8,128)}, f32[4,8,256]{2,1,0:T(8,128)}, f32[1,256]{1,0:T(1,128)}, bf16[32,256,512]{2,1,0:T(8,128)(2,1)}) custom-call(f32[6288,512]{1,0:T(8,128)} %table_ref.13, bf16[256,512]{1,0:T(8,128)(2,1)} %add_convert_fusion.1.own_ref, s32[8,1,256]{2,1,0:T(1,128)} %bitcast.145, f32[8,1,256]{2,1,0:T(1,128)} %bitcast.146), custom_call_target="tpu_custom_call" | custom-call | flops 26373783552 | bytes 12877824 | tf_op jit(solution)/shard_map/pallas_call | solution.py:940
  204.5 2.2 multiply_reduce_fusion.3
  206.7 2.0 fusion.79
  208.7 0.9 fusion.57
  209.5 1.5 copy-done.3
  212.2 1.2 copy.110
  213.4 1.5 stack_reshape.3
  214.8 1.3 fusion.49
  216.2 2.9 convolution_bitcast_fusion.1
  219.0 1.1 copy.144
  220.2 3.0 convolution_bitcast_fusion.2
  223.1 1.1 copy.145
  225.4 1.6 fusion.65
  227.9 2.2 fusion.20
  230.6 1.2 fusion.77
  231.9 1.7 copy-done.17
  233.6 1.0 multiply_reduce_fusion.4
  235.0 0.9 add_convert_fusion.own_ref
  235.9 2.4 fusion.59
  238.4 3.3 fusion.38
  241.6 0.9 fusion.40
  242.5 1.0 copy-done.2
  243.5 3.5 pad_maximum_fusion
  247.0 6.5 %select_reduce_fusion = (s32[16,512]{1,0:T(8,128)S(1)}, s32[16,512]{1,0:T(8,128)S(1)}) fusion(s32[16,512]{1,0:T(8,128)S(1)} %sub.172, s32[16,512]{1,0:T(8,128)S(1)} %convolution_convert_fusion.1, pred[16,512]{1,0:T(8,128)(4,1)S(1)} %compare_and_fusion.1), kind=kLoop, calls=%fused_computation.1 | loop fusion | flops 25149440 | bytes 139264 | tf_op jit(solution)/shard_map/reduce_sum | solution.py:1307
  253.6 5.2 reshape.375.moment_ref
  258.8 9.8 %all-gather.7.cloned.1.call-done = bf16[4,1572,512]{2,1,0:T(8,128)(2,1)} async-done(((bf16[1,1572,512]{2,1,0:T(8,128)(2,1)}), bf16[4,1572,512]{2,1,0:T(8,128)(2,1)}) %all-gather.7.cloned.1.call-update) | async-done | bytes 6438928 | tf_op jit(solution)/shard_map/all_gather | solution.py:1535
  268.6 5.5 reshape.377.moment_ref
  276.3 149.7 %shard_map.316 = (f32[6288,512]{1,0:T(8,128)}, f32[1,512]{1,0:T(1,128)}, bf16[32,256,512]{2,1,0:T(8,128)(2,1)}, f32[8,128]{1,0:T(8,128)}) custom-call(f32[6288,512]{1,0:T(8,128)} %table_ref.13, bf16[8192,512]{1,0:T(8,128)(2,1)} %bitcast.150, f32[4,1,2048]{2,1,0:T(1,128)} %compare_select_fusion.logsum_ref, f32[4,1,2048]{2,1,0:T(1,128)} %bitcast.131, ...), custom_call_target="tpu_custom_call" | custom-call | flops 105495134208 | bytes 42532864 | tf_op jit(solution)/shard_map/pallas_call | solution.py:1193
  426.0 13.9 %reduce-scatter.3.cloned.1.call-done = f32[64,3584]{1,0:T(8,128)} async-done(((f32[512,3584]{1,0:T(8,128)}), f32[64,3584]{1,0:T(8,128)}) %reduce-scatter.3.cloned.1.call-update) | async-done | bytes 917520 | tf_op jit(solution)/shard_map/reduce_scatter | solution.py:1602
  441.9 1.3 reduce_sum.357
  443.1 1.3 multiply_reduce_fusion.11
  444.4 19.6 %shard_map.317 = (f32[6288,512]{1,0:T(8,128)}, f32[1,512]{1,0:T(1,128)}) custom-call(s32[16]{0:T(128)} %reduce_sum.355.count_ref, s32[16,1,512]{2,1,0:T(1,128)} %reshape.363.place_ref, s32[16,1,512]{2,1,0:T(1,128)} %reshape.364.row_ref, bf16[8192,512]{1,0:T(8,128)(2,1)} %bitcast.115), custom_call_target="tpu_custom_call" | custom-call | tf_op jit(solution)/shard_map/pallas_call | solution.py:1349
  464.1 1.3 reduce_sum.356
  466.7 35.8 %all-reduce.8.cloned.1.call-done = (f32[64,3584]{1,0:T(8,128)}, f32[320,512]{1,0:T(8,128)}) async-done(((f32[64,3584]{1,0:T(8,128)}, f32[320,512]{1,0:T(8,128)}), (f32[64,3584]{1,0:T(8,128)}, f32[320,512]{1,0:T(8,128)})) %all-reduce.8.cloned.1.call-update) | async-done | bytes 1572880 | tf_op jit(solution)/shard_map/psum | solution.py:1618
  502.4 2.0 multiply_reduce_fusion.1
  504.5 1.9 multiply_reduce_fusion.2
  509.7 11.1 %shard_map.318 = f32[32,8,128]{2,1,0:T(8,128)} custom-call(f32[8,128]{1,0:T(8,128)} %pad.19.own_ref), custom_call_target="tpu_custom_call" | custom-call | tf_op jit(solution)/shard_map/pallas_call | solution.py:1289
  520.7 1.1 slice_reduce_fusion
  523.1 18.7 %shard_map.319 = f32[6288,512]{1,0:T(8,128)} custom-call(f32[1]{0:T(128)} %bitcast.33.clip_ref, f32[6288,512]{1,0:T(8,128)} %table_ref.11, f32[6288,512]{1,0:T(8,128)} %get-tuple-element.77.grad_ref, bf16[6288,512]{1,0:T(8,128)(2,1)} %reshape.375.moment_ref), custom_call_target="tpu_custom_call" | custom-call | tf_op jit(solution)/shard_map/pallas_call | solution.py:1403
  541.9 9.9 %shard_map.320 = (f32[1572,512]{1,0:T(8,128)}, f32[1572,512]{1,0:T(8,128)}) custom-call(f32[1]{0:T(128)} %bitcast.33.clip_ref, f32[6288,512]{1,0:T(8,128)} %table_ref.11, f32[6288,512]{1,0:T(8,128)} %get-tuple-element.77.grad_ref, f32[1572,512]{1,0:T(8,128)} %moment_ref, f32[1572,512]{1,0:T(8,128)} %average_ref.2), custom_call_target="tpu_custom_call" | custom-call | tf_op jit(solution)/shard_map/pallas_call | solution.py:1462
  551.8 18.8 %shard_map.321 = f32[6288,512]{1,0:T(8,128)} custom-call(f32[1]{0:T(128)} %bitcast.33.clip_ref, f32[6288,512]{1,0:T(8,128)} %table_ref.13, f32[6288,512]{1,0:T(8,128)} %get-tuple-element.81.grad_ref, bf16[6288,512]{1,0:T(8,128)(2,1)} %reshape.377.moment_ref), custom_call_target="tpu_custom_call" | custom-call | tf_op jit(solution)/shard_map/pallas_call | solution.py:1403
  570.5 10.1 %shard_map.322 = (f32[1572,512]{1,0:T(8,128)}, f32[1572,512]{1,0:T(8,128)}) custom-call(f32[1]{0:T(128)} %bitcast.33.clip_ref, f32[6288,512]{1,0:T(8,128)} %table_ref.13, f32[6288,512]{1,0:T(8,128)} %get-tuple-element.81.grad_ref, f32[1572,512]{1,0:T(8,128)} %moment_ref.1, f32[1572,512]{1,0:T(8,128)} %average_ref.3), custom_call_target="tpu_custom_call" | custom-call | tf_op jit(solution)/shard_map/pallas_call | solution.py:1462
  580.7 3.1 add_multiply_fusion
  583.9 1.5 add_multiply_fusion.1
  (197 shorter events, 16.7 us)
Async XLA Ops:
  7.2 246.4 %all-gather.5.cloned.1.call-start = ((), (), s32[]{:S(2)}) async-start(), calls=%async_computation.4 | async-start | bytes 8069120 | tf_op jit(solution)/shard_map/all_gather | solution.py:1534
  14.4 66.4 %copy-start.1 = (f32[1572,512]{1,0:T(8,128)S(1)}, f32[1572,512]{1,0:T(8,128)}, u32[]{:S(2)}) copy-start(f32[1572,512]{1,0:T(8,128)} %moment_ref) | copy-start | bytes 9658372
  82.2 3.4 copy-start.35
  82.2 186.4 %all-gather.7.cloned.1.call-start = ((), (), s32[]{:S(2)}) async-start(), calls=%async_computation.5 | async-start | bytes 8069120 | tf_op jit(solution)/shard_map/all_gather | solution.py:1535
  85.5 1.0 copy-start
  85.5 340.5 %reduce-scatter.5.cloned.1.call-start = ((), (), s32[]{:S(2)}) async-start(), calls=%async_computation.3 | async-start | bytes 5898240 | tf_op jit(solution)/shard_map/reduce_scatter | solution.py:1602
  85.7 3.5 copy-start.23
  85.7 3.5 copy-start.38
  85.7 3.5 copy-start.40
  85.7 12.7 %copy-start.26 = (f32[512]{0:T(512)}, f32[512]{0:T(512)S(1)}, u32[]{:S(2)}) copy-start(f32[512]{0:T(512)S(1)} %get-tuple-element.129) | copy-start | bytes 6148
  85.8 12.7 %copy-start.28 = (f32[512]{0:T(512)}, f32[512]{0:T(512)S(1)}, u32[]{:S(2)}) copy-start(f32[512]{0:T(512)S(1)} %get-tuple-element.130) | copy-start | bytes 6148
  86.7 11.7 %copy-start.31 = (f32[256]{0:T(256)}, f32[256]{0:T(256)S(1)}, u32[]{:S(2)}) copy-start(f32[256]{0:T(256)S(1)} %broadcast_multiply_fusion.5) | copy-start | bytes 3076
  86.9 11.5 %copy-start.33 = (f32[256]{0:T(256)}, f32[256]{0:T(256)S(1)}, u32[]{:S(2)}) copy-start(f32[256]{0:T(256)S(1)} %add_rsqrt_fusion.1) | copy-start | bytes 3076
  90.8 2.4 copy-start.25
  96.3 1.0 copy-start.24
  96.7 0.7 copy-start.20
  97.1 1.3 slice-start
  98.4 8.2 %copy-start.14 = (bf16[256,512]{1,0:T(8,128)(2,1)}, bf16[256,512]{1,0:T(8,128)(2,1)S(1)}, u32[]{:S(2)}) copy-start(bf16[256,512]{1,0:T(8,128)(2,1)S(1)} %reshape.378) | copy-start | bytes 786436
  98.5 8.1 %copy-start.9 = (bf16[8,320,512]{2,1,0:T(8,128)(2,1)S(1)}, bf16[8,320,512]{2,1,0:T(8,128)(2,1)}, u32[]{:S(2)}) copy-start(bf16[8,320,512]{2,1,0:T(8,128)(2,1)} %get-tuple-element.54) | copy-start | bytes 7864324
  106.6 1.0 copy-start.12
  109.4 95.1 %copy-start.21 = (f32[32,2,128]{2,1,0:T(2,128)}, f32[32,2,128]{2,1,0:T(2,128)S(1)}, u32[]{:S(2)}) copy-start(f32[32,2,128]{2,1,0:T(2,128)S(1)} %fusion.64) | copy-start | bytes 98308
  109.4 95.1 %copy-start.30 = (s32[32,2,128]{2,1,0:T(2,128)}, s32[32,2,128]{2,1,0:T(2,128)S(1)}, u32[]{:S(2)}) copy-start(s32[32,2,128]{2,1,0:T(2,128)S(1)} %pad_subtract_fusion) | copy-start | bytes 98308
  204.5 4.1 copy-start.10
  209.5 1.5 copy-start.3
  227.7 2.3 copy-start.11
  227.9 2.7 copy-start.4
  230.6 2.9 copy-start.17
  230.6 2.9 copy-start.29
  230.6 2.9 copy-start.32
  230.6 2.9 copy-start.34
  230.6 2.9 copy-start.41
  233.6 1.1 copy-start.37
  233.6 1.1 copy-start.46
  233.6 1.1 copy-start.45
  233.6 1.1 copy-start.42
  234.6 1.3 copy-start.39
  235.9 2.4 copy-start.13
  235.9 2.4 copy-start.15
  238.4 3.3 copy-start.27
  241.6 1.9 copy-start.2
  274.1 0.8 copy-start.36
  274.1 0.8 copy-start.22
  274.1 165.9 %reduce-scatter.3.cloned.1.call-start = ((), (), s32[]{:S(2)}) async-start(), calls=%async_computation.2 | async-start | bytes 8257536 | tf_op jit(solution)/shard_map/reduce_scatter | solution.py:1602
  274.7 227.8 %all-reduce.8.cloned.1.call-start = ((), (), s32[]{:S(2)}) async-start(), calls=%async_computation.6 | async-start | bytes 3145728 | tf_op jit(solution)/shard_map/psum | solution.py:1618
  276.3 163.7 %copy-start.49 = (f32[1,256]{1,0:T(1,128)S(1)}, f32[1,256]{1,0:T(1,128)}, u32[]{:S(2)}) copy-start(f32[1,256]{1,0:T(1,128)} %get-tuple-element.57) | copy-start | bytes 3076
  570.5 10.2 %copy-start.5 = (f32[64,3584]{1,0:T(8,128)S(1)}, f32[64,3584]{1,0:T(8,128)}, u32[]{:S(2)}) copy-start(f32[64,3584]{1,0:T(8,128)} %in_ref.1) | copy-start | bytes 2752516
  570.5 10.2 %copy-start.6 = (f32[64,3584]{1,0:T(8,128)S(1)}, f32[64,3584]{1,0:T(8,128)}, u32[]{:S(2)}) copy-start(f32[64,3584]{1,0:T(8,128)} %get-tuple-element.97) | copy-start | bytes 2752516
  570.5 10.2 %copy-start.16 = (f32[64,3584]{1,0:T(8,128)S(1)}, f32[64,3584]{1,0:T(8,128)}, u32[]{:S(2)}) copy-start(f32[64,3584]{1,0:T(8,128)} %param.31) | copy-start | bytes 2752516
  580.7 3.2 copy-start.7
  580.7 3.1 copy-start.8
  580.7 3.1 copy-start.18
  580.7 3.1 copy-start.19
  583.9 1.6 copy-start.43
  583.9 1.5 copy-start.44
  583.9 1.5 copy-start.47
  583.9 1.5 copy-start.48
Sparse Core Ops, SparseCore 0:
  82.3 114.0 all-gather.4
  198.8 69.7 all-gather.6
  274.2 77.8 reduce-scatter.4
  354.8 85.0 reduce-scatter.2
  443.0 59.4 all-reduce.7

commit v3 on v2

--- a/solution.py
+++ b/solution.py
@@ -41,39 +41,27 @@
     return (divisor.astype(jnp.int32), offset, counted.astype(jnp.int32))
 
 
-def vector_parts(vectors, width, hidden):
-    amounts = [width] * 6 + [3 * width, width, hidden, width]
-    parts = []
-    begin = 0
-    for amount in amounts:
-        parts.append(vectors[begin : begin + amount])
-        begin = begin + amount
-    return parts
-
-
-def rotary_tables(offset, rot):
+def rotary_tables(offset, head_size):
+    rot = head_size // 4
     half = rot // 2
+    lanes = 128
     freqs = jnp.power(10000.0, -2.0 * jnp.arange(half, dtype=FLOAT) / rot)
     angles = offset.astype(FLOAT)[:, None] * freqs[None, :]
-    return (jnp.cos(angles)[:, None, :], jnp.sin(angles)[:, None, :])
-
-
-def rotate(values, cosine, sine, rot):
-    half = rot // 2
-    first = values[..., :half]
-    second = values[..., half:rot]
-    return jnp.concatenate(
-        [first * cosine - second * sine, second * cosine + first * sine, values[..., rot:]], axis=-1
-    )
-
-
-def rotate_back(grads, cosine, sine, rot):
-    half = rot // 2
-    first = grads[..., :half]
-    second = grads[..., half:rot]
-    return jnp.concatenate(
-        [first * cosine + second * sine, second * cosine - first * sine, grads[..., rot:]], axis=-1
-    )
+    cosine, sine = jnp.cos(angles), jnp.sin(angles)
+    rows = offset.shape[0]
+    rest = head_size - rot
+    ones, none = jnp.ones((rows, rest), FLOAT), jnp.zeros((rows, rest), FLOAT)
+    blank = jnp.zeros((rows, half), FLOAT)
+    stay = jnp.concatenate([cosine, cosine, ones], axis=1)
+    ahead = jnp.concatenate([-sine, blank, none], axis=1)
+    behind = jnp.concatenate([blank, sine, none], axis=1)
+    return [
+        jnp.concatenate([part] * (lanes // head_size), axis=1) for part in (stay, ahead, behind)
+    ]
+
+
+def wide_tables(refs, width):
+    return [jnp.concatenate([ref[...]] * (width // ref.shape[1]), axis=1) for ref in refs]
 
 
 def norm_unit(values):
@@ -91,116 +79,318 @@
     )
 
 
-def gelu_slope(values):
-    return (
-        0.5 * (1.0 + lax.erf(values * 0.7071067811865476))
-        + values * jnp.exp(-0.5 * values * values) * 0.3989422804014327
-    )
-
-
-def attention_scores(queries, keys, allowed, factor):
-    scores = jnp.einsum("bqhd,bkhd->bhqk", queries, keys, preferred_element_type=FLOAT) * factor
-    return jnp.where(allowed[:, None, :, :], scores, -1e30)
-
-
-def layer_forward(resid, in_full, out_full, parts, allowed, cosine, sine, factor):
-    rows, width = resid.shape
-    batches = allowed.shape[0]
-    seq = rows // batches
-    head_size = width // HEADS
-    rot = head_size // 4
-    unit, scale = norm_unit(resid)
-    input_one = (unit * parts[0] + parts[1]).astype(NARROW)
-    input_two = (unit * parts[2] + parts[3]).astype(NARROW)
-    triple = (
-        jnp.dot(input_one, in_full[:, : 3 * width], preferred_element_type=FLOAT) + parts[6]
-    ).reshape(rows, 3, HEADS, head_size)
-    shape = (batches, seq, HEADS, head_size)
-    queries = rotate(triple[:, 0], cosine, sine, rot).astype(NARROW).reshape(shape)
-    keys = rotate(triple[:, 1], cosine, sine, rot).astype(NARROW).reshape(shape)
-    values = triple[:, 2].astype(NARROW).reshape(shape)
-    scores = attention_scores(queries, keys, allowed, factor)
+def vector_spans(width, hidden):
+    amounts = [width] * 6 + [3 * width, width, hidden, width]
+    spans = []
+    begin = 0
+    for amount in amounts:
+        spans.append(slice(begin, begin + amount))
+        begin = begin + amount
+    return spans
+
+
+def masked_probs(queries, keys, mask, factor):
+    scores = lax.dot_general(queries, keys, LAST_CONTRACT, preferred_element_type=FLOAT) * factor
+    scores = jnp.where(mask, scores, -1e30)
     top = jnp.max(scores, axis=-1, keepdims=True)
     logsum = top + jnp.log(jnp.sum(jnp.exp(scores - top), axis=-1, keepdims=True))
-    probs = jnp.exp(scores - logsum).astype(NARROW)
-    mixed = (
-        jnp.einsum("bhqk,bkhd->bqhd", probs, values, preferred_element_type=FLOAT)
-        .astype(NARROW)
-        .reshape(rows, width)
-    )
-    pre_act = jnp.dot(input_two, in_full[:, 3 * width :], preferred_element_type=FLOAT) + parts[8]
-    activated = jax.nn.gelu(pre_act, approximate=False).astype(NARROW)
-    joined = jnp.concatenate([mixed, activated], axis=1)
-    result = resid + jnp.dot(joined, out_full, preferred_element_type=FLOAT) + parts[7] + parts[9]
-    kept = (input_one, input_two, unit, scale, queries, keys, values, logsum, pre_act, joined)
-    return (result, kept)
-
-
-def layer_backward(grad_out, in_full, out_full, parts, kept, allowed, cosine, sine, factor):
-    input_one, input_two, unit, scale, queries, keys, values, logsum, pre_act, joined = kept
-    rows, width = grad_out.shape
-    batches = allowed.shape[0]
+    return jnp.exp(scores - logsum)
+
+
+def slot_mask(line_ref, column_ref, b, seq):
+    later = lax.broadcasted_iota(jnp.int32, (seq, seq), 1)
+    place = lax.broadcasted_iota(jnp.int32, (seq, seq), 0)
+    return (column_ref[b] == line_ref[b]) & (later <= place)
+
+
+def layer_forward(resid, in_full, out_full, vector, tables, lines, columns):
+    rows, width = resid.shape
+    hidden = out_full.shape[0] - width
+    batches, _, seq = lines.shape
     head_size = width // HEADS
-    rot = head_size // 4
-    grad_low = grad_out.astype(NARROW)
-    out_grad = lax.dot_general(joined, grad_low, ROWS_CONTRACT, preferred_element_type=FLOAT)
-    joined_grad = lax.dot_general(grad_low, out_full, LAST_CONTRACT, preferred_element_type=FLOAT)
-    mixed_grad = joined_grad[:, :width].astype(NARROW).reshape(batches, -1, HEADS, head_size)
-    pre_grad = joined_grad[:, width:] * gelu_slope(pre_act)
-    pre_low = pre_grad.astype(NARROW)
-    probs = jnp.exp(attention_scores(queries, keys, allowed, factor) - logsum)
-    prob_grad = jnp.einsum("bqhd,bkhd->bhqk", mixed_grad, values, preferred_element_type=FLOAT)
-    value_grad = jnp.einsum(
-        "bhqk,bqhd->bkhd", probs.astype(NARROW), mixed_grad, preferred_element_type=FLOAT
-    )
-    score_grad = (
-        probs * (prob_grad - jnp.sum(probs * prob_grad, axis=-1, keepdims=True)) * factor
-    ).astype(NARROW)
-    flat = (rows, HEADS, head_size)
-    query_grad = rotate_back(
-        jnp.einsum("bhqk,bkhd->bqhd", score_grad, keys, preferred_element_type=FLOAT).reshape(flat),
-        cosine,
-        sine,
-        rot,
-    )
-    key_grad = rotate_back(
-        jnp.einsum("bhqk,bqhd->bkhd", score_grad, queries, preferred_element_type=FLOAT).reshape(
-            flat
-        ),
-        cosine,
-        sine,
-        rot,
-    )
-    qkv_grad = jnp.stack([query_grad, key_grad, value_grad.reshape(flat)], axis=1).reshape(
-        rows, 3 * width
-    )
-    qkv_low = qkv_grad.astype(NARROW)
-    in_grad = jnp.concatenate(
-        [
-            lax.dot_general(input_one, qkv_low, ROWS_CONTRACT, preferred_element_type=FLOAT),
-            lax.dot_general(input_two, pre_low, ROWS_CONTRACT, preferred_element_type=FLOAT),
+    half = head_size // 8
+    factor = 1.0 / math.sqrt(head_size)
+    spans = vector_spans(width, hidden)
+
+    def kernel(
+        resid_ref,
+        in_ref,
+        out_ref,
+        vector_ref,
+        stay_ref,
+        ahead_ref,
+        behind_ref,
+        line_ref,
+        column_ref,
+        final_ref,
+        qkv_ref,
+        pre_ref,
+        joined_ref,
+        last_ref,
+    ):
+        def part(i):
+            return vector_ref[:, spans[i]]
+
+        start = resid_ref[...]
+        unit, _ = norm_unit(start)
+        input_one = (unit * part(0) + part(1)).astype(NARROW)
+        input_two = (unit * part(2) + part(3)).astype(NARROW)
+        stay, ahead, behind = wide_tables((stay_ref, ahead_ref, behind_ref), width)
+        bias = part(6)
+        for i in range(3):
+            span = slice(i * width, (i + 1) * width)
+            values = jnp.dot(input_one, in_ref[:, span], preferred_element_type=FLOAT)
+            values = values + bias[:, span]
+            if i < 2:
+                values = (
+                    values * stay
+                    + pltpu.roll(values, width - half, 1) * ahead
+                    + pltpu.roll(values, half, 1) * behind
+                )
+            qkv_ref[:, span] = values.astype(NARROW)
+        for b in range(batches):
+            mask = slot_mask(line_ref, column_ref, b, seq)
+            there = slice(b * seq, (b + 1) * seq)
+            for head in range(HEADS):
+                first = head * head_size
+                queries, keys, values = [
+                    qkv_ref[there, i * width + first : i * width + first + head_size]
+                    for i in range(3)
+                ]
+                probs = masked_probs(queries, keys, mask, factor).astype(NARROW)
+                joined_ref[there, first : first + head_size] = jnp.dot(
+                    probs, values, preferred_element_type=FLOAT
+                ).astype(NARROW)
+        bias = part(8)
+        for i in range(hidden // width):
+            span = slice(i * width, (i + 1) * width)
+            pre = (
+                jnp.dot(
+                    input_two,
+                    in_ref[:, (3 + i) * width : (4 + i) * width],
+                    preferred_element_type=FLOAT,
+                )
+                + bias[:, span]
+            )
+            pre_ref[:, span] = pre
+            joined_ref[:, (1 + i) * width : (2 + i) * width] = (
+                0.5 * pre * (1.0 + lax.erf(pre * 0.7071067811865476))
+            ).astype(NARROW)
+        last = (
+            start
+            + jnp.dot(joined_ref[...], out_ref[...], preferred_element_type=FLOAT)
+            + part(7)
+            + part(9)
+        )
+        last_ref[...] = last
+        unit_last, _ = norm_unit(last)
+        final_ref[...] = (unit_last * part(4) + part(5)).astype(NARROW)
+
+    return pl.pallas_call(
+        kernel,
+        out_shape=[
+            jax.ShapeDtypeStruct((rows, width), NARROW),
+            jax.ShapeDtypeStruct((rows, 3 * width), NARROW),
+            jax.ShapeDtypeStruct((rows, hidden), FLOAT),
+            jax.ShapeDtypeStruct((rows, width + hidden), NARROW),
+            jax.ShapeDtypeStruct((rows, width), FLOAT),
         ],
-        axis=1,
-    )
-    back_one = lax.dot_general(
-        qkv_low, in_full[:, : 3 * width], LAST_CONTRACT, preferred_element_type=FLOAT
-    )
-    back_two = lax.dot_general(
-        pre_low, in_full[:, 3 * width :], LAST_CONTRACT, preferred_element_type=FLOAT
-    )
-    resid_grad = grad_out + norm_back(back_one * parts[0] + back_two * parts[2], unit, scale)
-    residual_bias = jnp.sum(grad_out, axis=0)
-    small = (
-        jnp.sum(back_one * unit, axis=0),
-        jnp.sum(back_one, axis=0),
-        jnp.sum(back_two * unit, axis=0),
-        jnp.sum(back_two, axis=0),
-        jnp.sum(qkv_grad, axis=0),
-        residual_bias,
-        jnp.sum(pre_grad, axis=0),
-        residual_bias,
-    )
-    return (resid_grad, in_grad, out_grad, small)
+        compiler_params=pltpu.CompilerParams(vmem_limit_bytes=VMEM_LIMIT),
+    )(resid, in_full, out_full, vector, *tables, lines, columns)
+
+
+def layer_backward(
+    final_grad, resid, in_full, out_full, vector, tables, lines, columns, kept, groups
+):
+    rows, width = resid.shape
+    hidden = out_full.shape[0] - width
+    batches, _, seq = lines.shape
+    head_size = width // HEADS
+    half = head_size // 8
+    factor = 1.0 / math.sqrt(head_size)
+    spans = vector_spans(width, hidden)
+    blocks = in_full.shape[1] // width
+    in_rows = width // groups
+    out_rows = out_full.shape[0] // groups
+    first_out = blocks * in_rows
+    shard = first_out + out_rows
+
+    def kernel(
+        final_grad_ref,
+        resid_ref,
+        in_ref,
+        out_ref,
+        vector_ref,
+        stay_ref,
+        ahead_ref,
+        behind_ref,
+        line_ref,
+        column_ref,
+        qkv_ref,
+        pre_ref,
+        joined_ref,
+        last_ref,
+        token_ref,
+        small_ref,
+        owners_ref,
+        owners,
+        low,
+        wide,
+        sems,
+    ):
+        def part(i):
+            return vector_ref[:, spans[i]]
+
+        def column_sum(i, values):
+            small_ref[:, spans[i]] = jnp.sum(values, axis=0, keepdims=True)
+
+        final_grad_in = final_grad_ref[...]
+        unit_last, scale_last = norm_unit(last_ref[...])
+        column_sum(4, final_grad_in * unit_last)
+        column_sum(5, final_grad_in)
+        grad_out = norm_back(final_grad_in * part(4), unit_last, scale_last)
+        column_sum(7, grad_out)
+        column_sum(9, grad_out)
+        grad_low = grad_out.astype(NARROW)
+        for c in range((width + hidden) // width):
+            there = slice(c * width, (c + 1) * width)
+            piece = lax.dot_general(
+                joined_ref[:, there], grad_low, ROWS_CONTRACT, preferred_element_type=FLOAT
+            )
+            at = c * width
+            while at < (c + 1) * width:
+                owner, row = at // out_rows, at % out_rows
+                size = min(out_rows - row, (c + 1) * width - at)
+                owners[owner, first_out + row : first_out + row + size, :] = piece[
+                    at - c * width : at - c * width + size
+                ]
+                at = at + size
+        out_copy = pltpu.make_async_copy(
+            owners.at[:, pl.ds(first_out, out_rows), :],
+            owners_ref.at[:, pl.ds(first_out, out_rows), :],
+            sems.at[0],
+        )
+        out_copy.start()
+        unit, scale = norm_unit(resid_ref[...])
+        input_one = (unit * part(0) + part(1)).astype(NARROW)
+        input_two = (unit * part(2) + part(3)).astype(NARROW)
+
+        def in_piece(inputs, c, grads):
+            piece = lax.dot_general(
+                inputs, grads, ROWS_CONTRACT, preferred_element_type=FLOAT
+            )
+            for owner in range(groups):
+                owners[owner, c * in_rows : (c + 1) * in_rows, :] = piece[
+                    owner * in_rows : (owner + 1) * in_rows
+                ]
+
+        back_two = jnp.zeros((rows, width), FLOAT)
+        bias_sums = []
+        for i in range(hidden // width):
+            grads = lax.dot_general(
+                grad_low,
+                out_ref[(1 + i) * width : (2 + i) * width, :],
+                LAST_CONTRACT,
+                preferred_element_type=FLOAT,
+            )
+            pre = pre_ref[:, i * width : (i + 1) * width]
+            slope = (
+                0.5 * (1.0 + lax.erf(pre * 0.7071067811865476))
+                + pre * jnp.exp(-0.5 * pre * pre) * 0.3989422804014327
+            )
+            grads = grads * slope
+            bias_sums.append(jnp.sum(grads, axis=0, keepdims=True))
+            grads = grads.astype(NARROW)
+            in_piece(input_two, 3 + i, grads)
+            back_two = back_two + lax.dot_general(
+                grads,
+                in_ref[:, (3 + i) * width : (4 + i) * width],
+                LAST_CONTRACT,
+                preferred_element_type=FLOAT,
+            )
+        small_ref[:, spans[8]] = jnp.concatenate(bias_sums, axis=1)
+        low[...] = lax.dot_general(
+            grad_low, out_ref[:width, :], LAST_CONTRACT, preferred_element_type=FLOAT
+        ).astype(NARROW)
+        for b in range(batches):
+            mask = slot_mask(line_ref, column_ref, b, seq)
+            there = slice(b * seq, (b + 1) * seq)
+            for head in range(HEADS):
+                first = head * head_size
+                at = [
+                    slice(i * width + first, i * width + first + head_size) for i in range(3)
+                ]
+                queries, keys, values = [qkv_ref[there, at[i]] for i in range(3)]
+                mixed = low[there, first : first + head_size]
+                probs = masked_probs(queries, keys, mask, factor)
+                back = lax.dot_general(
+                    mixed, values, LAST_CONTRACT, preferred_element_type=FLOAT
+                )
+                wide[there, at[2]] = lax.dot_general(
+                    probs.astype(NARROW), mixed, ROWS_CONTRACT, preferred_element_type=FLOAT
+                )
+                scores = (
+                    probs
+                    * (back - jnp.sum(probs * back, axis=-1, keepdims=True))
+                    * factor
+                ).astype(NARROW)
+                wide[there, at[0]] = jnp.dot(scores, keys, preferred_element_type=FLOAT)
+                wide[there, at[1]] = lax.dot_general(
+                    scores, queries, ROWS_CONTRACT, preferred_element_type=FLOAT
+                )
+        stay, ahead, behind = wide_tables((stay_ref, ahead_ref, behind_ref), width)
+        back_one = jnp.zeros((rows, width), FLOAT)
+        bias_sums = []
+        for i in range(3):
+            span = slice(i * width, (i + 1) * width)
+            grads = wide[:, span]
+            if i < 2:
+                grads = (
+                    grads * stay
+                    + pltpu.roll(grads * ahead, half, 1)
+                    + pltpu.roll(grads * behind, width - half, 1)
+                )
+            bias_sums.append(jnp.sum(grads, axis=0, keepdims=True))
+            grads = grads.astype(NARROW)
+            in_piece(input_one, i, grads)
+            back_one = back_one + lax.dot_general(
+                grads, in_ref[:, span], LAST_CONTRACT, preferred_element_type=FLOAT
+            )
+        in_copy = pltpu.make_async_copy(
+            owners.at[:, pl.ds(0, first_out), :],
+            owners_ref.at[:, pl.ds(0, first_out), :],
+            sems.at[1],
+        )
+        in_copy.start()
+        small_ref[:, spans[6]] = jnp.concatenate(bias_sums, axis=1)
+        column_sum(0, back_one * unit)
+        column_sum(1, back_one)
+        column_sum(2, back_two * unit)
+        column_sum(3, back_two)
+        token_ref[...] = (
+            grad_out + norm_back(back_one * part(0) + back_two * part(2), unit, scale)
+        ).astype(NARROW)
+        out_copy.wait()
+        in_copy.wait()
+
+    whole = pl.BlockSpec(memory_space=pltpu.VMEM)
+    return pl.pallas_call(
+        kernel,
+        in_specs=[whole] * 14,
+        out_specs=[whole, whole, pl.BlockSpec(memory_space=pl.ANY)],
+        out_shape=[
+            jax.ShapeDtypeStruct((rows, width), NARROW),
+            jax.ShapeDtypeStruct(vector.shape, FLOAT),
+            jax.ShapeDtypeStruct((groups, shard, width), FLOAT),
+        ],
+        scratch_shapes=[
+            pltpu.VMEM((groups, shard, width), FLOAT),
+            pltpu.VMEM((rows, width), NARROW),
+            pltpu.VMEM((rows, 3 * width), FLOAT),
+            pltpu.SemaphoreType.DMA((2,)),
+        ],
+        compiler_params=pltpu.CompilerParams(vmem_limit_bytes=VMEM_LIMIT),
+    )(final_grad, resid, in_full, out_full, vector, *tables, lines, columns, *kept)
 
 
 def block_rows(rows, cap):
@@ -499,6 +689,16 @@
         def lap(step, carry):
             j = lax.rem(step + 1, chips)
             there = chip_at(j) * 2
+
+            @pl.when(step == chips // 2)
+            def _():
+                for w in range(2):
+                    for c in range(1, chips):
+                        lane_wait(w, c)
+                        if split:
+                            for k in range(1, replicas):
+                                plane_copy(w, k, c).start()
+
             to_core[j] = look(there + 1 - core)
             part_copy(j).start()
             mine = look(there + core).astype(FLOAT)
@@ -517,12 +717,6 @@
             return carry
 
         lax.fori_loop(0, chips, lap, 0)
-        for w in range(2):
-            for j in range(1, chips):
-                lane_wait(w, j)
-                if split:
-                    for k in range(1, replicas):
-                        plane_copy(w, k, j).start()
         for j in range(1, chips):
             sum_copy(j).wait_recv()
             resid_ref[...] += from_lane[j].astype(FLOAT)
@@ -997,7 +1191,7 @@
 
 
 def head_table_grad(
-    table, hidden, logsum, weights, target, token_grad, slices, groups, replicas
+    table, hidden, logsum, weights, target, token_grad, slices, owner_grads, cut, groups, replicas
 ):
     vocab, width = table.shape
     amount = groups * replicas
@@ -1009,7 +1203,14 @@
     steps = vocab // block
     chips = groups // 2
     last = steps - 1
-    when_plane, when_core = min(1, last), min(3, last)
+    shard = owner_grads.shape[1]
+    regions = ((0, cut), (cut, shard - cut))
+    firsts, seconds = (replicas, chips), (chips, replicas)
+    reduce = all(count % (8 * replicas) == 0 for _, count in regions)
+    laps = steps * tiles
+
+    def when(part):
+        return min(int(laps * part), laps - 1)
 
     def kernel(
         table_ref,
@@ -1019,11 +1220,30 @@
         target_ref,
         own_ref,
         slices_ref,
+        owner_ref,
         grad_ref,
         square_ref,
         all_ref,
         summed_ref,
+        owned_out,
         gathered,
+        owned_ref,
+        from_core,
+        acc_in,
+        acc_out,
+        one_in,
+        one_out,
+        two_in,
+        two_out,
+        piece_sem,
+        half_send,
+        half_recv,
+        one_send,
+        one_recv,
+        two_send,
+        two_recv,
+        end_send,
+        end_recv,
         local_sem,
         slice_send,
         slice_recv,
@@ -1085,9 +1305,124 @@
             )
 
         local = pltpu.make_async_copy(own_ref, all_ref.at[me], local_sem)
-
-        @pl.when(step == 0)
-        def _():
+        accs, ones, twos = (acc_in, acc_out), (one_in, one_out), (two_in, two_out)
+
+        def chip_at(j):
+            return lax.rem(place.chip + j, chips)
+
+        def pieces(g):
+            first, rows = regions[g]
+            size = rows // replicas
+            for k in range(firsts[g]):
+                for i in range(seconds[g]):
+                    if g == 0:
+                        chip, replica = i, place.plane_replica(k)
+                    else:
+                        chip, replica = chip_at(k), i
+                    yield k, i, chip, pl.multiple_of(first + replica * size, 8), size
+
+        def piece_copy(g, k, i, chip, row, size):
+            return pltpu.make_async_copy(
+                owner_ref.at[chip * 2 + place.core, pl.ds(row, size), :],
+                accs[g].at[k, i],
+                piece_sem.at[g, k, i],
+            )
+
+        def half_copy(c):
+            return remote(
+                owner_ref.at[c * 2 + 1 - place.core],
+                from_core.at[c],
+                half_send.at[c],
+                half_recv.at[c],
+                place.sibling(),
+            )
+
+        def partner(over_dp, k):
+            if over_dp:
+                return place.plane(k)
+            return place.lane(k)
+
+        def one_copy(g, k):
+            return remote(
+                accs[g].at[k],
+                ones[g].at[k],
+                one_send.at[g, k],
+                one_recv.at[g, k],
+                partner(g == 0, k),
+            )
+
+        def mine(g):
+            return place.chip if g == 0 else place.replica
+
+        def two_copy(g, k):
+            return remote(
+                accs[g].at[0, lax.rem(mine(g) + k, seconds[g])],
+                twos[g].at[k],
+                two_send.at[g, k],
+                two_recv.at[g, k],
+                partner(g == 1, k),
+            )
+
+        def end_copy(g, k, there):
+            first, rows = regions[g]
+            size = rows // replicas
+            span = owned_ref.at[pl.ds(pl.multiple_of(first + there * size, 8), size), :]
+            return remote(span, span, end_send.at[g, k], end_recv.at[g, k], place.plane(k))
+
+        def begin_sums():
+            for c in range(chips):
+                half_copy(c).start()
+            for g in range(2):
+                for item in pieces(g):
+                    piece_copy(g, *item).start()
+
+        def begin_one():
+            for c in range(chips):
+                half_copy(c).wait_recv()
+            for g in range(2):
+                for item in pieces(g):
+                    piece_copy(g, *item).wait()
+                    k, i, chip, row, size = item
+                    accs[g][k, i] += from_core[chip, pl.ds(row, size), :]
+                for k in range(1, firsts[g]):
+                    one_copy(g, k).start()
+
+        def begin_two(g):
+            for k in range(1, firsts[g]):
+                one_copy(g, k).wait_recv()
+            for i in range(seconds[g]):
+                total = accs[g][0, i]
+                for k in range(1, firsts[g]):
+                    total = total + ones[g][k, i]
+                accs[g][0, i] = total
+            for k in range(1, seconds[g]):
+                two_copy(g, k).start()
+
+        def begin_end(g):
+            first, rows = regions[g]
+            size = rows // replicas
+            total = accs[g][0, mine(g)]
+            for k in range(1, seconds[g]):
+                two_copy(g, k).wait_recv()
+                total = total + twos[g][k]
+            row = pl.multiple_of(first + place.replica * size, 8)
+            owned_ref[pl.ds(row, size), :] = total
+            for k in range(1, replicas):
+                end_copy(g, k, place.replica).start()
+
+        def end_sums():
+            for g in range(2):
+                for k in range(1, replicas):
+                    end_copy(g, k, lax.rem(place.replica + replicas - k, replicas)).wait_recv()
+                    end_copy(g, k, place.replica).wait_send()
+                for k in range(1, firsts[g]):
+                    one_copy(g, k).wait_send()
+                for k in range(1, seconds[g]):
+                    two_copy(g, k).wait_send()
+            for c in range(chips):
+                half_copy(c).wait_send()
+
+        def begin_all():
             barrier = pltpu.get_barrier_semaphore()
 
             def greet(k, carry):
@@ -1102,6 +1437,8 @@
             lax.fori_loop(1, amount, greet, 0)
             pl.semaphore_wait(barrier, amount - 1)
             local.start()
+            if reduce:
+                begin_sums()
             for k in range(1, chips):
                 lane_copy(k).start()
 
@@ -1112,18 +1449,19 @@
             lax.fori_loop(1, amount, give, 0)
             gathered[me] = slices_ref[place.member]
 
-        @pl.when(step == when_plane)
-        def _():
+        def token_lane():
             local.wait()
             for k in range(1, chips):
                 lane_wait(k)
             for c in range(chips):
+                core_copy(place.replica, c).start()
+
+        def token_plane():
+            for c in range(chips):
                 for k in range(1, replicas):
                     plane_copy(k, c).start()
-                core_copy(place.replica, c).start()
-
-        @pl.when(step == when_core)
-        def _():
+
+        def token_core():
             for k in range(1, replicas):
                 for c in range(chips):
                     plane_wait(k, c)
@@ -1131,11 +1469,28 @@
                 for c in range(chips):
                     core_copy(place.plane_replica(k), c).start()
 
+        plan = [(0.0, begin_all)]
+        if reduce:
+            plan = plan + [
+                (0.09, begin_one),
+                (0.25, token_lane),
+                (0.4, lambda: begin_two(0)),
+                (0.4, token_plane),
+                (0.65, lambda: begin_two(1)),
+                (0.75, lambda: begin_end(0)),
+                (0.8, lambda: begin_end(1)),
+                (0.8, token_core),
+            ]
+        else:
+            plan = plan + [(0.17, token_lane), (0.17, token_plane), (0.5, token_core)]
+
         start = step * block
         part = table_ref[...].astype(NARROW)
         places = lax.broadcasted_iota(jnp.int32, (block, tile), 0)
 
         def lap(k, carry):
+            for part_of, act in plan:
+                pl.when(step * tiles + k == when(part_of))(act)
             here = hidden_ref[pl.ds(pl.multiple_of(k * tile, tile), tile), :]
             logits = lax.dot_general(part, here, LAST_CONTRACT, preferred_element_type=FLOAT)
             probs = jnp.exp(logits - logsum_ref[k])
@@ -1174,6 +1529,9 @@
                 return carry
 
             lax.fori_loop(1, amount, take, 0)
+            if reduce:
+                end_sums()
+                owned_out[...] = owned_ref[...]
             summed_ref[...] = jnp.sum(gathered[...], axis=0)
             for r in range(replicas):
                 for c in range(chips):
@@ -1195,11 +1553,12 @@
         grid=(steps,),
         in_specs=[pl.BlockSpec((block, width), lambda i: (i, 0))]
         + [whole] * 4
-        + [anywhere, whole],
+        + [anywhere, whole, anywhere],
         out_specs=[
             pl.BlockSpec((block, width), lambda i: (i, 0)),
             pl.BlockSpec((1, width), lambda i: (0, 0)),
             anywhere,
+            whole,
             whole,
         ],
         out_shape=[
@@ -1207,9 +1566,33 @@
             jax.ShapeDtypeStruct((1, width), FLOAT),
             jax.ShapeDtypeStruct((groups * replicas, own, width), NARROW),
             jax.ShapeDtypeStruct(slices.shape[1:], FLOAT),
+            jax.ShapeDtypeStruct(owner_grads.shape[1:] if reduce else (8, 128), FLOAT),
         ],
         scratch_shapes=[
             pltpu.VMEM((amount,) + slices.shape[1:], FLOAT),
+            pltpu.VMEM(owner_grads.shape[1:] if reduce else (8, 128), FLOAT),
+            pltpu.VMEM((chips,) + owner_grads.shape[1:] if reduce else (8, 128), FLOAT),
+        ]
+        + [
+            pltpu.VMEM(
+                (counts[g], seconds[g], regions[g][1] // replicas, width)[skip:]
+                if reduce
+                else (8, 128),
+                FLOAT,
+            )
+            for counts, skip in ((firsts, 0), (firsts, 0), (seconds, 1))
+            for g in range(2)
+        ]
+        + [
+            dma((2, max(firsts), max(seconds))),
+            dma((chips,)),
+            dma((chips,)),
+            dma((2, max(firsts))),
+            dma((2, max(firsts))),
+            dma((2, max(seconds))),
+            dma((2, max(seconds))),
+            dma((2, replicas)),
+            dma((2, replicas)),
             dma,
             dma((amount,)),
             dma((amount,)),
@@ -1236,6 +1619,7 @@
         target.reshape(shape),
         token_grad,
         slices,
+        owner_grads,
     )
 
 
@@ -1383,96 +1767,156 @@
     return (new_weight, new_moment, new_average)
 
 
-def table_update(table, grad, moment_low, moment, average, rate, clip):
-    vocab, width = table.shape
-    sub = moment.shape[0]
-    block = 512
-
-    def whole_kernel(clip_ref, table_ref, grad_ref, moment_ref, new_ref):
-        new_ref[...], _, _ = update_rule(
-            table_ref[...],
-            grad_ref[...],
-            moment_ref[...].astype(FLOAT),
-            table_ref[...],
-            rate,
-            clip_ref[0],
-        )
-
-    spec = pl.BlockSpec((block, width), lambda i: (i, 0))
-    scalar = pl.BlockSpec(memory_space=pltpu.SMEM)
-    new_table = pl.pallas_call(
-        whole_kernel,
-        grid=(-(-vocab // block),),
-        in_specs=[scalar, spec, spec, spec],
-        out_specs=spec,
-        out_shape=jax.ShapeDtypeStruct((vocab, width), FLOAT),
-        compiler_params=pltpu.CompilerParams(vmem_limit_bytes=VMEM_LIMIT),
-    )(clip, table, grad, moment_low)
-
+def update_all(scalars, tables, matrices, rates):
+    vocab, width = tables[0][0].shape
+    sub = tables[0][3].shape[0]
+    block = block_rows(vocab, 1100)
+    blocks = vocab // block
     window = max(-(-(sub + sub * r % 8) // 8) * 8 for r in range(vocab // sub))
     tile = 264
     tiles = -(-window // tile)
-
-    def own_kernel(
-        clip_ref, table_ref, grad_ref, moment_ref, average_ref, moment_out, average_out, *scratch
-    ):
-        table_win, grad_win, sems = scratch
+    steps = 2 * blocks + 2 * tiles
+    count = len(matrices)
+
+    def kernel(*refs):
+        refs = list(refs)
+
+        def take(amount):
+            taken = refs[:amount]
+            del refs[:amount]
+            return taken
+
+        (scalars_ref,) = take(1)
+        whole_in = [take(3) for _ in range(2)]
+        own_in = [take(4) for _ in range(2)]
+        small_in = [take(4) for _ in range(count)]
+        new_tables = take(2)
+        own_out = [take(2) for _ in range(2)]
+        small_out = [take(3) for _ in range(count)]
+        (factor_ref,) = take(1)
+        windows = take(2)
+        (sems,) = take(1)
         step = pl.program_id(0)
         begin = lax.axis_index("dp") * sub
         low = pl.multiple_of(begin // 8 * 8, 8)
         shift = begin - low
 
-        def fetch(t):
+        def fetch(w, t):
             first = t * tile
             size = min(tile, window - first)
             return [
                 pltpu.make_async_copy(
-                    source.at[pl.ds(low + first, size), :],
-                    win.at[pl.ds(first, size), :],
-                    sems.at[i, t],
+                    own_in[w][i].at[pl.ds(low + first, size), :],
+                    windows[i].at[pl.ds(first, size), :],
+                    sems.at[w, i, t],
                 )
-                for i, (source, win) in enumerate(((table_ref, table_win), (grad_ref, grad_win)))
+                for i in range(2)
             ]
 
-        for t in range(tiles):
-
-            @pl.when(step == t)
+        @pl.when(step == 0)
+        def _():
+            total = jnp.sum(scalars_ref[...], axis=0)
+            norm = jnp.sqrt(total)
+            factor_ref[...] = CLIP_LEVEL / jnp.maximum(norm, CLIP_LEVEL)
+
+        factor = factor_ref[1:2, 0:1]
+        for w in range(2):
+
+            @pl.when((step >= w * blocks) & (step < (w + 1) * blocks))
             def _():
-                if t == 0:
-                    for other in range(tiles):
-                        for copy in fetch(other):
-                            copy.start()
-                    for copy in fetch(0):
-                        copy.wait()
-                if t + 1 < tiles:
-                    for copy in fetch(t + 1):
-                        copy.wait()
-
-        first = pl.multiple_of(step * tile, 8)
-        amount = jnp.where(shift == 0, 0, tile + 8 - shift)
-        own_table = pltpu.roll(table_win[pl.ds(first, tile + 8), :], amount, 0)[:tile]
-        own_grad = pltpu.roll(grad_win[pl.ds(first, tile + 8), :], amount, 0)[:tile]
-        _, moment_out[...], average_out[...] = update_rule(
-            own_table, own_grad, moment_ref[...], average_ref[...], rate, clip_ref[0]
+                table_ref, grad_ref, moment_ref = whole_in[w]
+                table = table_ref[...]
+                new_tables[w][...], _, _ = update_rule(
+                    table, grad_ref[...], moment_ref[...].astype(FLOAT), table, rates[w], factor
+                )
+
+        @pl.when(step == 1)
+        def _():
+            for i in range(count):
+                weight, grad, moment, average = [ref[...] for ref in small_in[i]]
+                results = update_rule(weight, grad, moment, average, rates[2 + i], factor)
+                for ref, result in zip(small_out[i], results):
+                    ref[...] = result
+
+        for w in range(2):
+            base = 2 * blocks + w * tiles
+            for t in range(tiles):
+
+                @pl.when(step == (base - tiles + t + 1 if w else blocks))
+                def _():
+                    for copy in fetch(w, t):
+                        copy.start()
+
+            for t in range(tiles):
+
+                @pl.when(step == base + t)
+                def _():
+                    if t == 0:
+                        for copy in fetch(w, 0):
+                            copy.wait()
+                    if t + 1 < tiles:
+                        for copy in fetch(w, t + 1):
+                            copy.wait()
+
+            @pl.when((step >= base) & (step < base + tiles))
+            def _():
+                first = pl.multiple_of((step - base) * tile, 8)
+                amount = jnp.where(shift == 0, 0, tile + 8 - shift)
+                own_table, own_grad = [
+                    pltpu.roll(win[pl.ds(first, tile + 8), :], amount, 0)[:tile]
+                    for win in windows
+                ]
+                _, own_out[w][0][...], own_out[w][1][...] = update_rule(
+                    own_table, own_grad, own_in[w][2][...], own_in[w][3][...], rates[w], factor
+                )
+
+    whole = pl.BlockSpec(memory_space=pltpu.VMEM)
+    anywhere = pl.BlockSpec(memory_space=pl.ANY)
+
+    def table_spec(w):
+        return pl.BlockSpec(
+            (block, width), lambda i: (jnp.clip(i - w * blocks, 0, blocks - 1), 0)
         )
 
-    anywhere = pl.BlockSpec(memory_space=pl.ANY)
+    def own_spec(w):
+        return pl.BlockSpec(
+            (tile, width),
+            lambda i: (jnp.clip(i - 2 * blocks - w * tiles, 0, tiles - 1), 0),
+        )
+
     state = jax.ShapeDtypeStruct((sub, width), FLOAT)
-    piece = pl.BlockSpec((tile, width), lambda i: (i, 0))
-    new_moment, new_average = pl.pallas_call(
-        own_kernel,
-        grid=(tiles,),
-        in_specs=[scalar, anywhere, anywhere, piece, piece],
-        out_specs=[piece, piece],
-        out_shape=[state, state],
-        scratch_shapes=[
-            pltpu.VMEM((tiles * tile + 8, width), FLOAT),
-            pltpu.VMEM((tiles * tile + 8, width), FLOAT),
-            pltpu.SemaphoreType.DMA((2, tiles)),
-        ],
+    operands = [scalars]
+    in_specs = [whole]
+    for w in range(2):
+        operands += list(tables[w][:3])
+        in_specs += [table_spec(w)] * 3
+    for w in range(2):
+        operands += [tables[w][0], tables[w][1], tables[w][3], tables[w][4]]
+        in_specs += [anywhere, anywhere, own_spec(w), own_spec(w)]
+    for item in matrices:
+        operands += list(item)
+        in_specs += [whole] * 4
+    out_specs = [table_spec(0), table_spec(1)]
+    out_shape = [jax.ShapeDtypeStruct((vocab, width), FLOAT)] * 2
+    for w in range(2):
+        out_specs += [own_spec(w)] * 2
+        out_shape += [state] * 2
+    for item in matrices:
+        out_specs += [whole] * 3
+        out_shape += [jax.ShapeDtypeStruct(item[0].shape, FLOAT)] * 3
+    results = pl.pallas_call(
+        kernel,
+        grid=(steps,),
+        in_specs=in_specs,
+        out_specs=out_specs,
+        out_shape=out_shape,
+        scratch_shapes=[pltpu.VMEM((8, 128), FLOAT)]
+        + [pltpu.VMEM((tiles * tile + 8, width), FLOAT)] * 2
+        + [pltpu.SemaphoreType.DMA((2, 2, tiles))],
         compiler_params=pltpu.CompilerParams(vmem_limit_bytes=VMEM_LIMIT),
-    )(clip, table, grad, moment, average)
-    return new_table, new_moment, new_average
+    )(*operands)
+    tables_out = [(results[w], *results[2 + 2 * w : 4 + 2 * w]) for w in range(2)]
+    return tables_out, [results[6 + 3 * i : 9 + 3 * i] for i in range(count)]
 
 
 def shards(
@@ -1502,10 +1946,7 @@
     replica = lax.axis_index("dp")
     batches, _, seq = token_ids.shape
     vocab_rows, width = embed_table.shape
-    hidden = out_weights.shape[0] * groups - width
     head_size = width // HEADS
-    rot = head_size // 4
-    factor = 1.0 / math.sqrt(head_size)
     vocab_start = member * vocab_rows
     own_rows = batches * seq
     rows_all = groups * own_rows
@@ -1528,9 +1969,6 @@
         packed, line, in_weights, out_weights, embed_table, batches, groups, replicas
     )
     vector_full = lines.reshape(groups, -1)[:, :amount].reshape(-1).astype(NARROW)
-    embed_moment, head_moment, everyone = lax.optimization_barrier(
-        (embed_moment, head_moment, everyone)
-    )
     embed_moment_low = lax.all_gather(embed_moment.astype(NARROW), "dp", axis=0, tiled=True)
     head_moment_low = lax.all_gather(head_moment.astype(NARROW), "dp", axis=0, tiled=True)
     tokens_all = everyone[:, :batches]
@@ -1549,15 +1987,10 @@
     def group_part(values):
         return lax.dynamic_slice_in_dim(values, replica * rows_all, rows_all, 0)
 
-    parts = vector_parts(vector_full.astype(FLOAT), width, hidden)
-    places = jnp.arange(seq, dtype=jnp.int32)
-    allowed = (buffers[:, :, None] == buffers[:, None, :]) & (
-        places[None, None, :] <= places[None, :, None]
-    )
-    cosine, sine = rotary_tables(offset.reshape(-1), rot)
-    layer_out, kept = layer_forward(resid, in_full, out_full, parts, allowed, cosine, sine, factor)
-    unit_last, scale_last = norm_unit(layer_out)
-    final = (unit_last * parts[4] + parts[5]).astype(NARROW)
+    vector = vector_full.astype(FLOAT).reshape(1, -1)
+    tables = rotary_tables(offset.reshape(-1), head_size)
+    lines_of, columns_of = buffers[:, None, :], buffers[:, :, None]
+    final, *kept = layer_forward(resid, in_full, out_full, vector, tables, lines_of, columns_of)
     final_grad, logsum_all, loss_part, all_hidden = head_kernel(
         head_table, final, group_part(target_all), group_part(weight_all), groups, replicas
     )
@@ -1567,43 +2000,22 @@
     chunk = min(512, rows_all)
     lists = chunk_lists(local_all, inside_all, chunk)
 
-    layer_grad = norm_back(final_grad * parts[4], unit_last, scale_last)
-    resid_grad, in_grad, out_grad, small = layer_backward(
-        layer_grad, in_full, out_full, parts, kept, allowed, cosine, sine, factor
+    token_grad, vector_grad, owner_grads = layer_backward(
+        final_grad,
+        resid,
+        in_full,
+        out_full,
+        vector,
+        tables,
+        lines_of,
+        columns_of,
+        kept,
+        groups,
     )
-    vector_grad = jnp.concatenate(
-        [
-            small[0],
-            small[1],
-            small[2],
-            small[3],
-            jnp.sum(final_grad * unit_last, axis=0),
-            jnp.sum(final_grad, axis=0),
-            small[4],
-            small[5],
-            small[6],
-            small[7],
-        ]
-    )
-    token_grad, in_grad, out_grad, vector_grad, embed_moment_low, head_moment_low, lists = (
-        lax.optimization_barrier(
-            (
-                resid_grad.astype(NARROW),
-                in_grad,
-                out_grad,
-                vector_grad,
-                embed_moment_low,
-                head_moment_low,
-                lists,
-            )
-        )
-    )
-    parts_low = [
-        lax.psum_scatter(grad, "fsdp", scatter_dimension=0, tiled=True)
-        for grad in (in_grad, out_grad)
-    ]
     slices = jnp.pad(vector_grad.reshape(groups, amount), ((0, 0), (0, -amount % 1024)))
-    head_grad, head_square, token_grads, vector_sum = head_table_grad(
+    in_rows = in_weights.shape[0]
+    cut = owner_grads.shape[1] - out_weights.shape[0]
+    head_grad, head_square, token_grads, vector_sum, owned = head_table_grad(
         head_table,
         all_hidden,
         shifted,
@@ -1611,39 +2023,48 @@
         target_all,
         token_grad,
         slices.reshape(groups, -1, 128),
+        owner_grads,
+        cut,
         groups,
         replicas,
     )
-    parts_low, token_grads = lax.optimization_barrier((parts_low, token_grads))
-    layer_grads = list(lax.psum(parts_low, "dp")) + [vector_sum.reshape(-1)[:amount]]
+    if owned.shape != owner_grads.shape[1:]:
+        owned = lax.psum(lax.psum_scatter(owner_grads, "fsdp", scatter_dimension=0), "dp")
+    layer_grads = [
+        owned[:cut].reshape(-1, in_rows, width).transpose(1, 0, 2).reshape(in_rows, -1),
+        owned[cut:],
+        vector_sum.reshape(-1)[:amount],
+    ]
     embed_grad, embed_square = embed_table_grad(token_grads, *lists, vocab_rows)
     square = jnp.sum(embed_square) + jnp.sum(head_square)
     for grad in layer_grads:
         square = square + jnp.sum(grad * grad)
     line = jnp.stack([loss_part, square / replicas])[:, None]
     line = jnp.pad(jnp.broadcast_to(line, (2, 128)), ((0, 6), (0, 0)))
-    pair = jnp.sum(exchange_scalars(line, groups, replicas)[:, :2, 0], axis=0)
+    scalars = exchange_scalars(line, groups, replicas)
+    pair = jnp.sum(scalars[:, :2, 0], axis=0)
     loss = pair[0]
     grad_norm = jnp.sqrt(pair[1])
-    clip_factor = CLIP_LEVEL / jnp.maximum(grad_norm, CLIP_LEVEL)
-    clip = clip_factor.reshape(1)
     base = math.sqrt(NPARAM) / CLIP_LEVEL
     root = math.sqrt(width)
-    embed = table_update(
-        embed_table, embed_grad, embed_moment_low, embed_moment, embed_average, base, clip
+
+    def row(values):
+        return values.reshape(1, -1)
+
+    (embed, head), (inner, outer, vector) = update_all(
+        scalars,
+        [
+            (embed_table, embed_grad, embed_moment_low, embed_moment, embed_average),
+            (head_table, head_grad, head_moment_low, head_moment, head_average),
+        ],
+        [
+            (in_weights, layer_grads[0], in_moment, in_average),
+            (out_weights, layer_grads[1], out_moment, out_average),
+            tuple(map(row, (vectors, layer_grads[2], vector_moment, vector_average))),
+        ],
+        (base, base / root, base / root, base / root, 0.3 * base),
     )
-    head = table_update(
-        head_table, head_grad, head_moment_low, head_moment, head_average, base / root, clip
-    )
-    inner = update_rule(
-        in_weights, layer_grads[0], in_moment, in_average, base / root, clip_factor
-    )
-    outer = update_rule(
-        out_weights, layer_grads[1], out_moment, out_average, base / root, clip_factor
-    )
-    vector = update_rule(
-        vectors, layer_grads[2], vector_moment, vector_average, 0.3 * base, clip_factor
-    )
+    vector = [values.reshape(-1) for values in vector]
     return (*embed, *head, *inner, *outer, *vector, loss, grad_norm)
 
 

time: 600 us -> 538 us (0.90)
  waiting for transfers between devices: 60.1 us -> 0.06 us
  Pallas kernels: 397 us -> 456 us
  matrix products: 30.4 us -> 0.18 us
  other arithmetic: 50.1 us -> 29.1 us
  local copies, waits for them, and re-layouts: 34.9 us -> 22.7 us
    psum x1 -> x0, waiting for transfers between devices: 35.8 us -> none  [shards(): lax.psum(parts_low, 'dp')]
    pallas_call x4 -> x3, Pallas kernels: 57.5 us -> 90.3 us  [the longest x1 57.4 us: update_all(): pl.pallas_call(kernel, grid=(steps,), in_specs=in_specs, out_specs=out_sp...]
    dot_general x15 -> x0, matrix products: 30.2 us -> none  [the longest x1 8.13 us: layer_forward(): jnp.dot(input_two, in_full[:, 3 * width:], preferred_element_type=FLOAT)]
    pallas_call x1, Pallas kernels: 11.1 us -> 27.9 us  [exchange_scalars(): pl.pallas_call(kernel, in_specs=[whole], out_specs=whole, out_shape=jax.S...]
    reduce_scatter x2 -> x0, waiting for transfers between devices: 14 us -> none  [shards(): lax.psum_scatter(grad, 'fsdp', scatter_dimension=0, tiled=True)]
    optimization_barrier x2 -> x0, local copies, waits for them, and re-layouts: 10.7 us -> none  [shards(): lax.optimization_barrier((resid_grad.astype(NARROW), in_grad, out_grad, v...]
    all_gather x1, waiting for transfers between devices: 9.81 us -> 0.01 us  [shards(): lax.all_gather(head_moment.astype(NARROW), 'dp', axis=0, tiled=True)]
    pallas_call x1, Pallas kernels: 150 us -> 158 us  [head_table_grad(): pl.pallas_call(kernel, grid=(steps,), in_specs=[pl.BlockSpec((block, widt...]
  transfers between devices with their start and end apart: 5 -> 2, of which waited for: 3 -> 0; matrix products, arithmetic and copies ran while one was open for 14% -> 8% of each run, Pallas kernels for 44% -> 75%
where the time goes in v3:
time: 538 us; the launch traced here: 529 us
  Pallas kernels  456 us (85%)
  other arithmetic  29.1 us (5%)
  local copies, waits for them, and re-layouts  22.7 us (4%)
  between operations  20.5 us (4%)
    pallas_call x1, Pallas kernels, head_table_grad(): pl.pallas_call(kernel, grid=(steps,), in_specs=[pl.BlockSpec((block, widt...  158 us
    pallas_call x1, Pallas kernels, head_kernel(): pl.pallas_call(kernel, in_specs=[anywhere, whole, whole, whole], out_spec...  91.5 us
    pallas_call x1, Pallas kernels, start_kernel(): pl.pallas_call(kernel, in_specs=[whole, whole, whole, whole, anywhere], o...  69.1 us
    pallas_call x1, Pallas kernels, update_all(): pl.pallas_call(kernel, grid=(steps,), in_specs=in_specs, out_specs=out_sp...  57.4 us
    pallas_call x1, Pallas kernels, exchange_scalars(): pl.pallas_call(kernel, in_specs=[whole], out_specs=whole, out_shape=jax.S...  27.9 us
    pallas_call x1, Pallas kernels, layer_backward(): pl.pallas_call(kernel, in_specs=[whole] * 14, out_specs=[whole, whole, pl...  21.2 us
    pallas_call x1, Pallas kernels, embed_table_grad(): pl.pallas_call(kernel, grid_spec=pltpu.PrefetchScalarGridSpec(num_scalar_...  19.4 us
    unnamed x32, local copies, waits for them, and re-layouts  12.2 us
  transfers between devices with their start and end apart: 2, of which 0 were waited for; matrix products, arithmetic and copies ran while one was open for 8% of the time, Pallas kernels for 75%

profile of v3, /device:TPU:0, one launch (start us, length us, event | category | flops | bytes accessed | tf_op | source)
XLA Modules:
  0.0 528.6 jit_solution(18106230193439888532)
XLA Ops:
  7.2 0.0 all-gather.5.cloned.1.call-start
  7.2 3.4 convert_bitcast_fusion.1
  10.7 0.0 copy-start.11
  10.7 0.0 all-gather.5.cloned.1.call-update
  10.7 0.0 all-gather.7.cloned.1.call-start
  10.8 1.4 convert_bitcast_fusion
  12.1 0.0 all-gather.7.cloned.1.call-update
  12.2 0.1 slice_compare_fusion
  12.3 0.1 fusion.8
  12.3 0.1 fusion.5
  12.4 0.1 fusion.6
  12.5 0.1 select_reduce_fusion.3
  12.7 0.6 convert_reduce_fusion
  13.4 0.6 pad_bitcast_fusion.1.line_ref
  13.9 0.6 broadcast_in_dim.115
  14.6 0.1 pad.24.clone
  14.7 0.7 add_add_fusion.packed_ref
  15.3 69.1 %shard_map.314 = (s32[32,8,128]{2,1,0:T(8,128)}, f32[8,8,128]{2,1,0:T(8,128)}, bf16[8,64,3584]{2,1,0:T(8,128)(2,1)}, bf16[8,320,512]{2,1,0:T(8,128)(2,1)}, f32[256,512]{1,0:T(8,128)}) custom-call(s32[8,128]{1,0:T(8,128)} %add_add_fusion.packed_ref, f32[8,128]{1,0:T(8,128)} %pad_bitcast_fusion.1.line_ref, f32[64,3584]{1,0:T(8,128)} %refs_15_.1, ...), custom_call_target="tpu_custom_call" | custom-call | bytes 12877824 | tf_op jit(solution)/shard_map/pallas_call | solution.py:762
  84.4 1.0 slice.44
  85.4 1.6 slice_reduce_fusion.1
  87.0 0.8 convert_bitcast_fusion.2
  87.8 0.7 reshape.254.vector_ref
  88.5 0.1 select_reduce_fusion.2
  88.6 0.5 multiply_sine_fusion
  89.2 0.9 concatenate.27.ahead_ref
  90.1 0.9 concatenate.28.behind_ref
  91.0 0.8 copy.54.column_ref
  92.4 0.9 fusion.3
  93.4 1.6 fusion.4
  95.0 0.6 dynamic_slice.6
  95.6 0.6 dynamic_slice.7
  96.2 0.9 concatenate.26.stay_ref
  97.1 11.8 %shard_map.315 = (bf16[256,512]{1,0:T(8,128)(2,1)}, bf16[256,1536]{1,0:T(8,128)(2,1)}, f32[256,2048]{1,0:T(8,128)}, bf16[256,2560]{1,0:T(8,128)(2,1)}, f32[256,512]{1,0:T(8,128)}) custom-call(f32[256,512]{1,0:T(8,128)} %get-tuple-element.56.resid_ref, bf16[512,3584]{1,0:T(8,128)(2,1)} %bitcast.61, bf16[2560,512]{1,0:T(8,128)(2,1)} %bitcast.63, ...), custom_call_target="tpu_custom_call" | custom-call | tf_op jit(solution)/shard_map/pallas_call | solution.py:189
  108.9 91.5 %shard_map.316 = (f32[256,512]{1,0:T(8,128)}, f32[4,8,256]{2,1,0:T(8,128)}, f32[1,256]{1,0:T(1,128)}, bf16[32,256,512]{2,1,0:T(8,128)(2,1)}) custom-call(f32[6288,512]{1,0:T(8,128)} %refs_11_.1, bf16[256,512]{1,0:T(8,128)(2,1)} %get-tuple-element.60.own_ref, s32[8,1,256]{2,1,0:T(1,128)} %bitcast.84, f32[8,1,256]{2,1,0:T(1,128)} %bitcast.85), custom_call_target="tpu_custom_call" | custom-call | flops 26373783552 | bytes 12877824 | tf_op jit(solution)/shard_map/pallas_call | solution.py:1134
  200.4 21.2 %shard_map.317 = (bf16[256,512]{1,0:T(8,128)(2,1)}, f32[1,7680]{1,0:T(1,128)}, f32[8,768,512]{2,1,0:T(8,128)}) custom-call(f32[256,512]{1,0:T(8,128)} %get-tuple-element.65.final_grad_ref, f32[256,512]{1,0:T(8,128)} %get-tuple-element.56.resid_ref, bf16[512,3584]{1,0:T(8,128)(2,1)} %bitcast.62, bf16[2560,512]{1,0:T(8,128)(2,1)} %bitcast.64, ...), custom_call_target="tpu_custom_call" | custom-call | tf_op jit(solution)/shard_map/pallas_call | solution.py:377
  221.5 0.8 reduce.5
  222.4 0.1 reshape.241
  222.4 0.6 copy.65
  223.2 0.2 convolution_convert_fusion
  223.3 6.7 %select_reduce_fusion = (s32[16,512]{1,0:T(8,128)S(1)}, s32[16,512]{1,0:T(8,128)S(1)}) fusion(s32[16,512]{1,0:T(8,128)S(1)} %sub.65, s32[16,512]{1,0:T(8,128)S(1)} %convolution_convert_fusion, pred[16,512]{1,0:T(8,128)(4,1)S(1)} %compare_and_fusion), kind=kLoop, calls=%fused_computation | loop fusion | flops 25149440 | bytes 139264 | tf_op jit(solution)/shard_map/reduce_sum | solution.py:1691
  230.0 0.6 reshape.236.place_ref
  230.6 0.6 reshape.237.row_ref
  231.3 0.1 reduce_sum.159
  231.3 0.6 reduce_sum.160.count_ref
  232.0 0.7 compare_select_fusion.logsum_ref
  232.7 157.7 %shard_map.318 = (f32[6288,512]{1,0:T(8,128)}, f32[1,512]{1,0:T(1,128)}, bf16[32,256,512]{2,1,0:T(8,128)(2,1)}, f32[8,128]{1,0:T(8,128)}, f32[768,512]{1,0:T(8,128)}) custom-call(f32[6288,512]{1,0:T(8,128)} %refs_11_.1, bf16[8192,512]{1,0:T(8,128)(2,1)} %bitcast.95, f32[4,1,2048]{2,1,0:T(1,128)} %compare_select_fusion.logsum_ref, f32[4,1,2048]{2,1,0:T(1,128)} %bitcast.71, ...), custom_call_target="tpu_custom_call" | custom-call | flops 105495134208 | bytes 42532864 | tf_op jit(solution)/shard_map/pallas_call | solution.py:1551
  390.5 19.4 %shard_map.319 = (f32[6288,512]{1,0:T(8,128)}, f32[1,512]{1,0:T(1,128)}) custom-call(s32[16]{0:T(128)} %reduce_sum.160.count_ref, s32[16,1,512]{2,1,0:T(1,128)} %reshape.236.place_ref, s32[16,1,512]{2,1,0:T(1,128)} %reshape.237.row_ref, bf16[8192,512]{1,0:T(8,128)(2,1)} %bitcast.65), custom_call_target="tpu_custom_call" | custom-call | tf_op jit(solution)/shard_map/pallas_call | solution.py:1733
  409.9 1.3 reduce_sum.163
  411.2 0.6 reduce_sum.164
  411.8 0.1 slice.48
  411.9 0.6 reduce_sum.157
  413.8 1.1 fusion.1
  415.6 1.6 fusion.10
  417.8 1.2 fusion.11
  419.7 0.7 fusion.9
  420.4 0.7 pad.19.own_ref
  421.0 27.9 %shard_map.320.refs_0_ = f32[32,8,128]{2,1,0:T(8,128)} custom-call(f32[8,128]{1,0:T(8,128)} %pad.19.own_ref), custom_call_target="tpu_custom_call" | custom-call | tf_op jit(solution)/shard_map/pallas_call | solution.py:1673
  449.0 1.0 copy.60
  450.0 1.1 slice_reduce_fusion
  451.0 0.6 fusion.12
  452.3 0.0 all-gather.5.cloned.1.call-done
  452.3 5.3 reshape.256.refs_3_
  457.6 5.2 reshape.258.refs_6_
  462.9 57.4 %shard_map.321 = (f32[6288,512]{1,0:T(8,128)}, f32[6288,512]{1,0:T(8,128)}, f32[1572,512]{1,0:T(8,128)}, f32[1572,512]{1,0:T(8,128)}, f32[1572,512]{1,0:T(8,128)...) custom-call(f32[32,8,128]{2,1,0:T(8,128)} %shard_map.320.refs_0_, ...), custom_call_target="tpu_custom_call" | custom-call | tf_op jit(solution)/shard_map/pallas_call | solution.py:1907
  (40 shorter events, 0.2 us)
Async XLA Ops:
  7.2 3.6 copy-start
  7.2 445.1 %all-gather.5.cloned.1.call-start = ((), (), s32[]{:S(2)}) async-start(), calls=%async_computation | async-start | bytes 8069120 | tf_op jit(solution)/shard_map/all_gather | solution.py:1972
  10.7 1.5 copy-start.3
  10.7 1.6 copy-start.9
  10.7 1.6 copy-start.12
  10.7 2.7 copy-start.6
  10.7 4.0 copy-start.11
  10.7 446.9 %all-gather.7.cloned.1.call-start = ((), (), s32[]{:S(2)}) async-start(), calls=%async_computation.1 | async-start | bytes 8069120 | tf_op jit(solution)/shard_map/all_gather | solution.py:1973
  93.4 138.6 %copy-start.2 = (f32[32,2,128]{2,1,0:T(2,128)}, f32[32,2,128]{2,1,0:T(2,128)S(1)}, u32[]{:S(2)}) copy-start(f32[32,2,128]{2,1,0:T(2,128)S(1)} %fusion.3) | copy-start | bytes 98308
  94.9 13.9 %copy-start.4 = (s32[32,2,128]{2,1,0:T(2,128)}, s32[32,2,128]{2,1,0:T(2,128)S(1)}, u32[]{:S(2)}) copy-start(s32[32,2,128]{2,1,0:T(2,128)S(1)} %get-tuple-element.108) | copy-start | bytes 98308
  200.3 22.7 %copy-start.5 = (f32[4,8,256]{2,1,0:T(8,128)S(1)}, f32[4,8,256]{2,1,0:T(8,128)}, u32[]{:S(2)}) copy-start(f32[4,8,256]{2,1,0:T(8,128)} %get-tuple-element.64) | copy-start | bytes 98308
  390.4 20.8 %copy-start.8 = (f32[1,512]{1,0:T(1,128)S(1)}, f32[1,512]{1,0:T(1,128)}, u32[]{:S(2)}) copy-start(f32[1,512]{1,0:T(1,128)} %get-tuple-element.75) | copy-start | bytes 6148
  390.4 21.4 %copy-start.1 = (f32[768,512]{1,0:T(8,128)S(1)}, f32[768,512]{1,0:T(8,128)}, u32[]{:S(2)}) copy-start(f32[768,512]{1,0:T(8,128)} %get-tuple-element.76) | copy-start | bytes 4718596
  390.4 21.4 %copy-start.10 = (f32[1,256]{1,0:T(1,128)S(1)}, f32[1,256]{1,0:T(1,128)}, u32[]{:S(2)}) copy-start(f32[1,256]{1,0:T(1,128)} %get-tuple-element.62) | copy-start | bytes 3076
  390.5 27.3 %copy-start.7 = (f32[8,128]{1,0:T(8,128)S(1)}, f32[8,128]{1,0:T(8,128)}, u32[]{:S(2)}) copy-start(f32[8,128]{1,0:T(8,128)} %get-tuple-element.77) | copy-start | bytes 12292
Sparse Core Ops, SparseCore 0:
  10.8 93.3 all-gather.4
  106.7 107.4 all-gather.6

commit v4 on v3

--- a/solution.py
+++ b/solution.py
@@ -458,7 +458,9 @@
     )
 
 
-def start_kernel(packed, line, in_shard, out_shard, table, batches, groups, replicas):
+def start_kernel(
+    packed, line, in_shard, out_shard, table, head, batches, groups, replicas
+):
     vocab, width = table.shape
     seq = packed.shape[1]
     own = batches * seq
@@ -475,11 +477,13 @@
         in_ref,
         out_ref,
         table_ref,
+        head_ref,
         every_ref,
         lines_ref,
         in_full,
         out_full,
         resid_ref,
+        aims_ref,
         in_low,
         out_low,
         wide,
@@ -670,13 +674,14 @@
         fetch.wait()
         start = member * vocab
 
-        def look(slot):
+        def look(slot, ahead):
             for b in range(batches):
 
                 def lap(i, carry):
                     for u in range(unroll):
                         spot = i * unroll + u
-                        row = ids[slot, b, spot] - start
+                        token = ids[slot, b, jnp.minimum(spot + ahead, seq - 1)]
+                        row = jnp.where(spot + ahead < seq, token, 0) - start
                         inside = (row >= 0) & (row < vocab)
                         safe = jnp.where(inside, row, 0)
                         keep = jnp.where(inside, 1.0, 0.0)
@@ -699,9 +704,9 @@
                             for k in range(1, replicas):
                                 plane_copy(w, k, c).start()
 
-            to_core[j] = look(there + 1 - core)
+            to_core[j] = look(there + 1 - core, 0)
             part_copy(j).start()
-            mine = look(there + core).astype(FLOAT)
+            mine = look(there + core, 0).astype(FLOAT)
             part_copy(j).wait_recv()
             mine = mine + from_core[j].astype(FLOAT)
 
@@ -717,6 +722,15 @@
             return carry
 
         lax.fori_loop(0, chips, lap, 0)
+        again = pltpu.make_async_copy(head_ref, wide, table_sem)
+        again.start()
+        again.wait()
+
+        def aim(slot, carry):
+            aims_ref[slot] = look(slot, 1)
+            return carry
+
+        lax.fori_loop(0, groups, aim, 0)
         for j in range(1, chips):
             sum_copy(j).wait_recv()
             resid_ref[...] += from_lane[j].astype(FLOAT)
@@ -759,16 +773,17 @@
     anywhere = pl.BlockSpec(memory_space=pl.ANY)
     dma = pltpu.SemaphoreType.DMA
     vmem = pltpu.VMEM
-    every, lines, in_full, out_full, resid = pl.pallas_call(
+    every, lines, in_full, out_full, resid, aims = pl.pallas_call(
         kernel,
-        in_specs=[whole, whole, whole, whole, anywhere],
-        out_specs=[whole, whole, anywhere, anywhere, whole],
+        in_specs=[whole, whole, whole, whole, anywhere, anywhere],
+        out_specs=[whole, whole, anywhere, anywhere, whole, whole],
         out_shape=[
             jax.ShapeDtypeStruct((amount,) + packed.shape, jnp.int32),
             jax.ShapeDtypeStruct((groups,) + line.shape, FLOAT),
             jax.ShapeDtypeStruct((groups,) + in_shard.shape, NARROW),
             jax.ShapeDtypeStruct((groups,) + out_shard.shape, NARROW),
             jax.ShapeDtypeStruct((own, width), FLOAT),
+            jax.ShapeDtypeStruct((groups, own, width), NARROW),
         ],
         scratch_shapes=[
             vmem(in_shard.shape, NARROW),
@@ -804,17 +819,18 @@
         cost_estimate=pl.CostEstimate(
             flops=0, bytes_accessed=vocab * width * 4, transcendentals=0
         ),
-    )(packed, line, in_shard, out_shard, table)
+    )(packed, line, in_shard, out_shard, table, head)
     return (
         every,
         lines,
         in_full.reshape(-1, in_shard.shape[1]),
         out_full.reshape(-1, out_shard.shape[1]),
         resid,
+        aims,
     )
 
 
-def head_kernel(table, own_hidden, target, weight, groups, replicas):
+def head_kernel(table, own_hidden, aims, target, weight, groups, replicas):
     vocab, width = table.shape
     own = own_hidden.shape[0]
     block = block_rows(vocab, 1100)
@@ -825,6 +841,7 @@
     def kernel(
         table_ref,
         own_ref,
+        aims_ref,
         target_ref,
         weight_ref,
         grad_ref,
@@ -837,12 +854,14 @@
         exps,
         tops,
         totals,
-        hits,
         shares,
         to_core,
         from_core,
         to_lane,
         from_lane,
+        aim_core,
+        aim_lane,
+        aim_from,
         table_sem,
         local_sem,
         lane_send,
@@ -861,6 +880,10 @@
         part_recv,
         sum_send,
         sum_recv,
+        aim_half_send,
+        aim_half_recv,
+        aim_send,
+        aim_recv,
     ):
         place = Place(groups, replicas)
         me = place.member
@@ -968,6 +991,20 @@
         def sum_copy(j):
             return remote(
                 to_lane.at[j], from_lane.at[j], sum_send.at[j], sum_recv.at[j], lane_device(j)
+            )
+
+        def aim_half(c):
+            return remote(
+                aims_ref.at[c * 2 + 1 - core],
+                aim_core.at[c],
+                aim_half_send.at[c],
+                aim_half_recv.at[c],
+                place.sibling(),
+            )
+
+        def aim_copy(j):
+            return remote(
+                aim_lane.at[j], aim_from.at[j], aim_send.at[j], aim_recv.at[j], lane_device(j)
             )
 
         table_copy(0).start()
@@ -983,6 +1020,8 @@
         hid[me] = own_ref[...]
         for k in range(1, replicas):
             plane_copy(k, 0).start()
+        for c in range(chips):
+            aim_half(c).start()
         for b in range(blocks):
             table_copy(b).wait()
             low[b] = wide[b % 2].astype(NARROW)
@@ -1017,10 +1056,20 @@
             def _():
                 core_wait(j)
 
+            @pl.when(step == groups // 2 + 1)
+            def _():
+                for c in range(chips):
+                    aim_half(c).wait_recv()
+                for i in range(chips):
+                    chip = chip_at(i)
+                    aim_lane[i] = (
+                        aims_ref[chip * 2 + core].astype(FLOAT) + aim_core[chip].astype(FLOAT)
+                    ).astype(NARROW)
+                for i in range(1, chips):
+                    aim_copy(i).start()
+
             member = chip_before(j) * 2 + lax.rem(core + other, 2)
             here = hid[member]
-            wanted = target_ref[member]
-            hit = jnp.zeros((1, own), FLOAT)
             for b in range(blocks):
                 logits = lax.dot_general(
                     low[b], here, LAST_CONTRACT, preferred_element_type=FLOAT
@@ -1029,11 +1078,7 @@
                 values = jnp.exp(logits - top)
                 tops[member, b : b + 1, :] = top
                 totals[member, b : b + 1, :] = jnp.sum(values, axis=0, keepdims=True)
-                hit = hit + jnp.sum(
-                    jnp.where(spots == wanted - b * block, logits, 0.0), axis=0, keepdims=True
-                )
                 exps[b, member] = values.astype(NARROW)
-            hits[pl.ds(member, 1), :] = hit
             block_tops = tops[member, :blocks, :]
             top = jnp.max(block_tops, axis=0, keepdims=True)
             total = jnp.sum(
@@ -1065,7 +1110,7 @@
             for b in range(blocks):
                 scale = weights * jnp.exp(tops[member, b : b + 1, :] - logsum)
                 grads = exps[b, member].astype(FLOAT) * scale
-                grads = jnp.where(spots == wanted - b * block, grads - weights, grads)
+                grads = jnp.where(spots == wanted - b * block, 0.0, grads)
                 total = total + lax.dot_general(
                     grads.astype(NARROW), low[b], ROWS_CONTRACT, preferred_element_type=FLOAT
                 )
@@ -1084,15 +1129,15 @@
                         pass_copy(k, c).start()
 
             there = chip_at(j) * 2
-            to_core[j] = member_back(there + 1 - core)
+            to_core[j] = member_back(there + 1 - core).astype(NARROW)
             part_copy(j).start()
             mine = member_back(there + core)
             part_copy(j).wait_recv()
-            mine = mine + from_core[j]
+            mine = mine + from_core[j].astype(FLOAT)
 
             @pl.when(j > 0)
             def _():
-                to_lane[j] = mine
+                to_lane[j] = mine.astype(NARROW)
                 sum_copy(j).start()
 
             @pl.when(j == 0)
@@ -1104,11 +1149,24 @@
         lax.fori_loop(0, chips, backward, 0)
         held = lax.broadcasted_iota(jnp.int32, (groups, own), 0) == me
         amounts = jnp.concatenate([weight_ref[m] for m in range(groups)], axis=0)
-        losses = amounts * (jnp.where(held, logsum_ref[place.replica], 0.0) - hits[...])
-        loss_ref[...] = jnp.sum(losses, axis=0, keepdims=True)
+
+        def own_column(values):
+            return jnp.sum(jnp.where(held, values, 0.0).T, axis=1, keepdims=True)
+
+        amount = own_column(amounts)
+        logsum = own_column(logsum_ref[place.replica])
+        aimed = aim_lane[0].astype(FLOAT)
+        for j in range(1, chips):
+            aim_copy(j).wait_recv()
+            aimed = aimed + aim_from[j].astype(FLOAT)
+        hit = jnp.sum(own_ref[...].astype(FLOAT) * aimed, axis=1, keepdims=True)
+        loss_ref[...] = amount * (logsum - hit)
+        part = (amount * (jnp.exp(hit - logsum) - 1.0)).astype(NARROW).astype(FLOAT)
+        total = grad_ref[...] + part * aimed
         for j in range(1, chips):
             sum_copy(j).wait_recv()
-            grad_ref[...] += from_lane[j]
+            total = total + from_lane[j].astype(FLOAT)
+        grad_ref[...] = total
         local.wait()
         own_core.wait_send()
         for k in range(1, groups):
@@ -1122,10 +1180,12 @@
                 pass_copy(k, j).wait_send()
         for j in range(chips):
             part_copy(j).wait_send()
+            aim_half(j).wait_send()
             if j > 0:
                 lane_copy(j).wait_send()
                 core_copy(j).wait_send()
                 sum_copy(j).wait_send()
+                aim_copy(j).wait_send()
 
     whole = pl.BlockSpec(memory_space=pltpu.VMEM)
     anywhere = pl.BlockSpec(memory_space=pl.ANY)
@@ -1133,12 +1193,12 @@
     vmem = pltpu.VMEM
     grad, logsum, loss, everyone = pl.pallas_call(
         kernel,
-        in_specs=[anywhere, whole, whole, whole],
+        in_specs=[anywhere, whole, whole, whole, whole],
         out_specs=[whole, whole, whole, anywhere],
         out_shape=[
             jax.ShapeDtypeStruct((own, width), FLOAT),
             jax.ShapeDtypeStruct((replicas, groups, own), FLOAT),
-            jax.ShapeDtypeStruct((1, own), FLOAT),
+            jax.ShapeDtypeStruct((own, 1), FLOAT),
             jax.ShapeDtypeStruct((replicas * groups, own, width), NARROW),
         ],
         scratch_shapes=[
@@ -1148,12 +1208,14 @@
             vmem((blocks, groups, block, own), NARROW),
             vmem((groups, lines, own), FLOAT),
             vmem((groups, lines, own), FLOAT),
-            vmem((groups, own), FLOAT),
             vmem((groups, groups, own), FLOAT),
-            vmem((chips, own, width), FLOAT),
-            vmem((chips, own, width), FLOAT),
-            vmem((chips, own, width), FLOAT),
-            vmem((chips, own, width), FLOAT),
+            vmem((chips, own, width), NARROW),
+            vmem((chips, own, width), NARROW),
+            vmem((chips, own, width), NARROW),
+            vmem((chips, own, width), NARROW),
+            vmem((chips, own, width), NARROW),
+            vmem((chips, own, width), NARROW),
+            vmem((chips, own, width), NARROW),
             dma((2,)),
             dma,
             dma((chips,)),
@@ -1172,9 +1234,13 @@
             dma((chips,)),
             dma((chips,)),
             dma((chips,)),
+            dma((chips,)),
+            dma((chips,)),
+            dma((chips,)),
+            dma((chips,)),
         ],
         compiler_params=pltpu.CompilerParams(
-            vmem_limit_bytes=VMEM_LIMIT, collective_id=3, has_side_effects=True
+            vmem_limit_bytes=VMEM_LIMIT + 2**21, collective_id=3, has_side_effects=True
         ),
         cost_estimate=pl.CostEstimate(
             flops=4 * vocab * groups * own * width,
@@ -1184,6 +1250,7 @@
     )(
         table,
         own_hidden,
+        aims,
         target.reshape(groups, 1, own),
         weight.reshape(groups, 1, own),
     )
@@ -1965,8 +2032,16 @@
     )
     amount = vectors.shape[0]
     line = jnp.pad(vectors, (0, -amount % 1024)).reshape(-1, 128)
-    everyone, lines, in_full, out_full, resid = start_kernel(
-        packed, line, in_weights, out_weights, embed_table, batches, groups, replicas
+    everyone, lines, in_full, out_full, resid, aims = start_kernel(
+        packed,
+        line,
+        in_weights,
+        out_weights,
+        embed_table,
+        head_table,
+        batches,
+        groups,
+        replicas,
     )
     vector_full = lines.reshape(groups, -1)[:, :amount].reshape(-1).astype(NARROW)
     embed_moment_low = lax.all_gather(embed_moment.astype(NARROW), "dp", axis=0, tiled=True)
@@ -1992,7 +2067,7 @@
     lines_of, columns_of = buffers[:, None, :], buffers[:, :, None]
     final, *kept = layer_forward(resid, in_full, out_full, vector, tables, lines_of, columns_of)
     final_grad, logsum_all, loss_part, all_hidden = head_kernel(
-        head_table, final, group_part(target_all), group_part(weight_all), groups, replicas
+        head_table, final, aims, group_part(target_all), group_part(weight_all), groups, replicas
     )
 
     less_weight = logsum_all - jnp.log(jnp.maximum(weight_all, 1e-30))

time: 538 us -> 534 us (level)
  no operation moved by 1% of the time
where the time goes in v4:
time: 534 us; the launch traced here: 526 us
  Pallas kernels  454 us (85%)
  other arithmetic  29.1 us (5%)
  local copies, waits for them, and re-layouts  22.7 us (4%)
  between operations  20.3 us (4%)
    pallas_call x1, Pallas kernels, head_table_grad(): pl.pallas_call(kernel, grid=(steps,), in_specs=[pl.BlockSpec((block, widt...  155 us
    pallas_call x1, Pallas kernels, head_kernel(): pl.pallas_call(kernel, in_specs=[anywhere, whole, whole, whole, whole], o...  82.3 us
    pallas_call x1, Pallas kernels, start_kernel(): pl.pallas_call(kernel, in_specs=[whole, whole, whole, whole, anywhere, an...  79.7 us
    pallas_call x1, Pallas kernels, update_all(): pl.pallas_call(kernel, grid=(steps,), in_specs=in_specs, out_specs=out_sp...  57.6 us
    pallas_call x1, Pallas kernels, exchange_scalars(): pl.pallas_call(kernel, in_specs=[whole], out_specs=whole, out_shape=jax.S...  26.2 us
    pallas_call x1, Pallas kernels, layer_backward(): pl.pallas_call(kernel, in_specs=[whole] * 14, out_specs=[whole, whole, pl...  21.2 us
    pallas_call x1, Pallas kernels, embed_table_grad(): pl.pallas_call(kernel, grid_spec=pltpu.PrefetchScalarGridSpec(num_scalar_...  19.9 us
    unnamed x32, local copies, waits for them, and re-layouts  12.2 us
  transfers between devices with their start and end apart: 2, of which 0 were waited for; matrix products, arithmetic and copies ran while one was open for 8% of the time, Pallas kernels for 75%

profile of v4, /device:TPU:0, one launch (start us, length us, event | category | flops | bytes accessed | tf_op | source)
XLA Modules:
  0.0 526.0 jit_solution(846222346214313544)
XLA Ops:
  7.2 0.0 copy-start
  7.2 0.0 all-gather.5.cloned.1.call-start
  7.2 3.4 convert_bitcast_fusion.1
  10.7 0.0 all-gather.5.cloned.1.call-update
  10.7 0.0 all-gather.7.cloned.1.call-start
  10.8 1.4 convert_bitcast_fusion
  12.1 0.0 all-gather.7.cloned.1.call-update
  12.2 0.1 slice_compare_fusion
  12.3 0.1 fusion.8
  12.3 0.1 fusion.5
  12.4 0.1 fusion.6
  12.5 0.1 select_reduce_fusion.3
  12.7 0.6 convert_reduce_fusion
  13.4 0.6 pad_bitcast_fusion.1.line_ref
  13.9 0.6 broadcast_in_dim.115
  14.6 0.1 pad.24.clone
  14.7 0.7 add_add_fusion.packed_ref
  15.3 79.7 %shard_map.314 = (s32[32,8,128]{2,1,0:T(8,128)}, f32[8,8,128]{2,1,0:T(8,128)}, bf16[8,64,3584]{2,1,0:T(8,128)(2,1)}, bf16[8,320,512]{2,1,0:T(8,128)(2,1)}, f32[2...) custom-call(s32[8,128]{1,0:T(8,128)} %add_add_fusion.packed_ref, f32[8,128]{1,0:T(8,128)} %pad_bitcast_fusion.1.line_ref, ...), custom_call_target="tpu_custom_call" | custom-call | bytes 12877824 | tf_op jit(solution)/shard_map/pallas_call | solution.py:776
  95.0 1.0 slice.44
  96.0 1.6 slice_reduce_fusion.1
  97.6 0.8 convert_bitcast_fusion.2
  98.4 0.7 reshape.254.vector_ref
  99.1 0.1 select_reduce_fusion.2
  99.2 0.5 multiply_sine_fusion
  99.7 0.9 concatenate.27.ahead_ref
  100.6 0.9 concatenate.28.behind_ref
  101.5 0.8 copy.54.column_ref
  103.0 0.9 fusion.3
  103.9 1.6 fusion.4
  105.5 0.6 dynamic_slice.6
  106.1 0.6 dynamic_slice.7
  106.7 0.9 concatenate.26.stay_ref
  107.6 11.8 %shard_map.315 = (bf16[256,512]{1,0:T(8,128)(2,1)}, bf16[256,1536]{1,0:T(8,128)(2,1)}, f32[256,2048]{1,0:T(8,128)}, bf16[256,2560]{1,0:T(8,128)(2,1)}, f32[256,512]{1,0:T(8,128)}) custom-call(f32[256,512]{1,0:T(8,128)} %get-tuple-element.57.resid_ref, bf16[512,3584]{1,0:T(8,128)(2,1)} %bitcast.61, bf16[2560,512]{1,0:T(8,128)(2,1)} %bitcast.63, ...), custom_call_target="tpu_custom_call" | custom-call | tf_op jit(solution)/shard_map/pallas_call | solution.py:189
  119.4 82.3 %shard_map.316 = (f32[256,512]{1,0:T(8,128)}, f32[4,8,256]{2,1,0:T(8,128)}, f32[256,1]{1,0:T(8,128)}, bf16[32,256,512]{2,1,0:T(8,128)(2,1)}) custom-call(f32[6288,512]{1,0:T(8,128)} %refs_11_.1, bf16[256,512]{1,0:T(8,128)(2,1)} %get-tuple-element.61.own_ref, bf16[8,256,512]{2,1,0:T(8,128)(2,1)} %get-tuple-element.62.aims_ref, s32[8,1,256]{2,1,0:T(1,128)} %bitcast.84, ...), custom_call_target="tpu_custom_call" | custom-call | flops 26373783552 | bytes 12877824 | tf_op jit(solution)/shard_map/pallas_call | solution.py:1194
  201.8 21.2 %shard_map.317 = (bf16[256,512]{1,0:T(8,128)(2,1)}, f32[1,7680]{1,0:T(1,128)}, f32[8,768,512]{2,1,0:T(8,128)}) custom-call(f32[256,512]{1,0:T(8,128)} %get-tuple-element.67.final_grad_ref, f32[256,512]{1,0:T(8,128)} %get-tuple-element.57.resid_ref, bf16[512,3584]{1,0:T(8,128)(2,1)} %bitcast.62, bf16[2560,512]{1,0:T(8,128)(2,1)} %bitcast.64, ...), custom_call_target="tpu_custom_call" | custom-call | tf_op jit(solution)/shard_map/pallas_call | solution.py:377
  223.0 0.8 reduce.5
  223.8 0.1 reshape.241
  223.9 0.6 copy.65
  224.6 0.2 convolution_convert_fusion
  224.8 6.7 %select_reduce_fusion = (s32[16,512]{1,0:T(8,128)S(1)}, s32[16,512]{1,0:T(8,128)S(1)}) fusion(s32[16,512]{1,0:T(8,128)S(1)} %sub.65, s32[16,512]{1,0:T(8,128)S(1)} %convolution_convert_fusion, pred[16,512]{1,0:T(8,128)(4,1)S(1)} %compare_and_fusion), kind=kLoop, calls=%fused_computation | loop fusion | flops 25149440 | bytes 139264 | tf_op jit(solution)/shard_map/reduce_sum | solution.py:1758
  231.4 0.6 reshape.236.place_ref
  232.1 0.6 reshape.237.row_ref
  232.7 0.1 reduce_sum.159
  232.8 0.6 reduce_sum.160.count_ref
  233.4 0.7 compare_select_fusion.logsum_ref
  234.1 154.9 %shard_map.318 = (f32[6288,512]{1,0:T(8,128)}, f32[1,512]{1,0:T(1,128)}, bf16[32,256,512]{2,1,0:T(8,128)(2,1)}, f32[8,128]{1,0:T(8,128)}, f32[768,512]{1,0:T(8,128)}) custom-call(f32[6288,512]{1,0:T(8,128)} %refs_11_.1, bf16[8192,512]{1,0:T(8,128)(2,1)} %bitcast.95, f32[4,1,2048]{2,1,0:T(1,128)} %compare_select_fusion.logsum_ref, f32[4,1,2048]{2,1,0:T(1,128)} %bitcast.71, ...), custom_call_target="tpu_custom_call" | custom-call | flops 105495134208 | bytes 42532864 | tf_op jit(solution)/shard_map/pallas_call | solution.py:1618
  389.0 19.9 %shard_map.319 = (f32[6288,512]{1,0:T(8,128)}, f32[1,512]{1,0:T(1,128)}) custom-call(s32[16]{0:T(128)} %reduce_sum.160.count_ref, s32[16,1,512]{2,1,0:T(1,128)} %reshape.236.place_ref, s32[16,1,512]{2,1,0:T(1,128)} %reshape.237.row_ref, bf16[8192,512]{1,0:T(8,128)(2,1)} %bitcast.65), custom_call_target="tpu_custom_call" | custom-call | tf_op jit(solution)/shard_map/pallas_call | solution.py:1800
  409.0 1.3 reduce_sum.163
  410.2 0.6 reduce_sum.164
  410.9 0.1 slice.48
  410.9 0.6 reduce_sum.157
  412.9 1.1 fusion.1
  414.7 1.6 fusion.10
  416.9 1.2 fusion.11
  418.7 0.7 fusion.9
  419.4 0.7 pad.19.own_ref
  420.1 26.2 %shard_map.320.refs_0_ = f32[32,8,128]{2,1,0:T(8,128)} custom-call(f32[8,128]{1,0:T(8,128)} %pad.19.own_ref), custom_call_target="tpu_custom_call" | custom-call | tf_op jit(solution)/shard_map/pallas_call | solution.py:1740
  446.4 1.0 copy.60
  447.4 1.1 slice_reduce_fusion
  448.4 0.6 fusion.12
  449.7 0.0 all-gather.5.cloned.1.call-done
  449.7 5.3 %reshape.256.refs_3_ = bf16[6288,512]{1,0:T(8,128)(2,1)} reshape(bf16[4,1572,512]{2,1,0:T(8,128)(2,1)} %all-gather.5.cloned.1.call-done) | data formatting | bytes 12877824
  455.0 5.2 reshape.258.refs_6_
  460.2 57.6 %shard_map.321 = (f32[6288,512]{1,0:T(8,128)}, f32[6288,512]{1,0:T(8,128)}, f32[1572,512]{1,0:T(8,128)}, f32[1572,512]{1,0:T(8,128)}, f32[1572,512]{1,0:T(8,128)...) custom-call(f32[32,8,128]{2,1,0:T(8,128)} %shard_map.320.refs_0_, ...), custom_call_target="tpu_custom_call" | custom-call | tf_op jit(solution)/shard_map/pallas_call | solution.py:1974
  (40 shorter events, 0.2 us)
Async XLA Ops:
  7.2 3.6 copy-start
  7.2 442.5 %all-gather.5.cloned.1.call-start = ((), (), s32[]{:S(2)}) async-start(), calls=%async_computation | async-start | bytes 8069120 | tf_op jit(solution)/shard_map/all_gather | solution.py:2047
  10.7 1.5 copy-start.4
  10.7 1.6 copy-start.10
  10.7 1.6 copy-start.12
  10.7 2.7 copy-start.7
  10.7 4.0 copy-start.11
  10.7 444.3 %all-gather.7.cloned.1.call-start = ((), (), s32[]{:S(2)}) async-start(), calls=%async_computation.1 | async-start | bytes 8069120 | tf_op jit(solution)/shard_map/all_gather | solution.py:2048
  103.9 129.5 %copy-start.2 = (f32[32,2,128]{2,1,0:T(2,128)}, f32[32,2,128]{2,1,0:T(2,128)S(1)}, u32[]{:S(2)}) copy-start(f32[32,2,128]{2,1,0:T(2,128)S(1)} %fusion.3) | copy-start | bytes 98308
  105.5 13.9 %copy-start.5 = (s32[32,2,128]{2,1,0:T(2,128)}, s32[32,2,128]{2,1,0:T(2,128)S(1)}, u32[]{:S(2)}) copy-start(s32[32,2,128]{2,1,0:T(2,128)S(1)} %get-tuple-element.110) | copy-start | bytes 98308
  201.8 22.7 %copy-start.6 = (f32[4,8,256]{2,1,0:T(8,128)S(1)}, f32[4,8,256]{2,1,0:T(8,128)}, u32[]{:S(2)}) copy-start(f32[4,8,256]{2,1,0:T(8,128)} %get-tuple-element.66) | copy-start | bytes 98308
  389.0 21.2 %copy-start.9 = (f32[1,512]{1,0:T(1,128)S(1)}, f32[1,512]{1,0:T(1,128)}, u32[]{:S(2)}) copy-start(f32[1,512]{1,0:T(1,128)} %get-tuple-element.77) | copy-start | bytes 6148
  389.0 21.8 %copy-start.1 = (f32[768,512]{1,0:T(8,128)S(1)}, f32[768,512]{1,0:T(8,128)}, u32[]{:S(2)}) copy-start(f32[768,512]{1,0:T(8,128)} %get-tuple-element.78) | copy-start | bytes 4718596
  389.0 21.9 %copy-start.3 = (f32[256,1]{1,0:T(8,128)S(1)}, f32[256,1]{1,0:T(8,128)}, u32[]{:S(2)}) copy-start(f32[256,1]{1,0:T(8,128)} %get-tuple-element.64) | copy-start | bytes 3076
  408.9 7.9 %copy-start.8 = (f32[8,128]{1,0:T(8,128)S(1)}, f32[8,128]{1,0:T(8,128)}, u32[]{:S(2)}) copy-start(f32[8,128]{1,0:T(8,128)} %get-tuple-element.79) | copy-start | bytes 12292
Sparse Core Ops, SparseCore 0:
  10.8 94.8 all-gather.4
  108.2 107.3 all-gather.6

commit v5 on v4

--- a/solution.py
+++ b/solution.py
@@ -487,6 +487,7 @@
         in_low,
         out_low,
         wide,
+        again,
         looked,
         to_core,
         from_core,
@@ -625,8 +626,14 @@
                 to_lane.at[j], from_lane.at[j], sum_send.at[j], sum_recv.at[j], lane_device(j)
             )
 
-        fetch = pltpu.make_async_copy(table_ref, wide, table_sem)
+        fetch = pltpu.make_async_copy(
+            table_ref, wide.at[pl.ds(0, vocab), :], table_sem.at[0]
+        )
+        refetch = pltpu.make_async_copy(
+            head_ref, again.at[pl.ds(0, vocab), :], table_sem.at[1]
+        )
         fetch.start()
+        refetch.start()
         barrier = pltpu.get_barrier_semaphore()
 
         def greet(k, carry):
@@ -636,6 +643,8 @@
             return carry
 
         lax.fori_loop(1, amount, greet, 0)
+        for held in (wide, again):
+            held[vocab : vocab + 8, :] = jnp.zeros((8, width), FLOAT)
         in_low[...] = in_ref[...].astype(NARROW)
         out_low[...] = out_ref[...].astype(NARROW)
         every_ref[me] = packed_ref[...]
@@ -674,18 +683,21 @@
         fetch.wait()
         start = member * vocab
 
-        def look(slot, ahead):
+        def look(slot, ahead, source):
             for b in range(batches):
 
                 def lap(i, carry):
+                    first = pl.multiple_of(i * unroll, unroll)
                     for u in range(unroll):
-                        spot = i * unroll + u
-                        token = ids[slot, b, jnp.minimum(spot + ahead, seq - 1)]
-                        row = jnp.where(spot + ahead < seq, token, 0) - start
-                        inside = (row >= 0) & (row < vocab)
-                        safe = jnp.where(inside, row, 0)
-                        keep = jnp.where(inside, 1.0, 0.0)
-                        looked[pl.ds(b * seq + spot, 1), :] = wide[pl.ds(safe, 1), :] * keep
+                        if ahead and u + ahead >= unroll:
+                            spot = first + u + ahead
+                            token = ids[slot, b, jnp.minimum(spot, seq - 1)]
+                            token = jnp.where(spot < seq, token, 0)
+                        else:
+                            token = ids[slot, b, first + u + ahead]
+                        row = token - start
+                        row = jnp.where((row >= 0) & (row < vocab), row, vocab)
+                        looked[pl.ds(b * seq + first + u, 1), :] = source[pl.ds(row, 1), :]
                     return carry
 
                 lax.fori_loop(0, seq // unroll, lap, 0)
@@ -695,7 +707,28 @@
             j = lax.rem(step + 1, chips)
             there = chip_at(j) * 2
 
-            @pl.when(step == chips // 2)
+            to_core[j] = look(there + 1 - core, 0, wide)
+            part_copy(j).start()
+            mine = look(there + core, 0, wide).astype(FLOAT)
+            part_copy(j).wait_recv()
+            mine = mine + from_core[j].astype(FLOAT)
+
+            @pl.when(j > 0)
+            def _():
+                to_lane[j] = mine.astype(NARROW)
+                sum_copy(j).start()
+
+            @pl.when(j == 0)
+            def _():
+                resid_ref[...] = mine
+
+            return carry
+
+        lax.fori_loop(0, chips, lap, 0)
+        refetch.wait()
+
+        def aim(slot, carry):
+            @pl.when(slot == 0)
             def _():
                 for w in range(2):
                     for c in range(1, chips):
@@ -704,30 +737,7 @@
                             for k in range(1, replicas):
                                 plane_copy(w, k, c).start()
 
-            to_core[j] = look(there + 1 - core, 0)
-            part_copy(j).start()
-            mine = look(there + core, 0).astype(FLOAT)
-            part_copy(j).wait_recv()
-            mine = mine + from_core[j].astype(FLOAT)
-
-            @pl.when(j > 0)
-            def _():
-                to_lane[j] = mine.astype(NARROW)
-                sum_copy(j).start()
-
-            @pl.when(j == 0)
-            def _():
-                resid_ref[...] = mine
-
-            return carry
-
-        lax.fori_loop(0, chips, lap, 0)
-        again = pltpu.make_async_copy(head_ref, wide, table_sem)
-        again.start()
-        again.wait()
-
-        def aim(slot, carry):
-            aims_ref[slot] = look(slot, 1)
+            aims_ref[slot] = look(slot, 1, again)
             return carry
 
         lax.fori_loop(0, groups, aim, 0)
@@ -788,14 +798,15 @@
         scratch_shapes=[
             vmem(in_shard.shape, NARROW),
             vmem(out_shard.shape, NARROW),
-            vmem((vocab, width), FLOAT),
+            vmem((vocab + 8, width), FLOAT),
+            vmem((vocab + 8, width), FLOAT),
             vmem((own, width), FLOAT),
             vmem((chips, own, width), NARROW),
             vmem((chips, own, width), NARROW),
             vmem((chips, own, width), NARROW),
             vmem((chips, own, width), NARROW),
             pltpu.SMEM((groups,) + packed.shape, jnp.int32),
-            dma,
+            dma((2,)),
             dma,
             dma((2,)),
             dma((amount,)),
@@ -909,6 +920,13 @@
         def replica_before(k):
             return lax.rem(place.replica + replicas - k, replicas)
 
+        def turn(step):
+            if isinstance(step, int):
+                return (step + 1) // 2 if step % 2 else (chips - step // 2) % chips
+            ahead = (step + 1) // 2
+            behind = lax.rem(chips - step // 2, chips)
+            return jnp.where(lax.rem(step, 2) == 1, ahead, behind)
+
         def lane_copy(j):
             return remote(own_ref, hid.at[me], lane_send.at[j], lane_recv.at[j], lane_device(j))
 
@@ -1015,8 +1033,8 @@
         )
         own_core = remote(own_ref, hid.at[me], core_send.at[0], core_recv.at[0], place.sibling())
         own_core.start()
-        for j in range(1, chips):
-            lane_copy(j).start()
+        for step in range(1, min(3, chips)):
+            lane_copy(turn(step)).start()
         hid[me] = own_ref[...]
         for k in range(1, replicas):
             plane_copy(k, 0).start()
@@ -1031,11 +1049,13 @@
         spots = lax.broadcasted_iota(jnp.int32, (block, own), 0)
 
         def forward(step, carry):
-            j = step // 2
+            j = turn(step // 2)
             other = lax.rem(step, 2)
 
             @pl.when(step == 1)
             def _():
+                for later in range(3, chips):
+                    lane_copy(turn(later)).start()
                 there = hid.at[place.sibling_member]
                 remote(
                     there, there, core_send.at[0], core_recv.at[0], place.sibling()
@@ -1117,7 +1137,7 @@
             return total
 
         def backward(step, carry):
-            j = lax.rem(step + 1, chips)
+            j = turn(chips - 1 - step)
 
             @pl.when(step == chips - 1)
             def _():

time: 534 us -> 546 us (1.022)
  Pallas kernels: 454 us -> 465 us
    pallas_call x1, Pallas kernels: 79.7 us -> 90.8 us  [start_kernel(): pl.pallas_call(kernel, in_specs=[whole, whole, whole, whole, anywhere, an...]
    pallas_call x1, Pallas kernels: 82.3 us -> 89.6 us  [head_kernel(): pl.pallas_call(kernel, in_specs=[anywhere, whole, whole, whole, whole], o...]
    pallas_call x1, Pallas kernels: 155 us -> 149 us  [head_table_grad(): pl.pallas_call(kernel, grid=(steps,), in_specs=[pl.BlockSpec((block, widt...]
  transfers between devices with their start and end apart: 2 -> 2, of which waited for: 0 -> 0; matrix products, arithmetic and copies ran while one was open for 8% -> 8% of each run, Pallas kernels for 75% -> 76%
where the time goes in v5:
time: 546 us; the launch traced here: 537 us
  Pallas kernels  465 us (85%)
  other arithmetic  29.1 us (5%)
  local copies, waits for them, and re-layouts  22.7 us (4%)
  between operations  20.3 us (4%)
    pallas_call x1, Pallas kernels, head_table_grad(): pl.pallas_call(kernel, grid=(steps,), in_specs=[pl.BlockSpec((block, widt...  149 us
    pallas_call x1, Pallas kernels, start_kernel(): pl.pallas_call(kernel, in_specs=[whole, whole, whole, whole, anywhere, an...  90.8 us
    pallas_call x1, Pallas kernels, head_kernel(): pl.pallas_call(kernel, in_specs=[anywhere, whole, whole, whole, whole], o...  89.6 us
    pallas_call x1, Pallas kernels, update_all(): pl.pallas_call(kernel, grid=(steps,), in_specs=in_specs, out_specs=out_sp...  57.6 us
    pallas_call x1, Pallas kernels, exchange_scalars(): pl.pallas_call(kernel, in_specs=[whole], out_specs=whole, out_shape=jax.S...  25.5 us
    pallas_call x1, Pallas kernels, layer_backward(): pl.pallas_call(kernel, in_specs=[whole] * 14, out_specs=[whole, whole, pl...  21.1 us
    pallas_call x1, Pallas kernels, embed_table_grad(): pl.pallas_call(kernel, grid_spec=pltpu.PrefetchScalarGridSpec(num_scalar_...  18.9 us
    pallas_call x1, Pallas kernels, layer_forward(): pl.pallas_call(kernel, out_shape=[jax.ShapeDtypeStruct((rows, width), NAR...  12.5 us
  transfers between devices with their start and end apart: 2, of which 0 were waited for; matrix products, arithmetic and copies ran while one was open for 8% of the time, Pallas kernels for 76%

profile of v5, /device:TPU:0, one launch (start us, length us, event | category | flops | bytes accessed | tf_op | source)
XLA Modules:
  0.0 537.3 jit_solution(5065033665829203705)
XLA Ops:
  7.2 0.0 all-gather.5.cloned.1.call-start
  7.2 3.4 convert_bitcast_fusion.1
  10.7 0.0 copy-start.11
  10.7 0.0 all-gather.5.cloned.1.call-update
  10.7 0.0 all-gather.7.cloned.1.call-start
  10.8 1.4 convert_bitcast_fusion
  12.1 0.0 all-gather.7.cloned.1.call-update
  12.2 0.1 slice_compare_fusion
  12.3 0.1 fusion.8
  12.3 0.1 fusion.5
  12.4 0.1 fusion.6
  12.5 0.1 select_reduce_fusion.3
  12.7 0.6 convert_reduce_fusion
  13.4 0.6 pad_bitcast_fusion.1.line_ref
  13.9 0.6 broadcast_in_dim.115
  14.6 0.1 pad.24.clone
  14.7 0.7 add_add_fusion.packed_ref
  15.3 90.8 %shard_map.314 = (s32[32,8,128]{2,1,0:T(8,128)}, f32[8,8,128]{2,1,0:T(8,128)}, bf16[8,64,3584]{2,1,0:T(8,128)(2,1)}, bf16[8,320,512]{2,1,0:T(8,128)(2,1)}, f32[2...) custom-call(s32[8,128]{1,0:T(8,128)} %add_add_fusion.packed_ref, f32[8,128]{1,0:T(8,128)} %pad_bitcast_fusion.1.line_ref, ...), custom_call_target="tpu_custom_call" | custom-call | bytes 12877824 | tf_op jit(solution)/shard_map/pallas_call | solution.py:786
  106.2 1.0 slice.44
  107.2 1.6 slice_reduce_fusion.1
  108.8 0.8 convert_bitcast_fusion.2
  109.5 0.7 reshape.254.vector_ref
  110.2 0.1 select_reduce_fusion.2
  110.3 0.5 multiply_sine_fusion
  110.9 0.9 concatenate.27.ahead_ref
  111.8 0.9 concatenate.28.behind_ref
  112.7 0.8 copy.54.column_ref
  114.1 0.9 fusion.3
  115.1 1.6 fusion.4
  116.7 0.6 dynamic_slice.6
  117.3 0.6 dynamic_slice.7
  117.9 0.9 concatenate.26.stay_ref
  118.8 12.5 %shard_map.315 = (bf16[256,512]{1,0:T(8,128)(2,1)}, bf16[256,1536]{1,0:T(8,128)(2,1)}, f32[256,2048]{1,0:T(8,128)}, bf16[256,2560]{1,0:T(8,128)(2,1)}, f32[256,512]{1,0:T(8,128)}) custom-call(f32[256,512]{1,0:T(8,128)} %get-tuple-element.57.resid_ref, bf16[512,3584]{1,0:T(8,128)(2,1)} %bitcast.61, bf16[2560,512]{1,0:T(8,128)(2,1)} %bitcast.63, ...), custom_call_target="tpu_custom_call" | custom-call | tf_op jit(solution)/shard_map/pallas_call | solution.py:189
  131.3 89.6 %shard_map.316 = (f32[256,512]{1,0:T(8,128)}, f32[4,8,256]{2,1,0:T(8,128)}, f32[256,1]{1,0:T(8,128)}, bf16[32,256,512]{2,1,0:T(8,128)(2,1)}) custom-call(f32[6288,512]{1,0:T(8,128)} %refs_11_.1, bf16[256,512]{1,0:T(8,128)(2,1)} %get-tuple-element.61.own_ref, bf16[8,256,512]{2,1,0:T(8,128)(2,1)} %get-tuple-element.62.aims_ref, s32[8,1,256]{2,1,0:T(1,128)} %bitcast.84, ...), custom_call_target="tpu_custom_call" | custom-call | flops 26373783552 | bytes 12877824 | tf_op jit(solution)/shard_map/pallas_call | solution.py:1214
  220.9 21.1 %shard_map.317 = (bf16[256,512]{1,0:T(8,128)(2,1)}, f32[1,7680]{1,0:T(1,128)}, f32[8,768,512]{2,1,0:T(8,128)}) custom-call(f32[256,512]{1,0:T(8,128)} %get-tuple-element.67.final_grad_ref, f32[256,512]{1,0:T(8,128)} %get-tuple-element.57.resid_ref, bf16[512,3584]{1,0:T(8,128)(2,1)} %bitcast.62, bf16[2560,512]{1,0:T(8,128)(2,1)} %bitcast.64, ...), custom_call_target="tpu_custom_call" | custom-call | tf_op jit(solution)/shard_map/pallas_call | solution.py:377
  242.1 0.8 reduce.5
  242.9 0.1 reshape.241
  243.0 0.6 copy.65
  243.7 0.2 convolution_convert_fusion
  243.9 6.7 %select_reduce_fusion = (s32[16,512]{1,0:T(8,128)S(1)}, s32[16,512]{1,0:T(8,128)S(1)}) fusion(s32[16,512]{1,0:T(8,128)S(1)} %sub.65, s32[16,512]{1,0:T(8,128)S(1)} %convolution_convert_fusion, pred[16,512]{1,0:T(8,128)(4,1)S(1)} %compare_and_fusion), kind=kLoop, calls=%fused_computation | loop fusion | flops 25149440 | bytes 139264 | tf_op jit(solution)/shard_map/reduce_sum | solution.py:1778
  250.6 0.6 reshape.236.place_ref
  251.2 0.6 reshape.237.row_ref
  251.9 0.1 reduce_sum.159
  251.9 0.6 reduce_sum.160.count_ref
  252.6 0.7 compare_select_fusion.logsum_ref
  253.3 148.8 %shard_map.318 = (f32[6288,512]{1,0:T(8,128)}, f32[1,512]{1,0:T(1,128)}, bf16[32,256,512]{2,1,0:T(8,128)(2,1)}, f32[8,128]{1,0:T(8,128)}, f32[768,512]{1,0:T(8,128)}) custom-call(f32[6288,512]{1,0:T(8,128)} %refs_11_.1, bf16[8192,512]{1,0:T(8,128)(2,1)} %bitcast.95, f32[4,1,2048]{2,1,0:T(1,128)} %compare_select_fusion.logsum_ref, f32[4,1,2048]{2,1,0:T(1,128)} %bitcast.71, ...), custom_call_target="tpu_custom_call" | custom-call | flops 105495134208 | bytes 42532864 | tf_op jit(solution)/shard_map/pallas_call | solution.py:1638
  402.1 18.9 %shard_map.319 = (f32[6288,512]{1,0:T(8,128)}, f32[1,512]{1,0:T(1,128)}) custom-call(s32[16]{0:T(128)} %reduce_sum.160.count_ref, s32[16,1,512]{2,1,0:T(1,128)} %reshape.236.place_ref, s32[16,1,512]{2,1,0:T(1,128)} %reshape.237.row_ref, bf16[8192,512]{1,0:T(8,128)(2,1)} %bitcast.65), custom_call_target="tpu_custom_call" | custom-call | tf_op jit(solution)/shard_map/pallas_call | solution.py:1820
  421.0 1.3 reduce_sum.163
  422.3 0.6 reduce_sum.164
  422.9 0.1 slice.48
  423.0 0.6 reduce_sum.157
  424.9 1.1 fusion.1
  426.7 1.6 fusion.10
  428.9 1.2 fusion.11
  430.8 0.7 fusion.9
  431.5 0.7 pad.19.own_ref
  432.1 25.5 %shard_map.320.refs_0_ = f32[32,8,128]{2,1,0:T(8,128)} custom-call(f32[8,128]{1,0:T(8,128)} %pad.19.own_ref), custom_call_target="tpu_custom_call" | custom-call | tf_op jit(solution)/shard_map/pallas_call | solution.py:1760
  457.7 1.0 copy.60
  458.7 1.1 slice_reduce_fusion
  459.7 0.6 fusion.12
  461.0 0.0 all-gather.5.cloned.1.call-done
  461.0 5.3 reshape.256.refs_3_
  466.3 5.2 reshape.258.refs_6_
  471.5 57.6 %shard_map.321 = (f32[6288,512]{1,0:T(8,128)}, f32[6288,512]{1,0:T(8,128)}, f32[1572,512]{1,0:T(8,128)}, f32[1572,512]{1,0:T(8,128)}, f32[1572,512]{1,0:T(8,128)...) custom-call(f32[32,8,128]{2,1,0:T(8,128)} %shard_map.320.refs_0_, ...), custom_call_target="tpu_custom_call" | custom-call | tf_op jit(solution)/shard_map/pallas_call | solution.py:1994
  (40 shorter events, 0.2 us)
Async XLA Ops:
  7.2 3.6 copy-start
  7.2 453.8 %all-gather.5.cloned.1.call-start = ((), (), s32[]{:S(2)}) async-start(), calls=%async_computation | async-start | bytes 8069120 | tf_op jit(solution)/shard_map/all_gather | solution.py:2067
  10.7 1.5 copy-start.4
  10.7 1.6 copy-start.10
  10.7 1.6 copy-start.12
  10.7 2.7 copy-start.7
  10.7 4.0 copy-start.11
  10.7 455.6 %all-gather.7.cloned.1.call-start = ((), (), s32[]{:S(2)}) async-start(), calls=%async_computation.1 | async-start | bytes 8069120 | tf_op jit(solution)/shard_map/all_gather | solution.py:2068
  115.1 137.5 %copy-start.2 = (f32[32,2,128]{2,1,0:T(2,128)}, f32[32,2,128]{2,1,0:T(2,128)S(1)}, u32[]{:S(2)}) copy-start(f32[32,2,128]{2,1,0:T(2,128)S(1)} %fusion.3) | copy-start | bytes 98308
  116.7 14.6 %copy-start.5 = (s32[32,2,128]{2,1,0:T(2,128)}, s32[32,2,128]{2,1,0:T(2,128)S(1)}, u32[]{:S(2)}) copy-start(s32[32,2,128]{2,1,0:T(2,128)S(1)} %get-tuple-element.110) | copy-start | bytes 98308
  220.9 22.7 %copy-start.6 = (f32[4,8,256]{2,1,0:T(8,128)S(1)}, f32[4,8,256]{2,1,0:T(8,128)}, u32[]{:S(2)}) copy-start(f32[4,8,256]{2,1,0:T(8,128)} %get-tuple-element.66) | copy-start | bytes 98308
  402.0 20.2 %copy-start.9 = (f32[1,512]{1,0:T(1,128)S(1)}, f32[1,512]{1,0:T(1,128)}, u32[]{:S(2)}) copy-start(f32[1,512]{1,0:T(1,128)} %get-tuple-element.77) | copy-start | bytes 6148
  402.0 20.8 %copy-start.1 = (f32[768,512]{1,0:T(8,128)S(1)}, f32[768,512]{1,0:T(8,128)}, u32[]{:S(2)}) copy-start(f32[768,512]{1,0:T(8,128)} %get-tuple-element.78) | copy-start | bytes 4718596
  402.1 20.9 %copy-start.3 = (f32[256,1]{1,0:T(8,128)S(1)}, f32[256,1]{1,0:T(8,128)}, u32[]{:S(2)}) copy-start(f32[256,1]{1,0:T(8,128)} %get-tuple-element.64) | copy-start | bytes 3076
  421.0 7.9 %copy-start.8 = (f32[8,128]{1,0:T(8,128)S(1)}, f32[8,128]{1,0:T(8,128)}, u32[]{:S(2)}) copy-start(f32[8,128]{1,0:T(8,128)} %get-tuple-element.79) | copy-start | bytes 12292
Sparse Core Ops, SparseCore 0:
  10.8 99.7 all-gather.4
  113.0 106.7 all-gather.6

commit v6 on v5

--- a/solution.py
+++ b/solution.py
@@ -2064,8 +2064,8 @@
         replicas,
     )
     vector_full = lines.reshape(groups, -1)[:, :amount].reshape(-1).astype(NARROW)
-    embed_moment_low = lax.all_gather(embed_moment.astype(NARROW), "dp", axis=0, tiled=True)
-    head_moment_low = lax.all_gather(head_moment.astype(NARROW), "dp", axis=0, tiled=True)
+    early_moment, resid = lax.optimization_barrier((head_moment, resid))
+    head_moment_low = lax.all_gather(early_moment.astype(NARROW), "dp", axis=0, tiled=True)
     tokens_all = everyone[:, :batches]
     count = jnp.maximum(jnp.sum(everyone[:, 2 * batches, 0]).astype(FLOAT), 1.0)
     divisor_all = everyone[:, batches : 2 * batches].astype(FLOAT)
@@ -2107,6 +2107,7 @@
         kept,
         groups,
     )
+    token_grad, head_moment_low = lax.optimization_barrier((token_grad, head_moment_low))
     slices = jnp.pad(vector_grad.reshape(groups, amount), ((0, 0), (0, -amount % 1024)))
     in_rows = in_weights.shape[0]
     cut = owner_grads.shape[1] - out_weights.shape[0]
@@ -2130,6 +2131,8 @@
         owned[cut:],
         vector_sum.reshape(-1)[:amount],
     ]
+    late_moment, token_grads = lax.optimization_barrier((embed_moment, token_grads))
+    embed_moment_low = lax.all_gather(late_moment.astype(NARROW), "dp", axis=0, tiled=True)
     embed_grad, embed_square = embed_table_grad(token_grads, *lists, vocab_rows)
     square = jnp.sum(embed_square) + jnp.sum(head_square)
     for grad in layer_grads:

time: 546 us -> 537 us (0.984)
  Pallas kernels: 465 us -> 441 us
  waiting for transfers between devices: 0.06 us -> 17.7 us
    pallas_call x1, Pallas kernels: 90.8 us -> 65.8 us  [start_kernel(): pl.pallas_call(kernel, in_specs=[whole, whole, whole, whole, anywhere, an...]
    all_gather x2, waiting for transfers between devices: 0.02 us -> 17.7 us  [the longest x1 17.7 us: shards(): lax.all_gather(late_moment.astype(NARROW), 'dp', axis=0, tiled=True)]
    unnamed x32 -> x29, local copies, waits for them, and re-layouts: 12.2 us -> 7.15 us
  transfers between devices with their start and end apart: 2 -> 2, of which waited for: 0 -> 1; matrix products, arithmetic and copies ran while one was open for 8% -> 6% of each run, Pallas kernels for 76% -> 32%
where the time goes in v6:
time: 537 us; the launch traced here: 529 us
  Pallas kernels  441 us (82%)
  other arithmetic  26.9 us (5%)
  local copies, waits for them, and re-layouts  22.7 us (4%)
  between operations  20.3 us (4%)
  waiting for transfers between devices  17.7 us (3%)
    pallas_call x1, Pallas kernels, head_table_grad(): pl.pallas_call(kernel, grid=(steps,), in_specs=[pl.BlockSpec((block, widt...  149 us
    pallas_call x1, Pallas kernels, head_kernel(): pl.pallas_call(kernel, in_specs=[anywhere, whole, whole, whole, whole], o...  89.6 us
    pallas_call x1, Pallas kernels, start_kernel(): pl.pallas_call(kernel, in_specs=[whole, whole, whole, whole, anywhere, an...  65.8 us
    pallas_call x1, Pallas kernels, update_all(): pl.pallas_call(kernel, grid=(steps,), in_specs=in_specs, out_specs=out_sp...  57.5 us
    pallas_call x1, Pallas kernels, exchange_scalars(): pl.pallas_call(kernel, in_specs=[whole], out_specs=whole, out_shape=jax.S...  26.4 us
    pallas_call x1, Pallas kernels, layer_backward(): pl.pallas_call(kernel, in_specs=[whole] * 14, out_specs=[whole, whole, pl...  21.4 us
    pallas_call x1, Pallas kernels, embed_table_grad(): pl.pallas_call(kernel, grid_spec=pltpu.PrefetchScalarGridSpec(num_scalar_...  19.5 us
    all_gather x1, waiting for transfers between devices, shards(): lax.all_gather(late_moment.astype(NARROW), 'dp', axis=0, tiled=True)  17.7 us
  transfers between devices with their start and end apart: 2, of which 1 were waited for; matrix products, arithmetic and copies ran while one was open for 6% of the time, Pallas kernels for 32%

profile of v6, /device:TPU:0, one launch (start us, length us, event | category | flops | bytes accessed | tf_op | source)
XLA Modules:
  0.0 529.0 jit_solution(13955959190806062208)
XLA Ops:
  7.2 0.0 all-gather.5.cloned.1.call-start
  7.2 0.8 slice_compare_fusion
  8.1 0.8 fusion.8
  8.8 0.8 fusion.5
  9.6 0.8 fusion.6
  10.4 0.6 convert_reduce_fusion
  11.0 1.3 pad_bitcast_fusion.1.line_ref
  12.3 0.6 broadcast_in_dim.115
  13.0 0.1 pad.24.clone
  13.0 1.3 add_add_fusion.packed_ref
  14.4 65.8 %shard_map.314 = (s32[32,8,128]{2,1,0:T(8,128)}, f32[8,8,128]{2,1,0:T(8,128)}, bf16[8,64,3584]{2,1,0:T(8,128)(2,1)}, bf16[8,320,512]{2,1,0:T(8,128)(2,1)}, f32[2...) custom-call(s32[8,128]{1,0:T(8,128)} %add_add_fusion.packed_ref, f32[8,128]{1,0:T(8,128)} %pad_bitcast_fusion.1.line_ref, ...), custom_call_target="tpu_custom_call" | custom-call | bytes 12877824 | tf_op jit(solution)/shard_map/pallas_call | solution.py:786
  80.2 0.0 copy-start.6
  80.3 1.4 convert_bitcast_fusion.1
  81.6 0.0 all-gather.5.cloned.1.call-update
  81.6 0.0 all-gather.7.cloned.1.call-start
  81.7 0.0 copy-done.8
  81.7 0.7 reshape.254.vector_ref
  82.4 0.2 select_reduce_fusion.3
  82.6 0.1 select_reduce_fusion.2
  82.7 0.5 multiply_sine_fusion
  83.3 0.9 concatenate.27.ahead_ref
  84.2 0.9 concatenate.28.behind_ref
  85.1 0.8 copy.54.column_ref
  85.9 0.1 slice.44
  86.0 0.7 slice_reduce_fusion.1
  87.3 0.7 fusion.4
  88.0 0.6 dynamic_slice.6
  88.6 0.0 copy-start.3
  88.6 0.6 dynamic_slice.7
  89.3 0.9 concatenate.26.stay_ref
  90.2 11.9 %shard_map.315 = (bf16[256,512]{1,0:T(8,128)(2,1)}, bf16[256,1536]{1,0:T(8,128)(2,1)}, f32[256,2048]{1,0:T(8,128)}, bf16[256,2560]{1,0:T(8,128)(2,1)}, f32[256,512]{1,0:T(8,128)}) custom-call(f32[256,512]{1,0:T(8,128)} %get-tuple-element.64.resid_ref, bf16[512,3584]{1,0:T(8,128)(2,1)} %bitcast.61, bf16[2560,512]{1,0:T(8,128)(2,1)} %bitcast.63, ...), custom_call_target="tpu_custom_call" | custom-call | tf_op jit(solution)/shard_map/pallas_call | solution.py:189
  102.0 89.6 %shard_map.316 = (f32[256,512]{1,0:T(8,128)}, f32[4,8,256]{2,1,0:T(8,128)}, f32[256,1]{1,0:T(8,128)}, bf16[32,256,512]{2,1,0:T(8,128)(2,1)}) custom-call(f32[6288,512]{1,0:T(8,128)} %refs_11_.1, bf16[256,512]{1,0:T(8,128)(2,1)} %get-tuple-element.68.own_ref, bf16[8,256,512]{2,1,0:T(8,128)(2,1)} %get-tuple-element.69.aims_ref, s32[8,1,256]{2,1,0:T(1,128)} %bitcast.84, ...), custom_call_target="tpu_custom_call" | custom-call | flops 26373783552 | bytes 12877824 | tf_op jit(solution)/shard_map/pallas_call | solution.py:1214
  191.7 21.4 %shard_map.317 = (bf16[256,512]{1,0:T(8,128)(2,1)}, f32[1,7680]{1,0:T(1,128)}, f32[8,768,512]{2,1,0:T(8,128)}) custom-call(f32[256,512]{1,0:T(8,128)} %get-tuple-element.74.final_grad_ref, f32[256,512]{1,0:T(8,128)} %get-tuple-element.64.resid_ref, bf16[512,3584]{1,0:T(8,128)(2,1)} %bitcast.62, bf16[2560,512]{1,0:T(8,128)(2,1)} %bitcast.64, ...), custom_call_target="tpu_custom_call" | custom-call | tf_op jit(solution)/shard_map/pallas_call | solution.py:377
  213.1 0.8 reduce.5
  213.9 0.1 reshape.241
  214.0 0.6 copy.65
  214.7 0.7 compare_select_fusion.logsum_ref
  215.4 5.2 reshape.256.refs_6_
  220.6 149.0 %shard_map.318 = (f32[6288,512]{1,0:T(8,128)}, f32[1,512]{1,0:T(1,128)}, bf16[32,256,512]{2,1,0:T(8,128)(2,1)}, f32[8,128]{1,0:T(8,128)}, f32[768,512]{1,0:T(8,128)}) custom-call(f32[6288,512]{1,0:T(8,128)} %refs_11_.1, bf16[8192,512]{1,0:T(8,128)(2,1)} %bitcast.95, f32[4,1,2048]{2,1,0:T(1,128)} %compare_select_fusion.logsum_ref, f32[4,1,2048]{2,1,0:T(1,128)} %bitcast.71, ...), custom_call_target="tpu_custom_call" | custom-call | flops 105495134208 | bytes 42532864 | tf_op jit(solution)/shard_map/pallas_call | solution.py:1638
  369.6 1.4 convert_bitcast_fusion
  371.0 0.0 all-gather.7.cloned.1.call-update
  371.1 0.2 convolution_convert_fusion
  371.3 6.5 %select_reduce_fusion = (s32[16,512]{1,0:T(8,128)S(1)}, s32[16,512]{1,0:T(8,128)S(1)}) fusion(s32[16,512]{1,0:T(8,128)S(1)} %sub.65, s32[16,512]{1,0:T(8,128)S(1)} %convolution_convert_fusion, pred[16,512]{1,0:T(8,128)(4,1)S(1)} %compare_and_fusion), kind=kLoop, calls=%fused_computation | loop fusion | flops 25149440 | bytes 139264 | tf_op jit(solution)/shard_map/reduce_sum | solution.py:1778
  377.7 0.6 reshape.236.place_ref
  378.4 0.6 reshape.237.row_ref
  379.0 0.1 reduce_sum.159
  379.1 0.6 reduce_sum.160.count_ref
  379.7 0.6 reduce_sum.157
  380.4 19.5 %shard_map.319 = (f32[6288,512]{1,0:T(8,128)}, f32[1,512]{1,0:T(1,128)}) custom-call(s32[16]{0:T(128)} %reduce_sum.160.count_ref, s32[16,1,512]{2,1,0:T(1,128)} %reshape.236.place_ref, s32[16,1,512]{2,1,0:T(1,128)} %reshape.237.row_ref, bf16[8192,512]{1,0:T(8,128)(2,1)} %bitcast.65), custom_call_target="tpu_custom_call" | custom-call | tf_op jit(solution)/shard_map/pallas_call | solution.py:1820
  399.9 1.3 reduce_sum.163
  401.2 0.6 reduce_sum.164
  401.8 0.1 slice.48
  403.2 1.1 fusion.1
  405.0 1.6 fusion.10
  407.2 1.2 fusion.11
  409.1 0.7 fusion.9
  409.8 0.7 pad.19.own_ref
  410.4 26.4 %shard_map.320.refs_0_ = f32[32,8,128]{2,1,0:T(8,128)} custom-call(f32[8,128]{1,0:T(8,128)} %pad.19.own_ref), custom_call_target="tpu_custom_call" | custom-call | tf_op jit(solution)/shard_map/pallas_call | solution.py:1760
  436.8 1.0 copy.60
  437.8 1.1 slice_reduce_fusion
  438.9 0.6 fusion.12
  440.2 17.7 %all-gather.7.cloned.1.call-done = bf16[4,1572,512]{2,1,0:T(8,128)(2,1)} async-done(((bf16[1,1572,512]{2,1,0:T(8,128)(2,1)}), bf16[4,1572,512]{2,1,0:T(8,128)(2,1)}) %all-gather.7.cloned.1.call-update) | async-done | bytes 6438928 | tf_op jit(solution)/shard_map/all_gather | solution.py:2135
  457.9 5.5 %reshape.258.refs_3_ = bf16[6288,512]{1,0:T(8,128)(2,1)} reshape(bf16[4,1572,512]{2,1,0:T(8,128)(2,1)} %all-gather.7.cloned.1.call-done) | data formatting | bytes 12877824
  463.3 57.5 %shard_map.321 = (f32[6288,512]{1,0:T(8,128)}, f32[6288,512]{1,0:T(8,128)}, f32[1572,512]{1,0:T(8,128)}, f32[1572,512]{1,0:T(8,128)}, f32[1572,512]{1,0:T(8,128)...) custom-call(f32[32,8,128]{2,1,0:T(8,128)} %shard_map.320.refs_0_, ...), custom_call_target="tpu_custom_call" | custom-call | tf_op jit(solution)/shard_map/pallas_call | solution.py:1994
  (38 shorter events, 0.3 us)
Async XLA Ops:
  7.2 208.2 %all-gather.5.cloned.1.call-start = ((), (), s32[]{:S(2)}) async-start(), calls=%async_computation | async-start | bytes 8069120 | tf_op jit(solution)/shard_map/all_gather | solution.py:2068
  14.4 65.9 %copy-start = (f32[1572,512]{1,0:T(8,128)S(1)}, f32[1572,512]{1,0:T(8,128)}, u32[]{:S(2)}) copy-start(f32[1572,512]{1,0:T(8,128)} %refs_13_.1) | copy-start | bytes 9658372
  80.2 1.5 copy-start.8
  80.2 2.2 copy-start.6
  80.2 5.6 %copy-start.5 = (s32[32,8,128]{2,1,0:T(8,128)S(1)}, s32[32,8,128]{2,1,0:T(8,128)}, u32[]{:S(2)}) copy-start(s32[32,8,128]{2,1,0:T(8,128)} %get-tuple-element.70) | copy-start | bytes 393220
  81.6 376.2 %all-gather.7.cloned.1.call-start = ((), (), s32[]{:S(2)}) async-start(), calls=%async_computation.1 | async-start | bytes 8069120 | tf_op jit(solution)/shard_map/all_gather | solution.py:2135
  88.0 14.1 %copy-start.7 = (s32[32,2,128]{2,1,0:T(2,128)}, s32[32,2,128]{2,1,0:T(2,128)S(1)}, u32[]{:S(2)}) copy-start(s32[32,2,128]{2,1,0:T(2,128)S(1)} %get-tuple-element.122) | copy-start | bytes 98308
  88.6 126.0 %copy-start.3 = (f32[32,2,128]{2,1,0:T(2,128)}, f32[32,2,128]{2,1,0:T(2,128)S(1)}, u32[]{:S(2)}) copy-start(f32[32,2,128]{2,1,0:T(2,128)S(1)} %fusion.3) | copy-start | bytes 98308
  191.7 22.9 %copy-start.9 = (f32[4,8,256]{2,1,0:T(8,128)S(1)}, f32[4,8,256]{2,1,0:T(8,128)}, u32[]{:S(2)}) copy-start(f32[4,8,256]{2,1,0:T(8,128)} %get-tuple-element.73) | copy-start | bytes 98308
  220.6 149.0 %copy-start.1 = (f32[1572,512]{1,0:T(8,128)S(1)}, f32[1572,512]{1,0:T(8,128)}, u32[]{:S(2)}) copy-start(f32[1572,512]{1,0:T(8,128)} %refs_9_.1) | copy-start | bytes 9658372
  369.6 10.1 %copy-start.4 = (f32[256,1]{1,0:T(8,128)S(1)}, f32[256,1]{1,0:T(8,128)}, u32[]{:S(2)}) copy-start(f32[256,1]{1,0:T(8,128)} %get-tuple-element.71) | copy-start | bytes 3076
  380.4 20.8 %copy-start.11 = (f32[1,512]{1,0:T(1,128)S(1)}, f32[1,512]{1,0:T(1,128)}, u32[]{:S(2)}) copy-start(f32[1,512]{1,0:T(1,128)} %get-tuple-element.87) | copy-start | bytes 6148
  380.4 21.5 %copy-start.2 = (f32[768,512]{1,0:T(8,128)S(1)}, f32[768,512]{1,0:T(8,128)}, u32[]{:S(2)}) copy-start(f32[768,512]{1,0:T(8,128)} %get-tuple-element.88) | copy-start | bytes 4718596
  380.4 26.8 %copy-start.10 = (f32[8,128]{1,0:T(8,128)S(1)}, f32[8,128]{1,0:T(8,128)}, u32[]{:S(2)}) copy-start(f32[8,128]{1,0:T(8,128)} %get-tuple-element.89) | copy-start | bytes 12292
Sparse Core Ops, SparseCore 0:
  81.8 107.2 all-gather.4
  371.1 86.6 all-gather.6

commit v7 on v6

--- a/solution.py
+++ b/solution.py
@@ -920,13 +920,6 @@
         def replica_before(k):
             return lax.rem(place.replica + replicas - k, replicas)
 
-        def turn(step):
-            if isinstance(step, int):
-                return (step + 1) // 2 if step % 2 else (chips - step // 2) % chips
-            ahead = (step + 1) // 2
-            behind = lax.rem(chips - step // 2, chips)
-            return jnp.where(lax.rem(step, 2) == 1, ahead, behind)
-
         def lane_copy(j):
             return remote(own_ref, hid.at[me], lane_send.at[j], lane_recv.at[j], lane_device(j))
 
@@ -1033,8 +1026,8 @@
         )
         own_core = remote(own_ref, hid.at[me], core_send.at[0], core_recv.at[0], place.sibling())
         own_core.start()
-        for step in range(1, min(3, chips)):
-            lane_copy(turn(step)).start()
+        for j in range(1, chips):
+            lane_copy(j).start()
         hid[me] = own_ref[...]
         for k in range(1, replicas):
             plane_copy(k, 0).start()
@@ -1049,13 +1042,11 @@
         spots = lax.broadcasted_iota(jnp.int32, (block, own), 0)
 
         def forward(step, carry):
-            j = turn(step // 2)
+            j = step // 2
             other = lax.rem(step, 2)
 
             @pl.when(step == 1)
             def _():
-                for later in range(3, chips):
-                    lane_copy(turn(later)).start()
                 there = hid.at[place.sibling_member]
                 remote(
                     there, there, core_send.at[0], core_recv.at[0], place.sibling()
@@ -1137,7 +1128,7 @@
             return total
 
         def backward(step, carry):
-            j = turn(chips - 1 - step)
+            j = lax.rem(step + 1, chips)
 
             @pl.when(step == chips - 1)
             def _():
@@ -1862,7 +1853,8 @@
     window = max(-(-(sub + sub * r % 8) // 8) * 8 for r in range(vocab // sub))
     tile = 264
     tiles = -(-window // tile)
-    steps = 2 * blocks + 2 * tiles
+    kinds = len(tables)
+    steps = kinds * (blocks + tiles)
     count = len(matrices)
 
     def kernel(*refs):
@@ -1874,11 +1866,11 @@
             return taken
 
         (scalars_ref,) = take(1)
-        whole_in = [take(3) for _ in range(2)]
-        own_in = [take(4) for _ in range(2)]
+        whole_in = [take(3) for _ in range(kinds)]
+        own_in = [take(4) for _ in range(kinds)]
         small_in = [take(4) for _ in range(count)]
-        new_tables = take(2)
-        own_out = [take(2) for _ in range(2)]
+        new_tables = take(kinds)
+        own_out = [take(2) for _ in range(kinds)]
         small_out = [take(3) for _ in range(count)]
         (factor_ref,) = take(1)
         windows = take(2)
@@ -1907,7 +1899,7 @@
             factor_ref[...] = CLIP_LEVEL / jnp.maximum(norm, CLIP_LEVEL)
 
         factor = factor_ref[1:2, 0:1]
-        for w in range(2):
+        for w in range(kinds):
 
             @pl.when((step >= w * blocks) & (step < (w + 1) * blocks))
             def _():
@@ -1921,15 +1913,15 @@
         def _():
             for i in range(count):
                 weight, grad, moment, average = [ref[...] for ref in small_in[i]]
-                results = update_rule(weight, grad, moment, average, rates[2 + i], factor)
+                results = update_rule(weight, grad, moment, average, rates[kinds + i], factor)
                 for ref, result in zip(small_out[i], results):
                     ref[...] = result
 
-        for w in range(2):
-            base = 2 * blocks + w * tiles
+        for w in range(kinds):
+            base = kinds * blocks + w * tiles
             for t in range(tiles):
 
-                @pl.when(step == (base - tiles + t + 1 if w else blocks))
+                @pl.when(step == (base - tiles + t + 1 if w else 1))
                 def _():
                     for copy in fetch(w, t):
                         copy.start()
@@ -1968,24 +1960,24 @@
     def own_spec(w):
         return pl.BlockSpec(
             (tile, width),
-            lambda i: (jnp.clip(i - 2 * blocks - w * tiles, 0, tiles - 1), 0),
+            lambda i: (jnp.clip(i - kinds * blocks - w * tiles, 0, tiles - 1), 0),
         )
 
     state = jax.ShapeDtypeStruct((sub, width), FLOAT)
     operands = [scalars]
     in_specs = [whole]
-    for w in range(2):
+    for w in range(kinds):
         operands += list(tables[w][:3])
         in_specs += [table_spec(w)] * 3
-    for w in range(2):
+    for w in range(kinds):
         operands += [tables[w][0], tables[w][1], tables[w][3], tables[w][4]]
         in_specs += [anywhere, anywhere, own_spec(w), own_spec(w)]
     for item in matrices:
         operands += list(item)
         in_specs += [whole] * 4
-    out_specs = [table_spec(0), table_spec(1)]
-    out_shape = [jax.ShapeDtypeStruct((vocab, width), FLOAT)] * 2
-    for w in range(2):
+    out_specs = [table_spec(w) for w in range(kinds)]
+    out_shape = [jax.ShapeDtypeStruct((vocab, width), FLOAT)] * kinds
+    for w in range(kinds):
         out_specs += [own_spec(w)] * 2
         out_shape += [state] * 2
     for item in matrices:
@@ -1999,11 +1991,13 @@
         out_shape=out_shape,
         scratch_shapes=[pltpu.VMEM((8, 128), FLOAT)]
         + [pltpu.VMEM((tiles * tile + 8, width), FLOAT)] * 2
-        + [pltpu.SemaphoreType.DMA((2, 2, tiles))],
+        + [pltpu.SemaphoreType.DMA((kinds, 2, tiles))],
         compiler_params=pltpu.CompilerParams(vmem_limit_bytes=VMEM_LIMIT),
     )(*operands)
-    tables_out = [(results[w], *results[2 + 2 * w : 4 + 2 * w]) for w in range(2)]
-    return tables_out, [results[6 + 3 * i : 9 + 3 * i] for i in range(count)]
+    tables_out = [
+        (results[w], *results[kinds + 2 * w : kinds + 2 + 2 * w]) for w in range(kinds)
+    ]
+    return tables_out, [results[3 * (kinds + i) : 3 * (kinds + i + 1)] for i in range(count)]
 
 
 def shards(
@@ -2149,18 +2143,23 @@
     def row(values):
         return values.reshape(1, -1)
 
-    (embed, head), (inner, outer, vector) = update_all(
+    (head,), (inner, outer, vector) = update_all(
         scalars,
-        [
-            (embed_table, embed_grad, embed_moment_low, embed_moment, embed_average),
-            (head_table, head_grad, head_moment_low, head_moment, head_average),
-        ],
+        [(head_table, head_grad, head_moment_low, head_moment, head_average)],
         [
             (in_weights, layer_grads[0], in_moment, in_average),
             (out_weights, layer_grads[1], out_moment, out_average),
             tuple(map(row, (vectors, layer_grads[2], vector_moment, vector_average))),
         ],
-        (base, base / root, base / root, base / root, 0.3 * base),
+        (base / root, base / root, base / root, 0.3 * base),
+    )
+    scalars, new_head = lax.optimization_barrier((scalars, head[0]))
+    head = (new_head, *head[1:])
+    (embed,), _ = update_all(
+        scalars,
+        [(embed_table, embed_grad, embed_moment_low, embed_moment, embed_average)],
+        [],
+        (base,),
     )
     vector = [values.reshape(-1) for values in vector]
     return (*embed, *head, *inner, *outer, *vector, loss, grad_norm)

time: 537 us -> 526 us (0.980)
  waiting for transfers between devices: 17.7 us -> 0.06 us
  Pallas kernels: 441 us -> 447 us
    all_gather x1, waiting for transfers between devices: 17.7 us -> 0.02 us  [shards(): lax.all_gather(late_moment.astype(NARROW), 'dp', axis=0, tiled=True)]
    pallas_call x1 -> x2, Pallas kernels: 57.5 us -> 59.5 us  [update_all(): pl.pallas_call(kernel, grid=(steps,), in_specs=in_specs, out_specs=out_sp...]
  transfers between devices with their start and end apart: 2 -> 2, of which waited for: 1 -> 0; matrix products, arithmetic and copies ran while one was open for 6% -> 6% of each run, Pallas kernels for 32% -> 39%
where the time goes in v7:
time: 526 us; the launch traced here: 517 us
  Pallas kernels  447 us (85%)
  other arithmetic  26.9 us (5%)
  local copies, waits for them, and re-layouts  22.6 us (4%)
  between operations  20.3 us (4%)
    pallas_call x1, Pallas kernels, head_table_grad(): pl.pallas_call(kernel, grid=(steps,), in_specs=[pl.BlockSpec((block, widt...  153 us
    pallas_call x1, Pallas kernels, head_kernel(): pl.pallas_call(kernel, in_specs=[anywhere, whole, whole, whole, whole], o...  89.6 us
    pallas_call x1, Pallas kernels, start_kernel(): pl.pallas_call(kernel, in_specs=[whole, whole, whole, whole, anywhere, an...  65.8 us
    pallas_call x2, Pallas kernels, update_all(): pl.pallas_call(kernel, grid=(steps,), in_specs=in_specs, out_specs=out_sp...  59.5 us
    pallas_call x1, Pallas kernels, exchange_scalars(): pl.pallas_call(kernel, in_specs=[whole], out_specs=whole, out_shape=jax.S...  24.4 us
    pallas_call x1, Pallas kernels, embed_table_grad(): pl.pallas_call(kernel, grid_spec=pltpu.PrefetchScalarGridSpec(num_scalar_...  21.8 us
    pallas_call x1, Pallas kernels, layer_backward(): pl.pallas_call(kernel, in_specs=[whole] * 14, out_specs=[whole, whole, pl...  21.2 us
    pallas_call x1, Pallas kernels, layer_forward(): pl.pallas_call(kernel, out_shape=[jax.ShapeDtypeStruct((rows, width), NAR...  11.9 us
  transfers between devices with their start and end apart: 2, of which 0 were waited for; matrix products, arithmetic and copies ran while one was open for 6% of the time, Pallas kernels for 39%

profile of v7, /device:TPU:0, one launch (start us, length us, event | category | flops | bytes accessed | tf_op | source)
XLA Modules:
  0.0 517.4 jit_solution(9658574246682811394)
XLA Ops:
  7.2 0.0 all-gather.5.cloned.1.call-start
  7.2 0.8 slice_compare_fusion
  8.1 0.8 fusion.8
  8.8 0.8 fusion.5
  9.6 0.8 fusion.6
  10.4 0.6 convert_reduce_fusion
  11.0 1.3 pad_bitcast_fusion.1.line_ref
  12.3 0.6 broadcast_in_dim.115
  13.0 0.1 pad.24.clone
  13.0 1.3 add_add_fusion.packed_ref
  14.4 65.8 %shard_map.314 = (s32[32,8,128]{2,1,0:T(8,128)}, f32[8,8,128]{2,1,0:T(8,128)}, bf16[8,64,3584]{2,1,0:T(8,128)(2,1)}, bf16[8,320,512]{2,1,0:T(8,128)(2,1)}, f32[2...) custom-call(s32[8,128]{1,0:T(8,128)} %add_add_fusion.packed_ref, f32[8,128]{1,0:T(8,128)} %pad_bitcast_fusion.1.line_ref, ...), custom_call_target="tpu_custom_call" | custom-call | bytes 12877824 | tf_op jit(solution)/shard_map/pallas_call | solution.py:786
  80.2 0.0 copy-start.6
  80.3 1.4 convert_bitcast_fusion.1
  81.6 0.0 all-gather.5.cloned.1.call-update
  81.6 0.0 all-gather.7.cloned.1.call-start
  81.7 0.0 copy-done.8
  81.7 0.7 reshape.254.vector_ref
  82.5 0.2 select_reduce_fusion.3
  82.6 0.1 select_reduce_fusion.2
  82.7 0.5 multiply_sine_fusion
  83.3 0.9 concatenate.27.ahead_ref
  84.2 0.9 concatenate.28.behind_ref
  85.1 0.8 copy.54.column_ref
  85.9 0.1 slice.44
  86.0 0.7 slice_reduce_fusion.1
  87.3 0.7 fusion.4
  88.0 0.6 dynamic_slice.6
  88.6 0.6 dynamic_slice.7
  89.3 0.9 concatenate.26.stay_ref
  90.2 11.9 %shard_map.315 = (bf16[256,512]{1,0:T(8,128)(2,1)}, bf16[256,1536]{1,0:T(8,128)(2,1)}, f32[256,2048]{1,0:T(8,128)}, bf16[256,2560]{1,0:T(8,128)(2,1)}, f32[256,512]{1,0:T(8,128)}) custom-call(f32[256,512]{1,0:T(8,128)} %get-tuple-element.66.resid_ref, bf16[512,3584]{1,0:T(8,128)(2,1)} %bitcast.61, bf16[2560,512]{1,0:T(8,128)(2,1)} %bitcast.63, ...), custom_call_target="tpu_custom_call" | custom-call | tf_op jit(solution)/shard_map/pallas_call | solution.py:189
  102.0 89.6 %shard_map.316 = (f32[256,512]{1,0:T(8,128)}, f32[4,8,256]{2,1,0:T(8,128)}, f32[256,1]{1,0:T(8,128)}, bf16[32,256,512]{2,1,0:T(8,128)(2,1)}) custom-call(f32[6288,512]{1,0:T(8,128)} %refs_4_.2, bf16[256,512]{1,0:T(8,128)(2,1)} %get-tuple-element.70.own_ref, bf16[8,256,512]{2,1,0:T(8,128)(2,1)} %get-tuple-element.71.aims_ref, s32[8,1,256]{2,1,0:T(1,128)} %bitcast.84, ...), custom_call_target="tpu_custom_call" | custom-call | flops 26373783552 | bytes 12877824 | tf_op jit(solution)/shard_map/pallas_call | solution.py:1205
  191.7 21.2 %shard_map.317 = (bf16[256,512]{1,0:T(8,128)(2,1)}, f32[1,7680]{1,0:T(1,128)}, f32[8,768,512]{2,1,0:T(8,128)}) custom-call(f32[256,512]{1,0:T(8,128)} %get-tuple-element.76.final_grad_ref, f32[256,512]{1,0:T(8,128)} %get-tuple-element.66.resid_ref, bf16[512,3584]{1,0:T(8,128)(2,1)} %bitcast.62, bf16[2560,512]{1,0:T(8,128)(2,1)} %bitcast.64, ...), custom_call_target="tpu_custom_call" | custom-call | tf_op jit(solution)/shard_map/pallas_call | solution.py:377
  212.9 0.8 reduce.5
  213.7 0.1 reshape.241
  213.8 0.6 copy.65
  214.4 0.7 compare_select_fusion.logsum_ref
  215.1 5.3 %reshape.256.refs_3_ = bf16[6288,512]{1,0:T(8,128)(2,1)} reshape(bf16[4,1572,512]{2,1,0:T(8,128)(2,1)} %all-gather.5.cloned.1.call-done) | data formatting | bytes 12877824 | tf_op jit(solution)/shard_map/optimization_barrier | solution.py:2104
  220.4 153.0 %shard_map.318 = (f32[6288,512]{1,0:T(8,128)}, f32[1,512]{1,0:T(1,128)}, bf16[32,256,512]{2,1,0:T(8,128)(2,1)}, f32[8,128]{1,0:T(8,128)}, f32[768,512]{1,0:T(8,128)}) custom-call(f32[6288,512]{1,0:T(8,128)} %refs_4_.2, bf16[8192,512]{1,0:T(8,128)(2,1)} %bitcast.95, f32[4,1,2048]{2,1,0:T(1,128)} %compare_select_fusion.logsum_ref, f32[4,1,2048]{2,1,0:T(1,128)} %bitcast.71, ...), custom_call_target="tpu_custom_call" | custom-call | flops 105495134208 | bytes 42532864 | tf_op jit(solution)/shard_map/pallas_call | solution.py:1629
  373.4 1.4 convert_bitcast_fusion
  374.8 0.0 all-gather.7.cloned.1.call-update
  374.9 0.2 convolution_convert_fusion
  375.1 6.5 %select_reduce_fusion = (s32[16,512]{1,0:T(8,128)S(1)}, s32[16,512]{1,0:T(8,128)S(1)}) fusion(s32[16,512]{1,0:T(8,128)S(1)} %sub.65, s32[16,512]{1,0:T(8,128)S(1)} %convolution_convert_fusion, pred[16,512]{1,0:T(8,128)(4,1)S(1)} %compare_and_fusion), kind=kLoop, calls=%fused_computation | loop fusion | flops 25149440 | bytes 139264 | tf_op jit(solution)/shard_map/reduce_sum | solution.py:1769
  381.6 0.6 reshape.236.place_ref
  382.2 0.6 reshape.237.row_ref
  382.8 0.1 reduce_sum.159
  382.9 0.6 reduce_sum.160.count_ref
  383.6 0.6 reduce_sum.157
  384.2 21.8 %shard_map.319 = (f32[6288,512]{1,0:T(8,128)}, f32[1,512]{1,0:T(1,128)}) custom-call(s32[16]{0:T(128)} %reduce_sum.160.count_ref, s32[16,1,512]{2,1,0:T(1,128)} %reshape.236.place_ref, s32[16,1,512]{2,1,0:T(1,128)} %reshape.237.row_ref, bf16[8192,512]{1,0:T(8,128)(2,1)} %bitcast.65), custom_call_target="tpu_custom_call" | custom-call | tf_op jit(solution)/shard_map/pallas_call | solution.py:1811
  406.0 1.3 reduce_sum.163
  407.3 0.6 reduce_sum.164
  407.9 0.1 slice.48
  409.3 1.1 fusion.1
  411.1 1.6 fusion.10
  413.3 1.2 fusion.11
  415.2 0.7 fusion.9
  415.9 0.7 pad.19.own_ref
  416.6 24.4 %shard_map.320.refs_0_ = f32[32,8,128]{2,1,0:T(8,128)} custom-call(f32[8,128]{1,0:T(8,128)} %pad.19.own_ref), custom_call_target="tpu_custom_call" | custom-call | tf_op jit(solution)/shard_map/pallas_call | solution.py:1751
  441.0 1.0 copy.60
  442.0 31.6 %shard_map.321 = (f32[6288,512]{1,0:T(8,128)}, f32[1572,512]{1,0:T(8,128)}, f32[1572,512]{1,0:T(8,128)}, f32[64,3584]{1,0:T(8,128)}, f32[64,3584]{1,0:T(8,128)},...) custom-call(f32[32,8,128]{2,1,0:T(8,128)} %shard_map.320.refs_0_, ...), custom_call_target="tpu_custom_call" | custom-call | tf_op jit(solution)/shard_map/pallas_call | solution.py:1986
  473.6 1.1 slice_reduce_fusion
  474.6 0.6 fusion.12
  475.9 0.0 all-gather.7.cloned.1.call-done
  475.9 5.3 %reshape.258.refs_3_ = bf16[6288,512]{1,0:T(8,128)(2,1)} reshape(bf16[4,1572,512]{2,1,0:T(8,128)(2,1)} %all-gather.7.cloned.1.call-done) | data formatting | bytes 12877824
  481.2 28.0 %shard_map.322 = (f32[6288,512]{1,0:T(8,128)}, f32[1572,512]{1,0:T(8,128)}, f32[1572,512]{1,0:T(8,128)}) custom-call(f32[32,8,128]{2,1,0:T(8,128)} %shard_map.320.refs_0_, f32[6288,512]{1,0:T(8,128)} %refs_4_.3, f32[6288,512]{1,0:T(8,128)} %get-tuple-element.96.refs_2_.refs_5_, bf16[6288,512]{1,0:T(8,128)(2,1)} %reshape.258.refs_3_, f32[6288,512]{1,0:T(8,128)} %refs_4_.3, ...), custom_call_target="tpu_custom_call" | custom-call | tf_op jit(solution)/shard_map/pallas_call | solution.py:1986
  (39 shorter events, 0.3 us)
Async XLA Ops:
  7.2 208.0 %all-gather.5.cloned.1.call-start = ((), (), s32[]{:S(2)}) async-start(), calls=%async_computation | async-start | bytes 8069120 | tf_op jit(solution)/shard_map/all_gather | solution.py:2062
  14.4 65.9 %copy-start = (f32[1572,512]{1,0:T(8,128)S(1)}, f32[1572,512]{1,0:T(8,128)}, u32[]{:S(2)}) copy-start(f32[1572,512]{1,0:T(8,128)} %refs_6_.2) | copy-start | bytes 9658372
  80.2 1.5 copy-start.8
  80.2 2.2 copy-start.6
  80.2 5.6 %copy-start.5 = (s32[32,8,128]{2,1,0:T(8,128)S(1)}, s32[32,8,128]{2,1,0:T(8,128)}, u32[]{:S(2)}) copy-start(s32[32,8,128]{2,1,0:T(8,128)} %get-tuple-element.72) | copy-start | bytes 393220
  81.6 394.3 %all-gather.7.cloned.1.call-start = ((), (), s32[]{:S(2)}) async-start(), calls=%async_computation.1 | async-start | bytes 8069120 | tf_op jit(solution)/shard_map/all_gather | solution.py:2129
  88.0 14.1 %copy-start.7 = (s32[32,2,128]{2,1,0:T(2,128)}, s32[32,2,128]{2,1,0:T(2,128)S(1)}, u32[]{:S(2)}) copy-start(s32[32,2,128]{2,1,0:T(2,128)S(1)} %get-tuple-element.126) | copy-start | bytes 98308
  88.6 125.8 %copy-start.3 = (f32[32,2,128]{2,1,0:T(2,128)}, f32[32,2,128]{2,1,0:T(2,128)S(1)}, u32[]{:S(2)}) copy-start(f32[32,2,128]{2,1,0:T(2,128)S(1)} %fusion.3) | copy-start | bytes 98308
  191.7 22.7 %copy-start.9 = (f32[4,8,256]{2,1,0:T(8,128)S(1)}, f32[4,8,256]{2,1,0:T(8,128)}, u32[]{:S(2)}) copy-start(f32[4,8,256]{2,1,0:T(8,128)} %get-tuple-element.75) | copy-start | bytes 98308
  220.4 153.0 %copy-start.1 = (f32[1572,512]{1,0:T(8,128)S(1)}, f32[1572,512]{1,0:T(8,128)}, u32[]{:S(2)}) copy-start(f32[1572,512]{1,0:T(8,128)} %refs_6_.3) | copy-start | bytes 9658372
  373.4 10.1 %copy-start.4 = (f32[256,1]{1,0:T(8,128)S(1)}, f32[256,1]{1,0:T(8,128)}, u32[]{:S(2)}) copy-start(f32[256,1]{1,0:T(8,128)} %get-tuple-element.73) | copy-start | bytes 3076
  384.2 23.1 %copy-start.11 = (f32[1,512]{1,0:T(1,128)S(1)}, f32[1,512]{1,0:T(1,128)}, u32[]{:S(2)}) copy-start(f32[1,512]{1,0:T(1,128)} %get-tuple-element.89) | copy-start | bytes 6148
  384.2 23.7 %copy-start.2 = (f32[768,512]{1,0:T(8,128)S(1)}, f32[768,512]{1,0:T(8,128)}, u32[]{:S(2)}) copy-start(f32[768,512]{1,0:T(8,128)} %get-tuple-element.90) | copy-start | bytes 4718596
  384.2 29.1 %copy-start.10 = (f32[8,128]{1,0:T(8,128)S(1)}, f32[8,128]{1,0:T(8,128)}, u32[]{:S(2)}) copy-start(f32[8,128]{1,0:T(8,128)} %get-tuple-element.91) | copy-start | bytes 12292
Sparse Core Ops, SparseCore 0:
  81.8 107.2 all-gather.4
  375.0 86.8 all-gather.6
